TPU v7x, 32 devices: a whole 2x2x4 slice. The times are simulated.
32 devices in a mesh: dp: 8 (over z, x), mod: 4 (over y, core).
Axes of the slice: x: 2, y: 2, z: 4, core: 2. Of those that a mesh axis runs over, the one named last changes fastest.
Arguments:
- latents: float32 [16384, 16], P(('dp', 'mod')), may hold values from -6 to 6
- noise: float32 [16384, 16], P(('dp', 'mod')), may hold values from -6 to 6
- timesteps: int32 [64], P(('dp', 'mod')), may hold values from 0 to 999
- labels: int32 [64], P(('dp', 'mod')), may hold values from 0 to 999
- dropped: int32 [64], P(('dp', 'mod')), may hold values 0 or 1
- block_master: float32 [15980544], P(('dp', 'mod')), may hold values from -2 to 2
- block_m: float32 [15980544], P(('dp', 'mod')), may hold values from -1 to 1
- block_v: float32 [15980544], P(('dp', 'mod')), may hold values from 0 to 1, as said below
- stem_master: float32 [5439744], P(('dp', 'mod')), may hold values from -8 to 8
- stem_m: float32 [5439744], P(('dp', 'mod')), may hold values from -1 to 1
- stem_v: float32 [5439744], P(('dp', 'mod')), may hold values from 0 to 1, as said below
- ada_w: float32 [1152, 6912], P('dp', 'mod'), may hold values from -0.25 to 0.25
- ada_w_m: float32 [1152, 6912], P('dp', 'mod'), may hold values from -1 to 1
- ada_w_v: float32 [1152, 6912], P('dp', 'mod'), may hold values from 0 to 1, as said below
Outputs:
- loss_sum: float32 [], replicated
- grad_norm: float32 [], replicated
- block_new: float32 [15980544], P(('dp', 'mod'))
- block_m_new: float32 [15980544], P(('dp', 'mod'))
- block_v_new: float32 [15980544], P(('dp', 'mod'))
- stem_new: float32 [5439744], P(('dp', 'mod'))
- stem_m_new: float32 [5439744], P(('dp', 'mod'))
- stem_v_new: float32 [5439744], P(('dp', 'mod'))
- ada_w_new: float32 [1152, 6912], P('dp', 'mod')
- ada_w_m_new: float32 [1152, 6912], P('dp', 'mod')
- ada_w_v_new: float32 [1152, 6912], P('dp', 'mod')
Inputs may be any that keep to these rules, and one draw needn't show every extreme that they name: `block_v`: positive. `stem_v`: positive. `ada_w_v`: positive.
All inputs are finite; a program needn't handle non-finite values. No bound on the sum of `dropped` on one device may be relied on, other than what follows from the above.
Results may differ from a plain program's by a relative error of at most 0.0024.
The roundings to bfloat16 on the way count: a program that leaves them out, or rounds other values in their place, can miss the bound.
Values may be sent and summed in bfloat16 or wider, within the bound.
No kernel may reach another device: no remote copies, remote signals or barrier semaphores. Data moves between devices by JAX's collectives and lax.ppermute only.
A program may use at most 320 MiB of HBM per device.

v0:
```python
import math

import jax
import jax.numpy as jnp
from jax import lax
from jax.sharding import PartitionSpec as P

D = 1152
HEADS = 16
HEAD_DIM = 72
FF = 4608
CLASSES = 1000
PATCH = 16
GRID = 16
FREQ = 256
TSTEPS = 1000
STEP = 10
SEQ = 256
WB = 13872
SROWS = 4722


HIGHEST_PRECISION = lax.Precision.HIGHEST
LOG_TWO = math.log(2.0)
THRESHOLD = 1.0
LEARN_RATE = 0.05
BETA_ONE = 0.9
BETA_TWO = 0.999
EPSILON = 1e-08


def matmul(form, left, right):
    return jnp.einsum(form, left, right, preferred_element_type=jnp.float32)


def plan(steps):
    step_index = jnp.arange(TSTEPS).astype(jnp.float32)
    beta_rows = 0.0001 + (0.02 - 0.0001) * step_index / (TSTEPS - 1)
    alpha_bar = jnp.cumprod(1.0 - beta_rows)
    previous = jnp.concatenate([jnp.ones((1,), jnp.float32), alpha_bar[:-1]])
    posterior = beta_rows * (1.0 - previous) / (1.0 - alpha_bar)
    clipped = jnp.concatenate([posterior[1:2], posterior[1:]])
    mean_factor = beta_rows * beta_rows * previous / ((1.0 - alpha_bar) * alpha_bar)
    plan_table = jnp.stack(
        [
            jnp.sqrt(alpha_bar),
            jnp.sqrt(1.0 - alpha_bar),
            mean_factor,
            jnp.log(clipped),
            jnp.log(beta_rows),
        ],
        1,
    )
    one_hot = (steps[:, None] == jnp.arange(TSTEPS)[None, :]).astype(jnp.float32)
    return jnp.dot(one_hot, plan_table, precision=HIGHEST_PRECISION)


def positions():
    quarter = D // 4
    omegas = 1.0 / 10000.0 ** (jnp.arange(quarter).astype(jnp.float32) / quarter)
    cells = jnp.arange(SEQ)
    column_angle = (cells % GRID).astype(jnp.float32)[:, None] * omegas[None, :]
    row_angle = (cells // GRID).astype(jnp.float32)[:, None] * omegas[None, :]
    return jnp.concatenate(
        [jnp.sin(column_angle), jnp.cos(column_angle), jnp.sin(row_angle), jnp.cos(row_angle)], 1
    )


def frequencies(steps):
    half_count = FREQ // 2
    frequency = jnp.exp(
        -math.log(10000.0) * jnp.arange(half_count).astype(jnp.float32) / half_count
    )
    angles = steps.astype(jnp.float32)[:, None] * frequency[None, :]
    return jnp.concatenate([jnp.cos(angles), jnp.sin(angles)], 1)


def modulate(stream, shifts, scales):
    average = jnp.mean(stream, -1, keepdims=True)
    centred = stream - average
    variance = jnp.mean(centred * centred, -1, keepdims=True)
    return centred * lax.rsqrt(variance + 1e-06) * (1.0 + scales[:, None, :]) + shifts[:, None, :]


def modulate_back(stream, shifts, scales, cotangent):
    unused, pullback = jax.vjp(modulate, stream, shifts, scales)
    return pullback(cotangent)


def smooth_back(function, inputs, cotangent):
    unused, pullback = jax.vjp(function, inputs)
    return pullback(cotangent)[0]


def gelu_tanh(inputs):
    return jax.nn.gelu(inputs, approximate=True)


def loss_terms(prediction, target, sched):
    guessed = prediction[..., :PATCH]
    variance_raw = prediction[..., PATCH:]
    mean_factor = sched[:, 2][:, None, None]
    posterior_log = sched[:, 3][:, None, None]
    beta_log = sched[:, 4][:, None, None]
    blend = 0.5 * (variance_raw + 1.0)
    model_log = blend * beta_log + (1.0 - blend) * posterior_log
    errors = guessed - target
    bound_term = 0.5 * (
        -1.0
        + model_log
        - posterior_log
        + jnp.exp(posterior_log - model_log)
        + mean_factor * errors * errors * jnp.exp(-model_log)
    )
    return jnp.sum(errors * errors + bound_term / LOG_TWO)


def stem_split(stacked):
    pieces = []
    offset = 0
    for extent in [FREQ, D, CLASSES + 1, 2 * D, 1, 2, 6]:
        pieces.append(stacked[offset : offset + extent])
        offset = offset + extent
    return pieces


def unpack(shared):
    block_rows = shared[0].reshape(D, WB)
    column_edges = [0, 3 * D, 4 * D, 4 * D + FF, 4 * D + 2 * FF, 4 * D + 2 * FF + PATCH, WB]
    pieces = [block_rows[:, column_edges[index] : column_edges[index + 1]] for index in range(6)]
    return (tuple(pieces[:4]), pieces[4], pieces[5], stem_split(shared[1].reshape(SROWS, D)))


def layer_forward(stream, modulation, layer_weights):
    w_qkv, w_proj, w_up, w_down = layer_weights
    images = stream.shape[0]
    pieces = jnp.split(modulation.astype(jnp.float32), 6, axis=1)
    normed = modulate(stream, pieces[0], pieces[1]).astype(jnp.bfloat16)
    triple = (
        matmul("isd,de->ise", normed, w_qkv)
        .astype(jnp.bfloat16)
        .reshape(images, SEQ, 3, HEADS, HEAD_DIM)
    )
    scores = matmul("iqhe,ikhe->ihqk", triple[:, :, 0], triple[:, :, 1]) * (
        1.0 / math.sqrt(HEAD_DIM)
    )
    totals = jax.nn.logsumexp(scores, axis=-1)
    weights = jnp.exp(scores - totals[..., None]).astype(jnp.bfloat16)
    mixed_heads = (
        matmul("ihqk,ikhe->iqhe", weights, triple[:, :, 2])
        .astype(jnp.bfloat16)
        .reshape(images, SEQ, D)
    )
    attended = matmul("isd,od->iso", mixed_heads, w_proj)
    middle = stream + pieces[2][:, None, :] * attended
    second = modulate(middle, pieces[3], pieces[4]).astype(jnp.bfloat16)
    inner_rows = matmul("isd,df->isf", second, w_up)
    active = gelu_tanh(inner_rows).astype(jnp.bfloat16)
    output = matmul("isf,of->iso", active, w_down)
    stored = (
        normed,
        triple,
        totals,
        mixed_heads,
        attended,
        middle,
        second,
        inner_rows,
        active,
        output,
    )
    return (middle + pieces[5][:, None, :] * output, stored)


def layer_backward(stream, modulation, layer_weights, stored, upstream):
    w_qkv, w_proj, w_up, w_down = layer_weights
    normed, triple, totals, mixed_heads, attended, middle, second, inner_rows, active, output = (
        stored
    )
    images = stream.shape[0]
    pieces = jnp.split(modulation.astype(jnp.float32), 6, axis=1)
    down_in = (pieces[5][:, None, :] * upstream).astype(jnp.bfloat16)
    gate_b = jnp.sum(upstream * output, 1)
    grad_down = matmul("iso,isf->of", down_in, active)
    inner_grad = smooth_back(gelu_tanh, inner_rows, matmul("iso,of->isf", down_in, w_down)).astype(
        jnp.bfloat16
    )
    grad_up = matmul("isd,isf->df", second, inner_grad)
    back_mid, shift_b, scale_b = modulate_back(
        middle, pieces[3], pieces[4], matmul("isf,df->isd", inner_grad, w_up)
    )
    grad_mid = upstream + back_mid
    proj_in = (pieces[2][:, None, :] * grad_mid).astype(jnp.bfloat16)
    gate_a = jnp.sum(grad_mid * attended, 1)
    grad_proj = matmul("iso,isd->od", proj_in, mixed_heads)
    mixed_grad = (
        matmul("iso,od->isd", proj_in, w_proj)
        .astype(jnp.bfloat16)
        .reshape(images, SEQ, HEADS, HEAD_DIM)
    )
    queries, key_rows, value_rows = (triple[:, :, 0], triple[:, :, 1], triple[:, :, 2])
    score_scale = 1.0 / math.sqrt(HEAD_DIM)
    softmax_rows = jnp.exp(
        matmul("iqhe,ikhe->ihqk", queries, key_rows) * score_scale - totals[..., None]
    )
    weight_grad = matmul("iqhe,ikhe->ihqk", mixed_grad, value_rows)
    score_grad = (
        softmax_rows * (weight_grad - jnp.sum(weight_grad * softmax_rows, -1, keepdims=True))
    ).astype(jnp.bfloat16)
    query_grad = matmul("ihqk,ikhe->iqhe", score_grad, key_rows) * score_scale
    key_grad = matmul("ihqk,iqhe->ikhe", score_grad, queries) * score_scale
    value_grad = matmul("ihqk,iqhe->ikhe", softmax_rows.astype(jnp.bfloat16), mixed_grad)
    triple_grad = (
        jnp.stack([query_grad, key_grad, value_grad], 2)
        .astype(jnp.bfloat16)
        .reshape(images, SEQ, 3 * D)
    )
    grad_qkv = matmul("isd,ise->de", normed, triple_grad)
    back_in, shift_a, scale_a = modulate_back(
        stream, pieces[0], pieces[1], matmul("ise,de->isd", triple_grad, w_qkv)
    )
    modulation_grad = jnp.concatenate([shift_a, scale_a, gate_a, shift_b, scale_b, gate_b], 1)
    return (
        grad_mid + back_in,
        modulation_grad,
        jnp.concatenate([grad_qkv, grad_proj, grad_up, grad_down], 1),
    )


def adam_update(weight, gradient, first, second):
    first_new = BETA_ONE * first + (1.0 - BETA_ONE) * gradient
    second_new = BETA_TWO * second + (1.0 - BETA_TWO) * gradient * gradient
    corrected = first_new / (1.0 - BETA_ONE**STEP)
    spread = jnp.sqrt(second_new / (1.0 - BETA_TWO**STEP))
    return (weight - LEARN_RATE * corrected / (spread + EPSILON), first_new, second_new)


def shards(
    latents,
    noise,
    timesteps,
    labels,
    dropped,
    block_master,
    block_m,
    block_v,
    stem_master,
    stem_m,
    stem_v,
    ada_w,
    ada_w_m,
    ada_w_v,
):
    images = timesteps.shape[0]
    shared = (
        lax.all_gather(block_master.astype(jnp.bfloat16), ("dp", "mod"), axis=0, tiled=True),
        lax.all_gather(stem_master.astype(jnp.bfloat16), ("dp", "mod"), axis=0, tiled=True),
    )
    layer_weights, w_patch, w_head, stem_parts = unpack(shared)
    w_time, w_time2, w_table, w_final, b_patch, b_final, b_ada = stem_parts
    sched = plan(timesteps)
    target = noise.reshape(images, SEQ, PATCH)
    noisy_rows = (
        sched[:, 0][:, None, None] * latents.reshape(images, SEQ, PATCH)
        + sched[:, 1][:, None, None] * target
    ).astype(jnp.bfloat16)
    stream = (
        matmul("isp,dp->isd", noisy_rows, w_patch)
        + b_patch[0].astype(jnp.float32)
        + positions()[None]
    )
    timing = frequencies(timesteps).astype(jnp.bfloat16)
    before = matmul("if,fd->id", timing, w_time)
    time_hidden = jax.nn.silu(before).astype(jnp.bfloat16)
    chosen = jnp.where(dropped == 1, CLASSES, labels)
    one_hot = chosen[:, None] == jnp.arange(CLASSES + 1)[None, :]
    condition = matmul("ik,kd->id", time_hidden, w_time2) + matmul(
        "ic,cd->id", one_hot.astype(jnp.bfloat16), w_table
    )
    signal = jax.nn.silu(condition).astype(jnp.bfloat16)
    rows_owned = lax.all_gather(ada_w.astype(jnp.bfloat16), "dp", axis=0, tiled=True)
    bias_all = b_ada.reshape(6 * D).astype(jnp.float32)
    owned_cols = rows_owned.shape[1]
    offset = lax.axis_index("mod") * owned_cols
    group_signal = lax.all_gather(signal, "mod", axis=0, tiled=True)
    own_bias = lax.dynamic_slice_in_dim(bias_all, offset, owned_cols)
    local_part = (matmul("gd,dc->gc", group_signal, rows_owned) + own_bias).astype(jnp.bfloat16)
    modulation = lax.all_to_all(local_part, "mod", split_axis=0, concat_axis=1, tiled=True)
    layer_out, stored = layer_forward(stream, modulation, layer_weights)
    final_mod = matmul("id,od->io", signal, w_final) + b_final.reshape(2 * D).astype(jnp.float32)
    final_shift, final_scale = (final_mod[:, :D], final_mod[:, D:])
    normed = modulate(layer_out, final_shift, final_scale).astype(jnp.bfloat16)
    prediction = matmul("isd,do->iso", normed, w_head)
    loss_local, loss_back = jax.vjp(
        lambda predicted: loss_terms(predicted, target, sched), prediction
    )
    loss_total = lax.psum(loss_local, ("dp", "mod"))
    out_grad = loss_back(jnp.ones_like(loss_local))[0].astype(jnp.bfloat16)
    grad_head = matmul("iso,isd->do", out_grad, normed)
    top_back, shift_grad, scale_grad = modulate_back(
        layer_out, final_shift, final_scale, matmul("iso,do->isd", out_grad, w_head)
    )
    final_grad = jnp.concatenate([shift_grad, scale_grad], 1)
    final_low = final_grad.astype(jnp.bfloat16)
    grad_final = matmul("io,id->od", final_low, signal)
    signal_grad = matmul("io,od->id", final_low, w_final)
    stream_grad, modulation_grad, layer_grad = layer_backward(
        stream, modulation, layer_weights, stored, top_back
    )
    modulation_low = modulation_grad.astype(jnp.bfloat16)
    returned = lax.all_to_all(modulation_low, "mod", split_axis=1, concat_axis=0, tiled=True)
    ada_part = matmul("gd,gc->dc", group_signal, returned)
    bias_part = jnp.sum(returned.astype(jnp.float32), 0)
    bias_grad = lax.dynamic_update_slice_in_dim(
        jnp.zeros((6 * D,), jnp.float32), bias_part, offset, 0
    )
    signal_grad = signal_grad + lax.psum_scatter(
        matmul("gc,dc->gd", returned, rows_owned).astype(jnp.bfloat16),
        "mod",
        scatter_dimension=0,
        tiled=True,
    ).astype(jnp.float32)
    ada_grad = lax.psum_scatter(
        ada_part.astype(jnp.bfloat16), "dp", scatter_dimension=0, tiled=True
    ).astype(jnp.float32)
    condition_grad = smooth_back(jax.nn.silu, condition, signal_grad)
    grad_table = jnp.dot(one_hot.astype(jnp.float32).T, condition_grad, precision=HIGHEST_PRECISION)
    condition_low = condition_grad.astype(jnp.bfloat16)
    grad_time2 = matmul("ik,id->kd", time_hidden, condition_low)
    before_grad = smooth_back(jax.nn.silu, before, matmul("id,kd->ik", condition_low, w_time2))
    grad_time = matmul("if,id->fd", timing, before_grad.astype(jnp.bfloat16))
    grad_patch = matmul("isp,isd->dp", noisy_rows, stream_grad.astype(jnp.bfloat16))
    block_grad = jnp.concatenate([layer_grad, grad_patch, grad_head], 1)
    stem_grad = jnp.concatenate(
        [
            grad_time,
            grad_time2,
            grad_table,
            grad_final,
            jnp.sum(stream_grad, (0, 1))[None],
            jnp.sum(final_grad, 0).reshape(2, D),
            bias_grad.reshape(6, D),
        ],
        0,
    )
    reduced = (
        lax.psum_scatter(
            block_grad.reshape(D * WB), ("dp", "mod"), scatter_dimension=0, tiled=True
        ),
        lax.psum_scatter(
            stem_grad.reshape(SROWS * D), ("dp", "mod"), scatter_dimension=0, tiled=True
        ),
    )
    squares = (
        jnp.sum(reduced[0] * reduced[0])
        + jnp.sum(reduced[1] * reduced[1])
        + jnp.sum(ada_grad * ada_grad)
    )
    grad_norm = jnp.sqrt(lax.psum(squares, ("dp", "mod")))
    factor = THRESHOLD / jnp.maximum(grad_norm, THRESHOLD)
    block_new = adam_update(block_master, reduced[0] * factor, block_m, block_v)
    stem_new = adam_update(stem_master, reduced[1] * factor, stem_m, stem_v)
    ada_new = adam_update(ada_w, ada_grad * factor, ada_w_m, ada_w_v)
    return (
        loss_total,
        grad_norm,
        block_new[0],
        block_new[1],
        block_new[2],
        stem_new[0],
        stem_new[1],
        stem_new[2],
        ada_new[0],
        ada_new[1],
        ada_new[2],
    )


def solution(mesh):
    return jax.shard_map(
        shards,
        mesh=mesh,
        in_specs=(
            P(("dp", "mod"), None),
            P(("dp", "mod"), None),
            P(("dp", "mod")),
            P(("dp", "mod")),
            P(("dp", "mod")),
            P(("dp", "mod")),
            P(("dp", "mod")),
            P(("dp", "mod")),
            P(("dp", "mod")),
            P(("dp", "mod")),
            P(("dp", "mod")),
            P("dp", "mod"),
            P("dp", "mod"),
            P("dp", "mod"),
        ),
        out_specs=(
            P(),
            P(),
            P(("dp", "mod")),
            P(("dp", "mod")),
            P(("dp", "mod")),
            P(("dp", "mod")),
            P(("dp", "mod")),
            P(("dp", "mod")),
            P("dp", "mod"),
            P("dp", "mod"),
            P("dp", "mod"),
        ),
        check_vma=False,
    )
```

profile of v0, /device:TPU:0, one launch (start us, length us, event | category | flops | bytes accessed | tf_op | source)
XLA Modules:
  0.0 2542.0 jit_solution(1607613647239931507)
XLA Ops:
  9.9 10.5 broadcast.297
  20.3 16.0 dynamic-update-slice
  57.5 673.4 %all-reduce.16.cloned.1.call-done = (bf16[15980544]{0:T(1024)(128)(2,1)}, bf16[5439744]{0:T(1024)(128)(2,1)}) async-done(((bf16[15980544]{0:T(1024)(128)(2,1)}, bf16[5439744]{0:T(1024)(128)(2,1)}), (bf16[15980544]{0:T(1024)(128)(2,1)}, bf16[5439744]{0:T(1024)(128)(2,1)})) %all-reduce.16.cloned.1.call-update) | async-done | bytes 42840592
  739.0 6.4 slice.194
  745.4 45.1 %reshape.339 = bf16[1152,13872]{1,0:T(8,128)(2,1)} reshape(bf16[15980544]{0:T(1024)(128)(2,1)} %get-tuple-element.31) | data formatting | bytes 63922176 | tf_op jit(solution)/shard_map/reshape | solution.py:128
  823.8 11.4 slice.170
  842.9 9.9 fusion.12
  869.7 13.2 fusion.8
  882.8 16.9 fusion.90
  908.3 16.9 fusion.6
  925.2 11.4 multiply_reduce_fusion.8
  965.7 9.1 multiply_reduce_fusion.5
  979.4 7.1 all_to_all.29
  1001.0 13.1 convolution_bitcast_fusion
  1014.2 10.5 convolution_bitcast_fusion.1
  1024.8 8.5 convolution_bitcast_fusion.2
  1033.3 68.8 %concatenate.43 = f32[1152,13872]{1,0:T(8,128)} concatenate(f32[1152,3456]{1,0:T(8,128)} %convolution_bitcast_fusion.2, f32[1152,1152]{1,0:T(8,128)} %convolution_bitcast_fusion.3, f32[1152,4608]{1,0:T(8,128)} %convolution_bitcast_fusion.1, f32[1152,4608]{1,0:T(8,128)} %convolution_bitcast_fusion, f32[1152,16]{1,0:T(8,128)S(1)} %convolution_bitcast_fusion.5, ...), dimensions={1} | concatenate | bytes 127844352 | tf_op jit(solution)/shard_map/concatenate | solution.py:333
  1102.1 58.1 %reshape.343 = f32[15980544]{0:T(1024)} reshape(f32[1152,13872]{1,0:T(8,128)} %concatenate.43) | data formatting | bytes 127844352 | tf_op jit(solution)/shard_map/reshape | solution.py:348
  1169.6 10.3 all-reduce.6
  1193.2 56.6 %concatenate.46 = f32[4722,1152]{1,0:T(8,128)} concatenate(f32[256,1152]{1,0:T(8,128)S(1)} %copy-done.21, f32[1152,1152]{1,0:T(8,128)} %fusion.58, f32[1001,1152]{1,0:T(8,128)} %fusion.46, f32[2304,1152]{1,0:T(8,128)} %fusion.80, f32[1,1152]{1,0:T(1,128)S(1)} %broadcast_in_dim.30, f32[2,1152]{1,0:T(2,128)S(1)} %reshape.344, f32[6,1152]{1,0:T(8,128)S(1)} %reshape.345), dimensions={0} | concatenate | bytes 43517952 | tf_op jit(solution)/shard_map/concatenate | solution.py:334
  1249.9 22.8 reshape.346
  1274.8 1198.8 %all-reduce.14.cloned.1.call-done = (f32[15980544]{0:T(1024)}, f32[5439744]{0:T(1024)}) async-done(((f32[15980544]{0:T(1024)}, f32[5439744]{0:T(1024)}), (f32[15980544]{0:T(1024)}, f32[5439744]{0:T(1024)})) %all-reduce.14.cloned.1.call-update) | async-done | bytes 85681168
  2480.3 39.4 %all-reduce.8 = (f32[]{:T(128)}, f32[]{:T(128)}) all-reduce(f32[]{:T(128)} %get-tuple-element.54, f32[]{:T(128)S(6)} %add.320), channel_id=1, replica_groups=mesh['dp'=8,'mod'=4] {'dp','mod'}, use_global_device_ids=true, to_apply=%region_11.12 | all-reduce | flops 2 | bytes 16 | tf_op jit(solution)/shard_map/psum | solution.py:297
  2520.5 7.2 divide_subtract_fusion
  (372 shorter events, 178.6 us)
Async XLA Ops:
  8.0 722.9 %all-reduce.16.cloned.1.call-start = ((), (), s32[]{:S(2)}) async-start(), calls=%async_computation.6 | async-start | bytes 85684224
  47.3 767.5 %all-gather.3.cloned.1.call-start = ((), (), s32[]{:S(2)}) async-start(), calls=%async_computation.3 | async-start | bytes 4644864 | tf_op jit(solution)/shard_map/all_gather | solution.py:281
  56.7 677.1 %copy-start.102 = (f32[2]{0:T(128)}, f32[2]{0:T(128)S(1)}, u32[]{:S(2)}) copy-start(f32[2]{0:T(128)S(1)} %get-tuple-element.22) | copy-start | bytes 28
  57.2 746.3 %copy-start.106 = (s32[2]{0:T(128)}, s32[2]{0:T(128)S(1)}, u32[]{:S(2)}) copy-start(s32[2]{0:T(128)S(1)} %compare_select_fusion) | copy-start | bytes 28
  57.3 745.5 %copy-start.98 = (bf16[2,128]{1,0:T(2,128)(2,1)}, bf16[2,128]{1,0:T(2,128)(2,1)S(1)}, u32[]{:S(2)}) copy-start(bf16[2,128]{1,0:T(2,128)(2,1)S(1)} %get-tuple-element.73) | copy-start | bytes 1540
  57.3 745.5 %copy-start.100 = (bf16[2,128]{1,0:T(2,128)(2,1)}, bf16[2,128]{1,0:T(2,128)(2,1)S(1)}, u32[]{:S(2)}) copy-start(bf16[2,128]{1,0:T(2,128)(2,1)S(1)} %get-tuple-element.74) | copy-start | bytes 1540
  57.5 764.7 %copy-start.44 = (bf16[2,256,16]{1,2,0:T(8,128)(2,1)}, bf16[2,256,16]{1,2,0:T(8,128)(2,1)S(1)}, u32[]{:S(2)}) copy-start(bf16[2,256,16]{1,2,0:T(8,128)(2,1)S(1)} %fusion.38) | copy-start | bytes 49156
  805.6 16.6 copy-start.22
  818.2 22.0 all-to-all-start
  822.1 450.7 %reduce-scatter.2.cloned.1.call-start = ((), (), s32[]{:S(2)}) async-start(), calls=%async_computation.4 | async-start | bytes 4644864 | tf_op jit(solution)/shard_map/reduce_scatter | solution.py:323
  823.7 18.5 copy-start.1
  823.7 18.5 copy-start.88
  868.9 69.3 %copy-start.74 = (f32[2,256]{1,0:T(2,128)}, f32[2,256]{1,0:T(2,128)S(1)}, u32[]{:S(2)}) copy-start(f32[2,256]{1,0:T(2,128)S(1)} %broadcast_multiply_fusion.1) | copy-start | bytes 6148
  869.3 68.9 %copy-start.81 = (f32[2,256]{1,0:T(2,128)}, f32[2,256]{1,0:T(2,128)S(1)}, u32[]{:S(2)}) copy-start(f32[2,256]{1,0:T(2,128)S(1)} %fusion.67) | copy-start | bytes 6148
  869.7 13.2 copy-start.66
  908.2 30.0 %copy-start.10 = (f32[2,256,1152]{2,1,0:T(8,128)}, f32[2,256,1152]{2,1,0:T(8,128)S(1)}, u32[]{:S(2)}) copy-start(f32[2,256,1152]{2,1,0:T(8,128)S(1)} %get-tuple-element.45) | copy-start | bytes 7077892
  989.9 1483.8 %all-reduce.14.cloned.1.call-start = ((), (), s32[]{:S(2)}) async-start(), calls=%async_computation.5 | async-start | bytes 171368448
  996.9 17.2 slice-start.2
  1102.1 58.1 %copy-start.76 = (f32[1152]{0:T(1024)S(1)}, f32[1152]{0:T(1024)}, u32[]{:S(2)}) copy-start(f32[1152]{0:T(1024)} %get-tuple-element.17) | copy-start | bytes 13828
  1102.1 58.1 %copy-start.45 = (f32[2,1152]{1,0:T(2,128)S(1)}, f32[2,1152]{1,0:T(2,128)}, u32[]{:S(2)}) copy-start(f32[2,1152]{1,0:T(2,128)} %get-tuple-element.13) | copy-start | bytes 27652
  1102.1 58.1 %copy-start.46 = (f32[2,1152]{1,0:T(2,128)S(1)}, f32[2,1152]{1,0:T(2,128)}, u32[]{:S(2)}) copy-start(f32[2,1152]{1,0:T(2,128)} %get-tuple-element.19) | copy-start | bytes 27652
  1102.1 58.2 %copy-start.62 = (bf16[2,1152]{1,0:T(2,128)(2,1)S(1)}, bf16[2,1152]{1,0:T(2,128)(2,1)}, u32[]{:S(2)}) copy-start(bf16[2,1152]{1,0:T(2,128)(2,1)} %copy-done.60) | copy-start | bytes 13828
  1165.9 14.0 copy-start.68
  1272.7 1247.7 %copy-start.18 = (f32[499392]{0:T(1024)S(1)}, f32[499392]{0:T(1024)}, u32[]{:S(2)}) copy-start(f32[499392]{0:T(1024)} %param.19) | copy-start | bytes 5992708
  (98 other events, 468.3 us)
Sparse Core Ops, SparseCore 0:
  47.4 683.4 all-reduce.15
  1272.8 1200.7 all-reduce.13
Sparse Core Ops, SparseCore 1:
  50.7 103.4 all-gather.2
  989.9 85.0 reduce-scatter.1
where the time goes:
time: 2560 us; the launch traced here: 2540 us
  waiting for transfers between devices  1870 us (73%)
  local copies, waits for them, and re-layouts  351 us (14%)
  matrix products  185 us (7%)
  blocking collectives  62 us (2%)
  other arithmetic  45.7 us (2%)
    unnamed x6, waiting for transfers between devices  1870 us
    dot_general x34, matrix products, matmul(): return jnp.einsum(form, left, right, preferred_element_type=jnp.float32)  180 us
    concatenate x1, local copies, waits for them, and re-layouts, shards(): block_grad = jnp.concatenate([layer_grad, grad_patch, grad_head], 1)  68.8 us
    reshape x1, local copies, waits for them, and re-layouts, shards(): block_grad.reshape(D * WB)  58.1 us
    concatenate x1, local copies, waits for them, and re-layouts, shards(): jnp.concatenate([grad_time, grad_time2, grad_table, grad_final, jnp.sum(s...  56.6 us
  transfers between devices with their start and end apart: 5, of which 2 were waited for; matrix products, arithmetic and copies ran while one was open for 15% of the time, Pallas kernels for 0%

commit v1 on v0

v1 whole, which is shorter than its diff:
```python
import functools
import math

import jax
import jax.numpy as jnp
from jax import lax
from jax.sharding import PartitionSpec as P

D = 1152
HEADS = 16
HEAD_DIM = 72
FF = 4608
CLASSES = 1000
PATCH = 16
GRID = 16
FREQ = 256
TSTEPS = 1000
STEP = 10
SEQ = 256
WB = 13872
SROWS = 4722


HIGHEST_PRECISION = lax.Precision.HIGHEST
AXES = ("dp", "mod")
LOG_TWO = math.log(2.0)
THRESHOLD = 1.0
LEARN_RATE = 0.05
BETA_ONE = 0.9
BETA_TWO = 0.999
EPSILON = 1e-08


def matmul(form, left, right):
    return jnp.einsum(form, left, right, preferred_element_type=jnp.float32)


def plan(steps):
    step_index = jnp.arange(TSTEPS).astype(jnp.float32)
    beta_rows = 0.0001 + (0.02 - 0.0001) * step_index / (TSTEPS - 1)
    alpha_bar = jnp.cumprod(1.0 - beta_rows)
    previous = jnp.concatenate([jnp.ones((1,), jnp.float32), alpha_bar[:-1]])
    posterior = beta_rows * (1.0 - previous) / (1.0 - alpha_bar)
    clipped = jnp.concatenate([posterior[1:2], posterior[1:]])
    mean_factor = beta_rows * beta_rows * previous / ((1.0 - alpha_bar) * alpha_bar)
    plan_table = jnp.stack(
        [
            jnp.sqrt(alpha_bar),
            jnp.sqrt(1.0 - alpha_bar),
            mean_factor,
            jnp.log(clipped),
            jnp.log(beta_rows),
        ],
        1,
    )
    one_hot = (steps[:, None] == jnp.arange(TSTEPS)[None, :]).astype(jnp.float32)
    return jnp.dot(one_hot, plan_table, precision=HIGHEST_PRECISION)


def positions():
    quarter = D // 4
    omegas = 1.0 / 10000.0 ** (jnp.arange(quarter).astype(jnp.float32) / quarter)
    cells = jnp.arange(SEQ)
    column_angle = (cells % GRID).astype(jnp.float32)[:, None] * omegas[None, :]
    row_angle = (cells // GRID).astype(jnp.float32)[:, None] * omegas[None, :]
    return jnp.concatenate(
        [jnp.sin(column_angle), jnp.cos(column_angle), jnp.sin(row_angle), jnp.cos(row_angle)], 1
    )


def frequencies(steps):
    half_count = FREQ // 2
    frequency = jnp.exp(
        -math.log(10000.0) * jnp.arange(half_count).astype(jnp.float32) / half_count
    )
    angles = steps.astype(jnp.float32)[:, None] * frequency[None, :]
    return jnp.concatenate([jnp.cos(angles), jnp.sin(angles)], 1)


def modulate(stream, shifts, scales):
    average = jnp.mean(stream, -1, keepdims=True)
    centred = stream - average
    variance = jnp.mean(centred * centred, -1, keepdims=True)
    return centred * lax.rsqrt(variance + 1e-06) * (1.0 + scales[:, None, :]) + shifts[:, None, :]


def modulate_back(stream, shifts, scales, cotangent):
    unused, pullback = jax.vjp(modulate, stream, shifts, scales)
    return pullback(cotangent)


def smooth_back(function, inputs, cotangent):
    unused, pullback = jax.vjp(function, inputs)
    return pullback(cotangent)[0]


def gelu_tanh(inputs):
    return jax.nn.gelu(inputs, approximate=True)


def loss_terms(prediction, target, sched):
    guessed = prediction[..., :PATCH]
    variance_raw = prediction[..., PATCH:]
    mean_factor = sched[:, 2][:, None, None]
    posterior_log = sched[:, 3][:, None, None]
    beta_log = sched[:, 4][:, None, None]
    blend = 0.5 * (variance_raw + 1.0)
    model_log = blend * beta_log + (1.0 - blend) * posterior_log
    errors = guessed - target
    bound_term = 0.5 * (
        -1.0
        + model_log
        - posterior_log
        + jnp.exp(posterior_log - model_log)
        + mean_factor * errors * errors * jnp.exp(-model_log)
    )
    return jnp.sum(errors * errors + bound_term / LOG_TWO)


class Links:
    def __init__(self, dp, mod):
        self.core = 2 if mod % 2 == 0 else 1
        self.y = mod // self.core
        self.x = self.y if dp % self.y == 0 else 1
        self.z = dp // self.x
        self.count = dp * mod
        self.size = {"z": self.z, "x": self.x, "y": self.y, "c": self.core}
        self.dim = {"z": 0, "x": 1, "y": 2}

    def place(self, axis):
        index = lax.axis_index(AXES)
        below = {"c": 1, "y": self.core, "x": self.core * self.y, "z": self.core * self.y * self.x}
        return index // below[axis] % self.size[axis]

    def send(self, block, axis, shift=1):
        pairs = []
        for index in range(self.count):
            spot = {
                "c": index % self.core,
                "y": index // self.core % self.y,
                "x": index // (self.core * self.y) % self.x,
                "z": index // (self.core * self.y * self.x),
            }
            spot[axis] = (spot[axis] + shift) % self.size[axis]
            target = ((spot["z"] * self.x + spot["x"]) * self.y + spot["y"]) * self.core + spot["c"]
            pairs.append((index, target))
        return lax.ppermute(block, AXES, pairs)

    def gather(self, block, axis):
        extent, dim = self.size[axis], self.dim[axis]
        if extent == 1:
            return block
        own = self.place(axis)
        pieces = [block] + [self.send(block, axis, shift) for shift in range(1, extent)]
        if extent == 2:
            return jnp.where(
                own == 0,
                jnp.concatenate(pieces, dim),
                jnp.concatenate(pieces[::-1], dim),
            )
        whole = jnp.concatenate(pieces, dim)
        for shift, piece in enumerate(pieces):
            whole = lax.dynamic_update_slice_in_dim(whole, piece, (own - shift) % extent, dim)
        return whole

    def reduce(self, block, axis, kind):
        extent, dim = self.size[axis], self.dim[axis]
        if extent == 1:
            return block
        own = self.place(axis)
        total = lax.dynamic_slice_in_dim(block, own, 1, dim)
        for shift in range(1, extent):
            part = lax.dynamic_slice_in_dim(block, (own + shift) % extent, 1, dim)
            total = total + self.send(part.astype(kind), axis, shift).astype(jnp.float32)
        return total

    def spread(self, block):
        copies = jnp.broadcast_to(block[None], (self.count, *block.shape))
        return lax.all_to_all(copies, AXES, split_axis=0, concat_axis=0, tiled=True)

    def deliver(self, blocks):
        return lax.all_to_all(blocks, AXES, split_axis=0, concat_axis=0, tiled=True)


def pick(own, first, second):
    return jnp.where(own == 0, first, second)


def joined(own, mine, other, dim):
    return pick(
        own, jnp.concatenate([mine, other], dim), jnp.concatenate([other, mine], dim)
    )


def column_half(rows, half):
    small = D // 2
    q_k_v_o = [rows[:, part * D + half * small : part * D + (half + 1) * small] for part in range(4)]
    up = rows[:, 4 * D + half * (FF // 2) : 4 * D + (half + 1) * (FF // 2)]
    down = rows[:, 4 * D + FF + half * (FF // 2) : 4 * D + FF + (half + 1) * (FF // 2)]
    return [
        jnp.concatenate(q_k_v_o[:2], 1),
        jnp.concatenate(q_k_v_o[2:], 1),
        up[:, :D],
        up[:, D:],
        down[:, :D],
        down[:, D:],
    ]


def whole_columns(first, second):
    small = D // 2
    pieces = [
        first[0][:, :small], second[0][:, :small],
        first[0][:, small:], second[0][:, small:],
        first[1][:, :small], second[1][:, :small],
        first[1][:, small:], second[1][:, small:],
        first[2], first[3], second[2], second[3],
        first[4], first[5], second[4], second[5],
    ]
    return jnp.concatenate(pieces, 1)


def chip_rows(links, flat):
    core = links.place("c")
    per_chip = D * links.core // links.count
    if (D % links.count) == 0:
        rows = flat.reshape(D // links.count, WB).astype(jnp.bfloat16)
        halves = [jnp.stack(column_half(rows, half)) for half in range(2)]
        small = rows[:, WB - PATCH - 2 * PATCH :]
        mine = pick(core, halves[0], halves[1])
        other = links.send(pick(core, halves[1], halves[0]), "c")
        both = joined(core, mine, other, 1)
        return both, joined(core, small, links.send(small, "c"), 0)
    low = flat.astype(jnp.bfloat16)
    rows = joined(core, low, links.send(low, "c"), 0).reshape(per_chip, WB)
    halves = [jnp.stack(column_half(rows, half)) for half in range(2)]
    return pick(core, halves[0], halves[1]), rows[:, WB - PATCH - 2 * PATCH :]


def gather_block(links, flat):
    chunks, small = chip_rows(links, flat)
    grid = lambda block: block[None, None, None]
    small = links.gather(links.gather(links.gather(grid(small), "z"), "x"), "y").reshape(D, -1)
    own = []
    for group in range(3):
        left, right = grid(chunks[2 * group]), grid(chunks[2 * group + 1])
        if group < 2:
            pair = links.gather(jnp.concatenate([left, right], 4), "z")
            left, right = pair[..., :D], pair[..., D:]
            left, right = links.gather(left, "x"), links.gather(right, "y")
        else:
            left, right = links.gather(left, "x"), links.gather(right, "y")
            left, right = links.gather(left, "z"), links.gather(right, "z")
        left, right = links.gather(left, "y"), links.gather(right, "x")
        own += [left.reshape(D, D), right.reshape(D, D)]
    other = [links.send(block, "c") for block in own]
    return own, other, small[:, :PATCH], small[:, PATCH:]


def reduce_pair(links, left, right, kind=jnp.bfloat16):
    per_chip = D * links.core // links.count
    shape = (links.z, links.x, links.y, per_chip)
    left, right = left.reshape(*shape, -1), right.reshape(*shape, -1)
    left, right = links.reduce(left, "y", kind), links.reduce(right, "x", kind)
    left, right = links.reduce(left, "x", kind), links.reduce(right, "y", kind)
    left, right = links.reduce(left, "z", kind), links.reduce(right, "z", kind)
    return left.reshape(per_chip, -1), right.reshape(per_chip, -1)


def flat_gradient(links, chunks, small):
    core = links.place("c")
    if (D % links.count) == 0:
        per_device = D // links.count
        stacked = jnp.stack(chunks)
        mine = lax.dynamic_slice_in_dim(stacked, core * per_device, per_device, 1)
        sent = lax.dynamic_slice_in_dim(stacked, (1 - core) * per_device, per_device, 1)
        other = links.send(sent, "c")
        rows = jnp.concatenate(
            [
                whole_columns(pick(core, mine, other), pick(core, other, mine)),
                lax.dynamic_slice_in_dim(small, core * per_device, per_device, 0),
            ],
            1,
        )
        return rows.reshape(per_device * WB)
    stacked = jnp.stack(chunks)
    other = links.send(stacked, "c")
    rows = jnp.concatenate(
        [whole_columns(pick(core, stacked, other), pick(core, other, stacked)), small], 1
    )
    flat = rows.reshape(-1)
    part = flat.shape[0] // 2
    return lax.dynamic_slice_in_dim(flat, core * part, part)


EXTENTS = [FREQ, D, CLASSES + 1, 2 * D, 1, 2, 6]
STARTS = [sum(EXTENTS[:index]) for index in range(len(EXTENTS) + 1)]


class Window:
    def __init__(self, links, length):
        self.length = length
        begins = [index * length for index in range(links.count)]
        rows = max((begin % D + length + D - 1) // D for begin in begins)
        self.rows = (rows + 15) // 16 * 16
        begin = lax.axis_index(AXES) * length
        self.first = begin // D
        self.offset = begin - self.first * D

    def fill(self, flat):
        padded = jnp.concatenate(
            [jnp.zeros((D,), flat.dtype), flat, jnp.zeros((self.rows * D,), flat.dtype)]
        )
        return lax.dynamic_slice_in_dim(padded, D - self.offset, self.rows * D).reshape(
            self.rows, D
        )

    def cut(self, columns, start):
        full = jnp.pad(columns, ((0, 0), (start, SROWS + self.rows - start - columns.shape[1])))
        return lax.dynamic_slice_in_dim(full, self.first, self.rows, 1)

    def put(self, columns, start, extent):
        full = jnp.zeros((columns.shape[0], SROWS + self.rows), columns.dtype)
        full = lax.dynamic_update_slice_in_dim(full, columns, self.first, 1)
        return full[:, start : start + extent]

    def flatten(self, rows):
        return lax.dynamic_slice_in_dim(rows.reshape(-1), self.offset, self.length)


def adam_update(weight, gradient, first, second):
    first_new = BETA_ONE * first + (1.0 - BETA_ONE) * gradient
    second_new = BETA_TWO * second + (1.0 - BETA_TWO) * gradient * gradient
    corrected = first_new / (1.0 - BETA_ONE**STEP)
    spread = jnp.sqrt(second_new / (1.0 - BETA_TWO**STEP))
    return (weight - LEARN_RATE * corrected / (spread + EPSILON), first_new, second_new)


def attend(normed, w_qk, w_v):
    images = normed.shape[0]
    heads = HEADS // 2
    low = jnp.bfloat16
    qk = matmul("isd,de->ise", normed, w_qk).astype(low).reshape(images, SEQ, 2, heads, HEAD_DIM)
    values = matmul("isd,de->ise", normed, w_v).astype(low).reshape(images, SEQ, heads, HEAD_DIM)
    queries, keys = qk[:, :, 0], qk[:, :, 1]
    scores = matmul("iqhe,ikhe->ihqk", queries, keys) * (1.0 / math.sqrt(HEAD_DIM))
    totals = jax.nn.logsumexp(scores, axis=-1)
    weights = jnp.exp(scores - totals[..., None]).astype(low)
    mixed = matmul("ihqk,ikhe->iqhe", weights, values).astype(low)
    return mixed.reshape(images, SEQ, D // 2), (queries, keys, values, totals)


def attend_back(kept, mixed_grad):
    queries, keys, values, totals = kept
    images = queries.shape[0]
    low = jnp.bfloat16
    mixed_grad = mixed_grad.astype(low).reshape(images, SEQ, HEADS // 2, HEAD_DIM)
    score_scale = 1.0 / math.sqrt(HEAD_DIM)
    softmax_rows = jnp.exp(
        matmul("iqhe,ikhe->ihqk", queries, keys) * score_scale - totals[..., None]
    )
    weight_grad = matmul("iqhe,ikhe->ihqk", mixed_grad, values)
    score_grad = (
        softmax_rows * (weight_grad - jnp.sum(weight_grad * softmax_rows, -1, keepdims=True))
    ).astype(low)
    query_grad = (matmul("ihqk,ikhe->iqhe", score_grad, keys) * score_scale).astype(low)
    key_grad = (matmul("ihqk,iqhe->ikhe", score_grad, queries) * score_scale).astype(low)
    value_grad = matmul("ihqk,iqhe->ikhe", softmax_rows.astype(low), mixed_grad).astype(low)
    return (
        jnp.stack([query_grad, key_grad], 2).reshape(images, SEQ, D),
        value_grad.reshape(images, SEQ, D // 2),
    )


def shards(
    links,
    latents,
    noise,
    timesteps,
    labels,
    dropped,
    block_master,
    block_m,
    block_v,
    stem_master,
    stem_m,
    stem_v,
    ada_w,
    ada_w_m,
    ada_w_v,
):
    low, wide = jnp.bfloat16, jnp.float32
    images = timesteps.shape[0]
    everyone = links.count * images
    own_cols = ada_w.shape[1]
    own_rows = ada_w.shape[0]
    row_at = lax.axis_index("dp") * own_rows
    col_at = lax.axis_index("mod") * own_cols
    groups = 6 * D // own_cols

    own, other, w_patch, w_head = gather_block(links, block_master)
    halves = (own, other)

    window = Window(links, stem_master.shape[0])
    stem = window.fill(stem_master.astype(low))
    ada_low = ada_w.astype(low)
    integers = links.spread(jnp.stack([timesteps, jnp.where(dropped == 1, CLASSES, labels)]))
    all_steps = integers[:, 0].reshape(everyone)
    chosen = integers[:, 1].reshape(everyone)
    timing = frequencies(all_steps).astype(low)
    one_hot = (chosen[:, None] == jnp.arange(CLASSES + 1)[None, :]).astype(low)
    bias_start, bias_extent = STARTS[4], 9
    bias_share = -(-bias_extent * D // links.count)
    mark = jnp.arange(bias_extent)[:, None] + bias_start == (
        window.first + jnp.arange(window.rows)
    )
    bias_part = matmul("br,rd->bd", mark.astype(low), stem).reshape(bias_extent * D)
    bias_part = jnp.pad(bias_part, (0, bias_share * links.count - bias_extent * D))

    before_part = matmul("ir,rd->id", window.cut(timing, STARTS[0]), stem)
    got = links.deliver(
        jnp.concatenate(
            [
                before_part.reshape(links.count, images * D),
                bias_part.reshape(links.count, bias_share),
            ],
            1,
        )
    ).sum(0)
    before = got[: images * D].reshape(images, D)
    time_hidden = jax.nn.silu(before).astype(low)
    got = links.spread(
        jnp.concatenate([time_hidden.reshape(images * D), got[images * D :].astype(low)])
    )
    all_hidden = got[:, : images * D].reshape(everyone, D)
    biases = got[:, images * D :].reshape(-1)[: bias_extent * D].reshape(bias_extent, D)
    biases = biases.astype(wide)
    left = window.cut(jnp.concatenate([all_hidden, one_hot], 1), STARTS[1])
    condition = links.deliver(
        matmul("ir,rd->id", left, stem).reshape(links.count, images, D)
    ).sum(0)
    signal = jax.nn.silu(condition).astype(low)
    all_signal = links.spread(signal).reshape(everyone, D)
    signal_rows = lax.dynamic_slice_in_dim(all_signal, row_at, own_rows, 1)
    parts = links.deliver(
        matmul("ir,rc->ic", signal_rows, ada_low).reshape(links.count, images, own_cols)
    )
    modulation = (
        parts.reshape(-1, groups, images, own_cols).sum(0).transpose(1, 0, 2).reshape(images, 6 * D)
        + biases[3:].reshape(6 * D)
    ).astype(low)
    pieces = jnp.split(modulation.astype(wide), 6, axis=1)
    final_part = window.put(matmul("id,rd->ir", all_signal, stem), STARTS[3], 2 * D)
    final_mod = links.deliver(final_part.reshape(links.count, images, 2 * D)).sum(0) + biases[
        1:3
    ].reshape(2 * D)
    final_shift, final_scale = final_mod[:, :D], final_mod[:, D:]

    sched = plan(timesteps)
    target = noise.reshape(images, SEQ, PATCH)
    noisy_rows = (
        sched[:, 0][:, None, None] * latents.reshape(images, SEQ, PATCH)
        + sched[:, 1][:, None, None] * target
    ).astype(low)
    stream = matmul("isp,dp->isd", noisy_rows, w_patch) + biases[0] + positions()[None]
    normed = modulate(stream, pieces[0], pieces[1]).astype(low)
    w_v = [half[1][:, : D // 2] for half in halves]
    w_proj = [half[1][:, D // 2 :] for half in halves]
    mixed, kept = [], []
    for half in range(2):
        rows, saved = attend(normed, halves[half][0], w_v[half])
        mixed.append(rows)
        kept.append(saved)
    attended = sum(matmul("isd,od->iso", mixed[half], w_proj[half]) for half in range(2))
    middle = stream + pieces[2][:, None, :] * attended
    second = modulate(middle, pieces[3], pieces[4]).astype(low)
    inner, active = [], []
    output = 0.0
    for half in range(2):
        for chunk in range(2):
            rows = matmul("isd,df->isf", second, halves[half][2 + chunk])
            inner.append(rows)
            active.append(gelu_tanh(rows).astype(low))
    for half in range(2):
        for chunk in range(2):
            output = output + matmul("isf,of->iso", active[2 * half + chunk], halves[half][4 + chunk])
    layer_out = middle + pieces[5][:, None, :] * output
    final_normed = modulate(layer_out, final_shift, final_scale).astype(low)
    prediction = matmul("isd,do->iso", final_normed, w_head)
    loss_local, loss_back = jax.vjp(
        lambda predicted: loss_terms(predicted, target, sched), prediction
    )

    def tokens(rows):
        return rows.reshape(images * SEQ, rows.shape[-1])

    def with_partner(mine, sent):
        return jnp.concatenate([tokens(mine), links.send(tokens(sent), "c")], 0)

    out_grad = loss_back(jnp.ones_like(loss_local))[0].astype(low)
    grad_head = matmul("iso,isd->do", out_grad, final_normed)
    upstream, shift_grad, scale_grad = modulate_back(
        layer_out, final_shift, final_scale, matmul("iso,do->isd", out_grad, w_head)
    )
    final_grad = jnp.concatenate([shift_grad, scale_grad], 1)
    down_in = (pieces[5][:, None, :] * upstream).astype(low)
    gate_b = jnp.sum(upstream * output, 1)
    down_both = with_partner(down_in, down_in)
    grad_down = [
        matmul("to,tf->of", down_both, with_partner(active[chunk], active[2 + chunk]))
        for chunk in range(2)
    ]
    reduced = [None] * 6
    reduced[4:] = reduce_pair(links, *grad_down)
    inner_grad = [
        smooth_back(
            gelu_tanh,
            inner[2 * half + chunk],
            matmul("iso,of->isf", down_in, halves[half][4 + chunk]),
        ).astype(low)
        for half in range(2)
        for chunk in range(2)
    ]
    second_both = with_partner(second, second)
    grad_up = [
        matmul("td,tf->df", second_both, with_partner(inner_grad[chunk], inner_grad[2 + chunk]))
        for chunk in range(2)
    ]
    reduced[2:4] = reduce_pair(links, *grad_up)
    second_grad = sum(
        matmul("isf,df->isd", inner_grad[2 * half + chunk], halves[half][2 + chunk])
        for half in range(2)
        for chunk in range(2)
    )
    back_mid, shift_b, scale_b = modulate_back(middle, pieces[3], pieces[4], second_grad)
    grad_mid = upstream + back_mid
    proj_in = (pieces[2][:, None, :] * grad_mid).astype(low)
    gate_a = jnp.sum(grad_mid * attended, 1)
    grad_proj = matmul("to,td->od", with_partner(proj_in, proj_in), with_partner(*mixed))
    qk_grad, v_grad = [], []
    for half in range(2):
        rows, more = attend_back(kept[half], matmul("iso,od->isd", proj_in, w_proj[half]))
        qk_grad.append(rows)
        v_grad.append(more)
    normed_both = with_partner(normed, normed)
    grad_qk = matmul("td,te->de", normed_both, with_partner(*qk_grad))
    grad_v = matmul("td,te->de", normed_both, with_partner(*v_grad))
    reduced[:2] = reduce_pair(links, grad_qk, jnp.concatenate([grad_v, grad_proj], 1))
    normed_grad = sum(
        matmul("ise,de->isd", qk_grad[half], halves[half][0])
        + matmul("ise,de->isd", v_grad[half], w_v[half])
        for half in range(2)
    )
    back_in, shift_a, scale_a = modulate_back(stream, pieces[0], pieces[1], normed_grad)
    stream_grad = grad_mid + back_in
    grad_patch = matmul("isp,isd->dp", noisy_rows, stream_grad.astype(low))
    small = jnp.concatenate([grad_patch, grad_head], 1)
    small = small + links.send(small, "c") if links.core == 2 else small
    small = small.reshape(links.z, links.x, links.y, -1, 3 * PATCH)
    for axis in "yxz":
        small = links.reduce(small, axis, wide)
    small = small.reshape(-1, 3 * PATCH)

    modulation_low = jnp.concatenate(
        [shift_a, scale_a, gate_a, shift_b, scale_b, gate_b], 1
    ).astype(low)
    final_low = final_grad.astype(low)
    sums = jnp.concatenate([jnp.sum(stream_grad, (0, 1)), jnp.sum(final_grad, 0)])
    all_sums = links.spread(sums).sum(0)
    all_final = links.spread(final_low).reshape(everyone, 2 * D)
    all_modulation = links.spread(modulation_low).reshape(everyone, 6 * D)
    own_modulation = lax.dynamic_slice_in_dim(all_modulation, col_at, own_cols, 1)
    ada_grad = matmul("ir,ic->rc", signal_rows, own_modulation)
    signal_part = matmul("ir,rd->id", window.cut(all_final, STARTS[3]), stem)
    ada_part = matmul("ic,rc->ir", own_modulation, ada_low)
    signal_part = lax.dynamic_update_slice_in_dim(
        signal_part,
        lax.dynamic_slice_in_dim(signal_part, row_at, own_rows, 1) + ada_part,
        row_at,
        1,
    )
    signal_grad = links.deliver(signal_part.reshape(links.count, images, D)).sum(0)
    condition_grad = smooth_back(jax.nn.silu, condition, signal_grad)
    all_condition = links.spread(condition_grad).reshape(everyone, D)
    condition_low = all_condition.astype(low)
    hidden_part = window.put(matmul("id,rd->ir", condition_low, stem), STARTS[1], D)
    hidden_grad = links.deliver(hidden_part.reshape(links.count, images, D)).sum(0)
    before_grad = smooth_back(jax.nn.silu, before, hidden_grad).astype(low)
    all_before = links.spread(before_grad).reshape(everyone, D)
    bias_rows = jnp.concatenate(
        [all_sums, jnp.sum(all_modulation.astype(wide), 0)]
    ).reshape(bias_extent, D)
    low_left = jnp.concatenate(
        [
            window.cut(timing, STARTS[0]),
            window.cut(all_hidden, STARTS[1]),
            window.cut(all_final, STARTS[3]),
        ],
        0,
    )
    low_right = jnp.concatenate([all_before, condition_low, all_signal], 0)
    stem_rows = matmul("ir,id->rd", low_left, low_right)
    wide_left = jnp.concatenate(
        [window.cut(one_hot.astype(wide), STARTS[2]), mark.astype(wide)], 0
    )
    wide_right = jnp.concatenate([all_condition, bias_rows], 0)
    stem_rows = stem_rows + jnp.dot(wide_left.T, wide_right, precision=HIGHEST_PRECISION)
    stem_grad = window.flatten(stem_rows)

    block_grad = flat_gradient(links, reduced, small)
    squares = (
        jnp.sum(block_grad * block_grad)
        + jnp.sum(stem_grad * stem_grad)
        + jnp.sum(ada_grad * ada_grad)
    )
    totals = links.spread(jnp.stack([loss_local, squares])).sum(0)
    loss_total = totals[0]
    grad_norm = jnp.sqrt(totals[1])
    factor = THRESHOLD / jnp.maximum(grad_norm, THRESHOLD)
    block_new = adam_update(block_master, block_grad * factor, block_m, block_v)
    stem_new = adam_update(stem_master, stem_grad * factor, stem_m, stem_v)
    ada_new = adam_update(ada_w, ada_grad * factor, ada_w_m, ada_w_v)
    return (loss_total, grad_norm, *block_new, *stem_new, *ada_new)


def solution(mesh):
    return jax.shard_map(
        functools.partial(shards, Links(mesh.shape["dp"], mesh.shape["mod"])),
        mesh=mesh,
        in_specs=(
            P(("dp", "mod"), None),
            P(("dp", "mod"), None),
            P(("dp", "mod")),
            P(("dp", "mod")),
            P(("dp", "mod")),
            P(("dp", "mod")),
            P(("dp", "mod")),
            P(("dp", "mod")),
            P(("dp", "mod")),
            P(("dp", "mod")),
            P(("dp", "mod")),
            P("dp", "mod"),
            P("dp", "mod"),
            P("dp", "mod"),
        ),
        out_specs=(
            P(),
            P(),
            P(("dp", "mod")),
            P(("dp", "mod")),
            P(("dp", "mod")),
            P(("dp", "mod")),
            P(("dp", "mod")),
            P(("dp", "mod")),
            P("dp", "mod"),
            P("dp", "mod"),
            P("dp", "mod"),
        ),
        check_vma=False,
    )
```

time: 2560 us -> 873 us (0.34)
  waiting for transfers between devices: 1870 us -> 210 us
  local copies, waits for them, and re-layouts: 351 us -> 134 us
  starting transfers between devices: 4.03 us -> 199 us
  other arithmetic: 45.7 us -> 131 us
  blocking collectives: 62 us -> 9.09 us
    unnamed x6 -> x0, waiting for transfers between devices: 1870 us -> none
    ppermute x0 -> x85, starting transfers between devices: none -> 133 us  [send(): return lax.ppermute(block, AXES, pairs)]
    ppermute x0 -> x85, waiting for transfers between devices: none -> 122 us  [send(): return lax.ppermute(block, AXES, pairs)]
    reshape x6 -> x20, local copies, waits for them, and re-layouts: 126 us -> 9.61 us  [the longest x1 1.16 us: shards(): final_part.reshape(links.count, images, 2 * D)]
    concatenate x3 -> x6, local copies, waits for them, and re-layouts: 125 us -> 16.2 us  [the longest x1 7.01 us: shards(): jnp.concatenate([grad_v, grad_proj], 1)]
    all_to_all x1 -> x14, waiting for transfers between devices: 0.01 us -> 88.4 us  [the longest x8 50.8 us: spread(): return lax.all_to_all(copies, AXES, split_axis=0, concat_axis=0, tiled=True)]
    all_to_all x1 -> x14, starting transfers between devices: 3.86 us -> 66.2 us  [the longest x8 40.7 us: spread(): return lax.all_to_all(copies, AXES, split_axis=0, concat_axis=0, tiled=True)]
    select_n x2 -> x20, other arithmetic: 0.01 us -> 41.6 us  [the longest x14 36.6 us: gather(): jnp.where(own == 0, jnp.concatenate(pieces, dim), jnp.concatenate(pieces[...]
  transfers between devices with their start and end apart: 5 -> 99, of which waited for: 2 -> 22; matrix products, arithmetic and copies ran while one was open for 15% -> 45% of each run, Pallas kernels for 0% -> 0%
where the time goes in v1:
time: 873 us; the launch traced here: 861 us
  waiting for transfers between devices  210 us (24%)
  starting transfers between devices  199 us (23%)
  matrix products  170 us (19%)
  local copies, waits for them, and re-layouts  134 us (15%)
  other arithmetic  131 us (15%)
  blocking collectives  9.09 us (1%)
    dot_general x62, matrix products, matmul(): return jnp.einsum(form, left, right, preferred_element_type=jnp.float32)  169 us
    ppermute x85, starting transfers between devices, send(): return lax.ppermute(block, AXES, pairs)  133 us
    ppermute x85, waiting for transfers between devices, send(): return lax.ppermute(block, AXES, pairs)  122 us
    all_to_all x8, waiting for transfers between devices, spread(): return lax.all_to_all(copies, AXES, split_axis=0, concat_axis=0, tiled=True)  50.8 us
    all_to_all x8, starting transfers between devices, spread(): return lax.all_to_all(copies, AXES, split_axis=0, concat_axis=0, tiled=True)  40.7 us
    all_to_all x6, waiting for transfers between devices, deliver(): return lax.all_to_all(blocks, AXES, split_axis=0, concat_axis=0, tiled=True)  37.6 us
    select_n x14, other arithmetic, gather(): jnp.where(own == 0, jnp.concatenate(pieces, dim), jnp.concatenate(pieces[...  36.6 us
    unnamed x257, local copies, waits for them, and re-layouts  27.3 us
  transfers between devices with their start and end apart: 99, of which 22 were waited for; matrix products, arithmetic and copies ran while one was open for 45% of the time, Pallas kernels for 0%

profile of v1, /device:TPU:0, one launch (start us, length us, event | category | flops | bytes accessed | tf_op | source)
XLA Modules:
  0.0 861.1 jit_solution(16047003038174771285)
XLA Ops:
  2.6 7.3 all-to-all-start
  89.1 16.8 %collective-permute-done.17 = bf16[1,1,1,72,2304]{4,3,2,1,0:T(8,128)(2,1)S(1)} collective-permute-done((bf16[1,1,1,72,2304]{4,3,2,1,0:T(8,128)(2,1)}, bf16[1,1,1,72,2304]{4,3,2,1,0:T(8,128)(2,1)S(1)}, u32[]{:S(2)}, u32[]{:S(2)}) %collective-permute-start.17) | collective-permute-done | bytes 331808 | tf_op jit(solution)/shard_map/ppermute | solution.py:147
  112.2 17.6 %collective-permute-start.29 = (bf16[1,1,2,72,1152]{4,3,2,1,0:T(8,128)(2,1)}, bf16[1,1,2,72,1152]{4,3,2,1,0:T(8,128)(2,1)}, u32[]{:S(2)}, u32[]{:S(2)}) collective-permute-start(bf16[1,1,2,72,1152]{4,3,2,1,0:T(8,128)(2,1)} %maximum_select_fusion.12), channel_id=1, source_target_pairs={{0,8},{1,9},{2,10},{3,11},{4,12},{5,13},{6,14},{7,15},{8,16},{9,17... | collective-permute-start | bytes 995336 | tf_op jit(solution)/shard_map/ppermute | solution.py:147
  129.9 8.5 collective-permute-done.8
  138.3 12.3 %collective-permute-start.23 = (bf16[1,2,1,72,1152]{4,3,2,1,0:T(8,128)(2,1)}, bf16[1,2,1,72,1152]{4,3,2,1,0:T(8,128)(2,1)}, u32[]{:S(2)}, u32[]{:S(2)}) collective-permute-start(bf16[1,2,1,72,1152]{4,3,2,1,0:T(8,128)(2,1)} %maximum_select_fusion.11), channel_id=1, source_target_pairs={{0,16},{1,17},{2,18},{3,19},{4,20},{5,21},{6,22},{7,23},{8,24},{9,... | collective-permute-start | bytes 995336 | tf_op jit(solution)/shard_map/ppermute | solution.py:147
  201.2 5.5 all-to-all-start.4
  214.6 45.7 %all-to-all-done.4 = bf16[32,2,1152]{2,1,0:T(2,128)(2,1)S(1)} async-done(((bf16[32,2,1152]{2,1,0:T(2,128)(2,1)}), bf16[32,2,1152]{2,1,0:T(2,128)(2,1)S(1)}, u32[]{:S(2)}, u32[]{:S(2)}) %all-to-all-start.4) | async-done | bytes 147488 | tf_op jit(solution)/shard_map/all_to_all | solution.py:179
  282.7 10.9 %all-to-all-done.5 = f32[32,2,1728]{2,1,0:T(2,128)} async-done(((f32[32,2,1728]{2,1,0:T(2,128)}), f32[32,2,1728]{2,1,0:T(2,128)}, u32[]{:S(2)}, u32[]{:S(2)}) %all-to-all-start.5) | async-done | bytes 442400 | tf_op jit(solution)/shard_map/all_to_all | solution.py:182
  429.7 5.3 fusion.42
  479.9 5.9 all-to-all-start.7
  550.7 7.0 copy.341
  558.1 5.6 fusion.50
  566.9 5.3 fusion.58
  605.6 5.7 fusion.70
  615.5 26.7 %all-to-all-done.9 = f32[32,2,1152]{2,1,0:T(2,128)S(1)} async-done(((f32[32,2,1152]{2,1,0:T(2,128)}), f32[32,2,1152]{2,1,0:T(2,128)S(1)}, u32[]{:S(2)}, u32[]{:S(2)}) %all-to-all-start.9) | async-done | bytes 294944 | tf_op jit(solution)/shard_map/all_to_all | solution.py:182
  670.9 11.7 %collective-permute-done.73 = bf16[4,1,2,72,1152]{4,3,2,1,0:T(8,128)(2,1)S(1)} collective-permute-done((bf16[4,1,2,72,1152]{4,3,2,1,0:T(8,128)(2,1)}, bf16[4,1,2,72,1152]{4,3,2,1,0:T(8,128)(2,1)S(1)}, u32[]{:S(2)}, u32[]{:S(2)}) %collective-permute-start.73) | collective-permute-done | bytes 1327136 | tf_op jit(solution)/shard_map/ppermute | solution.py:147
  704.6 8.9 %collective-permute-done.55 = bf16[4,1,1,72,1152]{4,3,2,1,0:T(8,128)(2,1)} collective-permute-done((bf16[4,1,1,72,1152]{4,3,2,1,0:T(8,128)(2,1)}, bf16[4,1,1,72,1152]{4,3,2,1,0:T(8,128)(2,1)}, u32[]{:S(2)}, u32[]{:S(2)}) %collective-permute-start.55) | collective-permute-done | bytes 663584 | tf_op jit(solution)/shard_map/ppermute | solution.py:147
  719.8 7.9 collective-permute-done.68
  737.8 9.5 %collective-permute-done.50 = bf16[1,1,1,72,1152]{4,3,2,1,0:T(8,128)(2,1)S(1)} collective-permute-done((bf16[1,1,1,72,1152]{4,3,2,1,0:T(8,128)(2,1)S(1)}, bf16[1,1,1,72,1152]{4,3,2,1,0:T(8,128)(2,1)S(1)}, u32[]{:S(2)}, u32[]{:S(2)}) %collective-permute-start.50) | collective-permute-done | bytes 165920 | tf_op jit(solution)/shard_map/ppermute | solution.py:147
  757.0 10.1 %collective-permute-done.57 = bf16[1,1,1,72,1152]{4,3,2,1,0:T(8,128)(2,1)S(1)} collective-permute-done((bf16[1,1,1,72,1152]{4,3,2,1,0:T(8,128)(2,1)S(1)}, bf16[1,1,1,72,1152]{4,3,2,1,0:T(8,128)(2,1)S(1)}, u32[]{:S(2)}, u32[]{:S(2)}) %collective-permute-start.57) | collective-permute-done | bytes 165920 | tf_op jit(solution)/shard_map/ppermute | solution.py:147
  771.4 10.0 %collective-permute-done.63 = bf16[1,1,1,72,1152]{4,3,2,1,0:T(8,128)(2,1)S(1)} collective-permute-done((bf16[1,1,1,72,1152]{4,3,2,1,0:T(8,128)(2,1)S(1)}, bf16[1,1,1,72,1152]{4,3,2,1,0:T(8,128)(2,1)S(1)}, u32[]{:S(2)}, u32[]{:S(2)}) %collective-permute-start.63) | collective-permute-done | bytes 165920 | tf_op jit(solution)/shard_map/ppermute | solution.py:147
  785.6 10.0 %collective-permute-done.70 = bf16[1,1,1,72,1152]{4,3,2,1,0:T(8,128)(2,1)S(1)} collective-permute-done((bf16[1,1,1,72,1152]{4,3,2,1,0:T(8,128)(2,1)S(1)}, bf16[1,1,1,72,1152]{4,3,2,1,0:T(8,128)(2,1)S(1)}, u32[]{:S(2)}, u32[]{:S(2)}) %collective-permute-start.70) | collective-permute-done | bytes 165920 | tf_op jit(solution)/shard_map/ppermute | solution.py:147
  795.7 6.1 collective-permute-done.76
  833.6 9.1 %all_to_all.85 = f32[32,1,2]{2,1,0:T(1,128)S(1)} all-to-all(f32[32,1,2]{2,1,0:T(1,128)S(1)} %broadcast_in_dim.55), channel_id=1, replica_groups=mesh['dp'=8,'mod'=4] {'dp','mod'}, dimensions={0} | all-to-all | bytes 512 | tf_op jit(solution)/shard_map/all_to_all | solution.py:179
  (782 shorter events, 584.4 us)
Async XLA Ops:
  73.8 80.5 %all-to-all-start.2 = ((bf16[32,2,1314]{2,1,0:T(2,128)(2,1)}), bf16[32,2,1314]{2,1,0:T(2,128)(2,1)}, u32[]{:S(2)}, u32[]{:S(2)}) async-start(bf16[32,2,1314]{2,1,0:T(2,128)(2,1)} %reshape.1140), calls=%async_computation.2 | async-start | bytes 360448 | tf_op jit(solution)/shard_map/all_to_all | solution.py:179
  84.2 54.1 %collective-permute-start.8 = (bf16[1,1,1,72,2304]{4,3,2,1,0:T(8,128)(2,1)}, bf16[1,1,1,72,2304]{4,3,2,1,0:T(8,128)(2,1)S(1)}, u32[]{:S(2)}, u32[]{:S(2)}) collective-permute-start(bf16[1,1,1,72,2304]{4,3,2,1,0:T(8,128)(2,1)} %pad_maximum_fusion.17), channel_id=1, source_target_pairs={{0,16},{1,17},{2,18},{3,19},{4,20},{5,21},{6,22},{7,23},{8,24},{9,... | collective-permute-start | bytes 995336 | tf_op jit(solution)/shard_map/ppermute | solution.py:147
  106.0 60.9 %collective-permute-start.31 = (bf16[1,1,2,72,1152]{4,3,2,1,0:T(8,128)(2,1)}, bf16[1,1,2,72,1152]{4,3,2,1,0:T(8,128)(2,1)}, u32[]{:S(2)}, u32[]{:S(2)}) collective-permute-start(bf16[1,1,2,72,1152]{4,3,2,1,0:T(8,128)(2,1)} %maximum_select_fusion.12), channel_id=1, source_target_pairs={{0,24},{1,25},{2,26},{3,27},{4,28},{5,29},{6,30},{7,31},{8,0},{9,1... | collective-permute-start | bytes 995336 | tf_op jit(solution)/shard_map/ppermute | solution.py:147
  106.0 62.6 %collective-permute-start.30 = (bf16[1,1,2,72,1152]{4,3,2,1,0:T(8,128)(2,1)}, bf16[1,1,2,72,1152]{4,3,2,1,0:T(8,128)(2,1)}, u32[]{:S(2)}, u32[]{:S(2)}) collective-permute-start(bf16[1,1,2,72,1152]{4,3,2,1,0:T(8,128)(2,1)} %maximum_select_fusion.12), channel_id=1, source_target_pairs={{0,16},{1,17},{2,18},{3,19},{4,20},{5,21},{6,22},{7,23},{8,24},{9,... | collective-permute-start | bytes 995336 | tf_op jit(solution)/shard_map/ppermute | solution.py:147
  112.2 57.8 %collective-permute-start.29 = (bf16[1,1,2,72,1152]{4,3,2,1,0:T(8,128)(2,1)}, bf16[1,1,2,72,1152]{4,3,2,1,0:T(8,128)(2,1)}, u32[]{:S(2)}, u32[]{:S(2)}) collective-permute-start(bf16[1,1,2,72,1152]{4,3,2,1,0:T(8,128)(2,1)} %maximum_select_fusion.12), channel_id=1, source_target_pairs={{0,8},{1,9},{2,10},{3,11},{4,12},{5,13},{6,14},{7,15},{8,16},{9,17... | collective-permute-start | bytes 995336 | tf_op jit(solution)/shard_map/ppermute | solution.py:147
  185.2 87.0 %collective-permute-start.32 = (bf16[4,1,2,72,1152]{4,3,2,1,0:T(8,128)(2,1)}, bf16[4,1,2,72,1152]{4,3,2,1,0:T(8,128)(2,1)}, u32[]{:S(2)}, u32[]{:S(2)}) collective-permute-start(bf16[4,1,2,72,1152]{4,3,2,1,0:T(8,128)(2,1)} %constant_dynamic-update-slice_fusion.6), channel_id=1, source_target_pairs={{0,4},{1,5},{2,6},{3,7},{4,0},{5,1},{6,2},{7,3},{8,12},{9,13},{10,... | collective-permute-start | bytes 3981320 | tf_op jit(solution)/shard_map/ppermute | solution.py:147
  193.1 85.3 %collective-permute-start.25 = (bf16[4,2,1,72,1152]{4,3,2,1,0:T(8,128)(2,1)}, bf16[4,2,1,72,1152]{4,3,2,1,0:T(8,128)(2,1)}, u32[]{:S(2)}, u32[]{:S(2)}) collective-permute-start(bf16[4,2,1,72,1152]{4,3,2,1,0:T(8,128)(2,1)} %constant_dynamic-update-slice_fusion.10), channel_id=1, source_target_pairs={{0,2},{1,3},{2,0},{3,1},{4,6},{5,7},{6,4},{7,5},{8,10},{9,11},{10,... | collective-permute-start | bytes 3981320 | tf_op jit(solution)/shard_map/ppermute | solution.py:147
  197.1 103.8 %collective-permute-start.13 = (bf16[4,2,1,72,1152]{4,3,2,1,0:T(8,128)(2,1)}, bf16[4,2,1,72,1152]{4,3,2,1,0:T(8,128)(2,1)}, u32[]{:S(2)}, u32[]{:S(2)}) collective-permute-start(bf16[4,2,1,72,1152]{4,3,2,1,0:T(8,128)(2,1)} %maximum_select_fusion.7), channel_id=1, source_target_pairs={{0,2},{1,3},{2,0},{3,1},{4,6},{5,7},{6,4},{7,5},{8,10},{9,11},{10,... | collective-permute-start | bytes 3981320 | tf_op jit(solution)/shard_map/ppermute | solution.py:147
  201.2 59.1 %all-to-all-start.4 = ((bf16[32,2,1152]{2,1,0:T(2,128)(2,1)}), bf16[32,2,1152]{2,1,0:T(2,128)(2,1)S(1)}, u32[]{:S(2)}, u32[]{:S(2)}) async-start(bf16[32,2,1152]{2,1,0:T(2,128)(2,1)} %broadcast_in_dim.43), calls=%async_computation.4 | async-start | bytes 294912 | tf_op jit(solution)/shard_map/all_to_all | solution.py:179
  206.6 98.8 %collective-permute-start.11 = (bf16[4,1,2,72,1152]{4,3,2,1,0:T(8,128)(2,1)}, bf16[4,1,2,72,1152]{4,3,2,1,0:T(8,128)(2,1)}, u32[]{:S(2)}, u32[]{:S(2)}) collective-permute-start(bf16[4,1,2,72,1152]{4,3,2,1,0:T(8,128)(2,1)} %maximum_select_fusion.6), channel_id=1, source_target_pairs={{0,4},{1,5},{2,6},{3,7},{4,0},{5,1},{6,2},{7,3},{8,12},{9,13},{10,... | collective-permute-start | bytes 3981320 | tf_op jit(solution)/shard_map/ppermute | solution.py:147
  211.6 122.3 %collective-permute-start.27 = (bf16[4,1,2,72,1152]{4,3,2,1,0:T(8,128)(2,1)}, bf16[4,1,2,72,1152]{4,3,2,1,0:T(8,128)(2,1)}, u32[]{:S(2)}, u32[]{:S(2)}) collective-permute-start(bf16[4,1,2,72,1152]{4,3,2,1,0:T(8,128)(2,1)} %maximum_select_fusion.9), channel_id=1, source_target_pairs={{0,4},{1,5},{2,6},{3,7},{4,0},{5,1},{6,2},{7,3},{8,12},{9,13},{10,... | collective-permute-start | bytes 3981320 | tf_op jit(solution)/shard_map/ppermute | solution.py:147
  272.3 66.4 %collective-permute-start.20 = (bf16[4,2,1,72,1152]{4,3,2,1,0:T(8,128)(2,1)}, bf16[4,2,1,72,1152]{4,3,2,1,0:T(8,128)(2,1)}, u32[]{:S(2)}, u32[]{:S(2)}) collective-permute-start(bf16[4,2,1,72,1152]{4,3,2,1,0:T(8,128)(2,1)} %maximum_select_fusion.8), channel_id=1, source_target_pairs={{0,2},{1,3},{2,0},{3,1},{4,6},{5,7},{6,4},{7,5},{8,10},{9,11},{10,... | collective-permute-start | bytes 3981320 | tf_op jit(solution)/shard_map/ppermute | solution.py:147
  278.4 101.7 %collective-permute-start.36 = (bf16[1152,1152]{1,0:T(8,128)(2,1)}, bf16[1152,1152]{1,0:T(8,128)(2,1)}, u32[]{:S(2)}, u32[]{:S(2)}) collective-permute-start(bf16[1152,1152]{1,0:T(8,128)(2,1)} %bitcast.59), channel_id=1, source_target_pairs={{0,1},{1,0},{2,3},{3,2},{4,5},{5,4},{6,7},{7,6},{8,9},{9,8},{10,11... | collective-permute-start | bytes 7962632 | tf_op jit(solution)/shard_map/ppermute | solution.py:147
  300.9 97.0 %collective-permute-start.34 = (bf16[1152,1152]{1,0:T(8,128)(2,1)}, bf16[1152,1152]{1,0:T(8,128)(2,1)}, u32[]{:S(2)}, u32[]{:S(2)}) collective-permute-start(bf16[1152,1152]{1,0:T(8,128)(2,1)} %bitcast.54), channel_id=1, source_target_pairs={{0,1},{1,0},{2,3},{3,2},{4,5},{5,4},{6,7},{7,6},{8,9},{9,8},{10,11... | collective-permute-start | bytes 7962632 | tf_op jit(solution)/shard_map/ppermute | solution.py:147
  334.0 196.7 %collective-permute-start.37 = (bf16[512,1152]{1,0:T(8,128)(2,1)}, bf16[512,1152]{1,0:T(8,128)(2,1)}, u32[]{:S(2)}, u32[]{:S(2)}) collective-permute-start(bf16[512,1152]{1,0:T(8,128)(2,1)} %bitcast.67), channel_id=1, source_target_pairs={{0,1},{1,0},{2,3},{3,2},{4,5},{5,4},{6,7},{7,6},{8,9},{9,8},{10,11... | collective-permute-start | bytes 3538952 | tf_op jit(solution)/shard_map/ppermute | solution.py:147
  458.3 85.9 %collective-permute-start.45 = (bf16[512,1152]{1,0:T(8,128)(2,1)}, bf16[512,1152]{1,0:T(8,128)(2,1)}, u32[]{:S(2)}, u32[]{:S(2)}) collective-permute-start(bf16[512,1152]{1,0:T(8,128)(2,1)} %bitcast.86), channel_id=1, source_target_pairs={{0,1},{1,0},{2,3},{3,2},{4,5},{5,4},{6,7},{7,6},{8,9},{9,8},{10,11... | collective-permute-start | bytes 3538952 | tf_op jit(solution)/shard_map/ppermute | solution.py:147
  460.2 71.1 %collective-permute-start.44 = (bf16[512,576]{0,1:T(8,128)(2,1)}, bf16[512,576]{0,1:T(8,128)(2,1)}, u32[]{:S(2)}, u32[]{:S(2)}) collective-permute-start(bf16[512,576]{0,1:T(8,128)(2,1)} %bitcast.173), channel_id=1, source_target_pairs={{0,1},{1,0},{2,3},{3,2},{4,5},{5,4},{6,7},{7,6},{8,9},{9,8},{10,11... | collective-permute-start | bytes 1769480 | tf_op jit(solution)/shard_map/ppermute | solution.py:147
  537.8 59.2 %all-to-all-start.8 = ((bf16[32,2,6912]{2,1,0:T(2,128)(2,1)}), bf16[32,2,6912]{2,1,0:T(2,128)(2,1)S(1)}, u32[]{:S(2)}, u32[]{:S(2)}) async-start(bf16[32,2,6912]{2,1,0:T(2,128)(2,1)} %broadcast_in_dim.51), calls=%async_computation.8 | async-start | bytes 1769472 | tf_op jit(solution)/shard_map/all_to_all | solution.py:179
  565.2 82.5 %collective-permute-start.39 = (bf16[4,2,1,72,1152]{4,3,2,1,0:T(8,128)(2,1)}, bf16[4,2,1,72,1152]{4,3,2,1,0:T(8,128)(2,1)}, u32[]{:S(2)}, u32[]{:S(2)}) collective-permute-start(bf16[4,2,1,72,1152]{4,3,2,1,0:T(8,128)(2,1)} %dynamic-slice_convert_fusion.5), channel_id=1, source_target_pairs={{0,2},{1,3},{2,0},{3,1},{4,6},{5,7},{6,4},{7,5},{8,10},{9,11},{10,... | collective-permute-start | bytes 3981320 | tf_op jit(solution)/shard_map/ppermute | solution.py:147
  578.4 74.7 %collective-permute-start.47 = (bf16[4,1,2,72,1152]{4,3,2,1,0:T(8,128)(2,1)}, bf16[4,1,2,72,1152]{4,3,2,1,0:T(8,128)(2,1)}, u32[]{:S(2)}, u32[]{:S(2)}) collective-permute-start(bf16[4,1,2,72,1152]{4,3,2,1,0:T(8,128)(2,1)} %dynamic-slice_convert_fusion.4), channel_id=1, source_target_pairs={{0,4},{1,5},{2,6},{3,7},{4,0},{5,1},{6,2},{7,3},{8,12},{9,13},{10,... | collective-permute-start | bytes 3981320 | tf_op jit(solution)/shard_map/ppermute | solution.py:147
  586.5 70.4 %collective-permute-start.54 = (bf16[4,2,1,72,1152]{4,3,2,1,0:T(8,128)(2,1)}, bf16[4,2,1,72,1152]{4,3,2,1,0:T(8,128)(2,1)}, u32[]{:S(2)}, u32[]{:S(2)}) collective-permute-start(bf16[4,2,1,72,1152]{4,3,2,1,0:T(8,128)(2,1)} %dynamic-slice_convert_fusion.3), channel_id=1, source_target_pairs={{0,2},{1,3},{2,0},{3,1},{4,6},{5,7},{6,4},{7,5},{8,10},{9,11},{10,... | collective-permute-start | bytes 3981320 | tf_op jit(solution)/shard_map/ppermute | solution.py:147
  587.6 74.7 %collective-permute-start.60 = (bf16[4,1,2,72,1152]{4,3,2,1,0:T(8,128)(2,1)}, bf16[4,1,2,72,1152]{4,3,2,1,0:T(8,128)(2,1)}, u32[]{:S(2)}, u32[]{:S(2)}) collective-permute-start(bf16[4,1,2,72,1152]{4,3,2,1,0:T(8,128)(2,1)} %dynamic-slice_convert_fusion.2), channel_id=1, source_target_pairs={{0,4},{1,5},{2,6},{3,7},{4,0},{5,1},{6,2},{7,3},{8,12},{9,13},{10,... | collective-permute-start | bytes 3981320 | tf_op jit(solution)/shard_map/ppermute | solution.py:147
  603.7 63.2 %collective-permute-start.67 = (bf16[4,2,1,72,1152]{4,3,2,1,0:T(8,128)(2,1)}, bf16[4,2,1,72,1152]{4,3,2,1,0:T(8,128)(2,1)}, u32[]{:S(2)}, u32[]{:S(2)}) collective-permute-start(bf16[4,2,1,72,1152]{4,3,2,1,0:T(8,128)(2,1)} %dynamic-slice_convert_fusion.1), channel_id=1, source_target_pairs={{0,2},{1,3},{2,0},{3,1},{4,6},{5,7},{6,4},{7,5},{8,10},{9,11},{10,... | collective-permute-start | bytes 3981320 | tf_op jit(solution)/shard_map/ppermute | solution.py:147
  691.1 111.9 %all-to-all-start.11 = ((f32[32,2,1152]{2,1,0:T(2,128)}), f32[32,2,1152]{2,1,0:T(2,128)S(1)}, u32[]{:S(2)}, u32[]{:S(2)}) async-start(f32[32,2,1152]{2,1,0:T(2,128)} %reshape.1092), calls=%async_computation.11 | async-start | bytes 589824 | tf_op jit(solution)/shard_map/all_to_all | solution.py:182
  (195 other events, 3304.4 us)

commit v2 on v1

v2 whole, which is shorter than its diff:
```python
import functools
import math

import jax
import jax.numpy as jnp
from jax import lax
from jax.sharding import PartitionSpec as P

D = 1152
HEADS = 16
HEAD_DIM = 72
FF = 4608
CLASSES = 1000
PATCH = 16
GRID = 16
FREQ = 256
TSTEPS = 1000
STEP = 10
SEQ = 256
WB = 13872
SMALL = 3 * PATCH
SROWS = 4722


HIGHEST_PRECISION = lax.Precision.HIGHEST
AXES = ("z", "x", "y", "c")
CORE_FIRST = ("c", "z", "x", "y")
LOG_TWO = math.log(2.0)
THRESHOLD = 1.0
LEARN_RATE = 0.05
BETA_ONE = 0.9
BETA_TWO = 0.999
EPSILON = 1e-08


def matmul(form, left, right):
    return jnp.einsum(form, left, right, preferred_element_type=jnp.float32)


def plan(steps):
    step_index = jnp.arange(TSTEPS).astype(jnp.float32)
    beta_rows = 0.0001 + (0.02 - 0.0001) * step_index / (TSTEPS - 1)
    alpha_bar = jnp.cumprod(1.0 - beta_rows)
    previous = jnp.concatenate([jnp.ones((1,), jnp.float32), alpha_bar[:-1]])
    posterior = beta_rows * (1.0 - previous) / (1.0 - alpha_bar)
    clipped = jnp.concatenate([posterior[1:2], posterior[1:]])
    mean_factor = beta_rows * beta_rows * previous / ((1.0 - alpha_bar) * alpha_bar)
    plan_table = jnp.stack(
        [
            jnp.sqrt(alpha_bar),
            jnp.sqrt(1.0 - alpha_bar),
            mean_factor,
            jnp.log(clipped),
            jnp.log(beta_rows),
        ],
        1,
    )
    one_hot = (steps[:, None] == jnp.arange(TSTEPS)[None, :]).astype(jnp.float32)
    return jnp.dot(one_hot, plan_table, precision=HIGHEST_PRECISION)


def positions():
    quarter = D // 4
    omegas = 1.0 / 10000.0 ** (jnp.arange(quarter).astype(jnp.float32) / quarter)
    cells = jnp.arange(SEQ)
    column_angle = (cells % GRID).astype(jnp.float32)[:, None] * omegas[None, :]
    row_angle = (cells // GRID).astype(jnp.float32)[:, None] * omegas[None, :]
    return jnp.concatenate(
        [jnp.sin(column_angle), jnp.cos(column_angle), jnp.sin(row_angle), jnp.cos(row_angle)], 1
    )


def frequencies(steps):
    half_count = FREQ // 2
    frequency = jnp.exp(
        -math.log(10000.0) * jnp.arange(half_count).astype(jnp.float32) / half_count
    )
    angles = steps.astype(jnp.float32)[:, None] * frequency[None, :]
    return jnp.concatenate([jnp.cos(angles), jnp.sin(angles)], 1)


def modulate(stream, shifts, scales):
    average = jnp.mean(stream, -1, keepdims=True)
    centred = stream - average
    variance = jnp.mean(centred * centred, -1, keepdims=True)
    return centred * lax.rsqrt(variance + 1e-06) * (1.0 + scales[:, None, :]) + shifts[:, None, :]


def modulate_back(stream, shifts, scales, cotangent):
    unused, pullback = jax.vjp(modulate, stream, shifts, scales)
    return pullback(cotangent)


def smooth_back(function, inputs, cotangent):
    unused, pullback = jax.vjp(function, inputs)
    return pullback(cotangent)[0]


def gelu_tanh(inputs):
    return jax.nn.gelu(inputs, approximate=True)


def loss_terms(prediction, target, sched):
    guessed = prediction[..., :PATCH]
    variance_raw = prediction[..., PATCH:]
    mean_factor = sched[:, 2][:, None, None]
    posterior_log = sched[:, 3][:, None, None]
    beta_log = sched[:, 4][:, None, None]
    blend = 0.5 * (variance_raw + 1.0)
    model_log = blend * beta_log + (1.0 - blend) * posterior_log
    errors = guessed - target
    bound_term = 0.5 * (
        -1.0
        + model_log
        - posterior_log
        + jnp.exp(posterior_log - model_log)
        + mean_factor * errors * errors * jnp.exp(-model_log)
    )
    return jnp.sum(errors * errors + bound_term / LOG_TWO)


class Links:
    def __init__(self, dp, mod):
        self.core = 2 if mod % 2 == 0 else 1
        self.y = mod // self.core
        self.x = self.y if dp % self.y == 0 else 1
        self.z = dp // self.x
        self.count = dp * mod
        self.size = {"z": self.z, "x": self.x, "y": self.y, "c": self.core}
        self.dim = {"z": 0, "x": 1, "y": 2}

    def place(self, axis):
        index = lax.axis_index(AXES)
        below = {"c": 1, "y": self.core, "x": self.core * self.y, "z": self.core * self.y * self.x}
        return index // below[axis] % self.size[axis]

    def send(self, block, axis, shift=1):
        pairs = []
        for index in range(self.count):
            spot = {
                "c": index % self.core,
                "y": index // self.core % self.y,
                "x": index // (self.core * self.y) % self.x,
                "z": index // (self.core * self.y * self.x),
            }
            spot[axis] = (spot[axis] + shift) % self.size[axis]
            target = ((spot["z"] * self.x + spot["x"]) * self.y + spot["y"]) * self.core + spot["c"]
            pairs.append((index, target))
        return lax.ppermute(block, AXES, pairs)

    def spread(self, block):
        copies = jnp.broadcast_to(block[None], (self.count, *block.shape))
        return lax.all_to_all(copies, AXES, split_axis=0, concat_axis=0, tiled=True)

    def deliver(self, blocks):
        return lax.all_to_all(blocks, AXES, split_axis=0, concat_axis=0, tiled=True)


def pick(own, first, second):
    return jnp.where(own == 0, first, second)


def joined(own, mine, other, dim):
    return pick(
        own, jnp.concatenate([mine, other], dim), jnp.concatenate([other, mine], dim)
    )


def column_half(rows, half):
    small = D // 2
    attention = [rows[:, part * D + half * small : part * D + (half + 1) * small] for part in range(4)]
    wide = FF // 2
    return [
        jnp.concatenate(attention, 1),
        rows[:, 4 * D + half * wide : 4 * D + (half + 1) * wide],
        rows[:, 4 * D + FF + half * wide : 4 * D + FF + (half + 1) * wide],
    ]


def whole_columns(first, second):
    small = D // 2
    pieces = [
        half[0][:, part * small : (part + 1) * small] for part in range(4) for half in (first, second)
    ]
    return jnp.concatenate([*pieces, first[1], second[1], first[2], second[2]], 1)


def chip_rows(links, flat):
    core = links.place("c")
    per_chip = D * links.core // links.count
    if (D % links.count) == 0:
        rows = flat.reshape(D // links.count, WB).astype(jnp.bfloat16)
        halves = [jnp.concatenate(column_half(rows, half), 1) for half in range(2)]
        mine = pick(core, halves[0], halves[1])
        other = links.send(pick(core, halves[1], halves[0]), "c")
        return joined(core, mine, other, 0), rows[:, WB - SMALL :].reshape(-1)
    low = flat.astype(jnp.bfloat16)
    rows = joined(core, low, links.send(low, "c"), 0).reshape(per_chip, WB)
    halves = [jnp.concatenate(column_half(rows, half), 1) for half in range(2)]
    small = rows[:, WB - SMALL :].reshape(2, -1)
    return pick(core, halves[0], halves[1]), pick(core, small[0], small[1])


def gather_halves(chunk):
    whole = lax.all_gather(chunk, CORE_FIRST, axis=0, tiled=True)
    return whole[:D], whole[D:]


class Reduction:
    def __init__(self, links, gradients, kind=jnp.bfloat16):
        self.links, self.kind = links, kind
        shape = (links.z, links.x, links.y, D * links.core // links.count)
        self.blocks = [rows.reshape(*shape, -1) for rows in gradients]
        total = sum(rows.shape[1] for rows in gradients)
        middle = total // 256 * 128
        self.spans = [[], []]
        for index, rows in enumerate(gradients):
            before = sum(earlier.shape[1] for earlier in gradients[:index])
            edge = min(max(middle - before, 0), rows.shape[1])
            if edge > 0:
                self.spans[0].append((index, 0, edge))
            if edge < rows.shape[1]:
                self.spans[1].append((index, edge, rows.shape[1]))

    def cut(self, sources, axis, spot):
        dim = self.links.dim[axis]
        parts = [
            lax.dynamic_slice_in_dim(self.blocks[index][..., low:high], spot, 1, dim)
            for index, low, high in sources
        ]
        return jnp.concatenate(parts, 4) if len(parts) > 1 else parts[0]

    def send(self, order):
        self.order = order
        self.got = []
        for sources, axis in zip(self.spans, order):
            extent, own = self.links.size[axis], self.links.place(axis)
            for shift in range(1, extent):
                part = self.cut(sources, axis, (own + shift) % extent).astype(self.kind)
                self.got.append(self.links.send(part, axis, shift))
        return self.got

    def add(self, got):
        got = list(got)
        blocks, spans = [], []
        for sources, axis in zip(self.spans, self.order):
            extent, own = self.links.size[axis], self.links.place(axis)
            total = self.cut(sources, axis, own).astype(jnp.float32)
            for _ in range(1, extent):
                total = total + got.pop(0).astype(jnp.float32)
            spans.append([(len(blocks), 0, total.shape[-1])])
            blocks.append(total)
        self.blocks, self.spans = blocks, spans

    def join(self):
        self.spans = [[span for sources in self.spans for span in sources]]

    def result(self):
        return self.blocks[0].reshape(-1, self.blocks[0].shape[-1])


def flat_gradient(links, joint, small):
    core = links.place("c")
    edges = [0, 2 * D, 4 * D, 6 * D]
    split = lambda rows: [rows[:, edges[part] : edges[part + 1]] for part in range(3)]
    per_device = D // links.count
    if (D % links.count) == 0:
        mine = lax.dynamic_slice_in_dim(joint, core * per_device, per_device, 0)
        sent = lax.dynamic_slice_in_dim(joint, (1 - core) * per_device, per_device, 0)
    else:
        mine, sent = joint, joint
        small = joined(core, small, links.send(small, "c"), 0)
    other = links.send(sent, "c")
    columns = whole_columns(split(pick(core, mine, other)), split(pick(core, other, mine)))
    flat = jnp.concatenate([columns, small.reshape(-1, SMALL)], 1).reshape(-1)
    if (D % links.count) == 0:
        return flat
    part = flat.shape[0] // 2
    return lax.dynamic_slice_in_dim(flat, core * part, part)


EXTENTS = [FREQ, D, CLASSES + 1, 2 * D, 1, 2, 6]
STARTS = [sum(EXTENTS[:index]) for index in range(len(EXTENTS) + 1)]


class Window:
    def __init__(self, links, length):
        self.length = length
        begins = [index * length for index in range(links.count)]
        rows = max((begin % D + length + D - 1) // D for begin in begins)
        self.rows = (rows + 15) // 16 * 16
        begin = lax.axis_index(AXES) * length
        self.first = begin // D
        self.firsts = [start // D for start in begins]
        self.offset = begin - self.first * D

    def fill(self, flat):
        padded = jnp.concatenate(
            [jnp.zeros((D,), flat.dtype), flat, jnp.zeros((self.rows * D,), flat.dtype)]
        )
        return lax.dynamic_slice_in_dim(padded, D - self.offset, self.rows * D).reshape(
            self.rows, D
        )

    def cut(self, columns, start):
        full = jnp.pad(columns, ((0, 0), (start, SROWS + self.rows - start - columns.shape[1])))
        return lax.dynamic_slice_in_dim(full, self.first, self.rows, 1)

    def put(self, columns, start, extent):
        full = jnp.zeros((columns.shape[0], SROWS + self.rows), columns.dtype)
        full = lax.dynamic_update_slice_in_dim(full, columns, self.first, 1)
        return full[:, start : start + extent]

    def assemble(self, windows, start, extent):
        inside = [
            index
            for index, first in enumerate(self.firsts)
            if first < start + extent and first + self.rows > start
        ]
        low, high = inside[0], inside[-1] + 1
        firsts = jnp.array(self.firsts[low:high])
        rows = firsts[:, None] + jnp.arange(self.rows)[None, :]
        chosen = jnp.arange(extent)[:, None, None] + start == rows[None]
        return matmul("kir,dkr->id", windows[low:high], chosen.astype(windows.dtype))

    def flatten(self, rows):
        return lax.dynamic_slice_in_dim(rows.reshape(-1), self.offset, self.length)


def adam_update(weight, gradient, first, second):
    first_new = BETA_ONE * first + (1.0 - BETA_ONE) * gradient
    second_new = BETA_TWO * second + (1.0 - BETA_TWO) * gradient * gradient
    corrected = first_new / (1.0 - BETA_ONE**STEP)
    spread = jnp.sqrt(second_new / (1.0 - BETA_TWO**STEP))
    return (weight - LEARN_RATE * corrected / (spread + EPSILON), first_new, second_new)


def attend(normed, w_qkv):
    images = normed.shape[0]
    heads = HEADS // 2
    low = jnp.bfloat16
    triple = matmul("isd,de->ise", normed, w_qkv).astype(low)
    triple = triple.reshape(images, SEQ, 3, heads, HEAD_DIM)
    queries, keys, values = triple[:, :, 0], triple[:, :, 1], triple[:, :, 2]
    scores = matmul("iqhe,ikhe->ihqk", queries, keys) * (1.0 / math.sqrt(HEAD_DIM))
    totals = jax.nn.logsumexp(scores, axis=-1)
    weights = jnp.exp(scores - totals[..., None]).astype(low)
    mixed = matmul("ihqk,ikhe->iqhe", weights, values).astype(low)
    return mixed.reshape(images, SEQ, D // 2), (queries, keys, values, totals)


def attend_back(kept, mixed_grad):
    queries, keys, values, totals = kept
    images = queries.shape[0]
    low = jnp.bfloat16
    mixed_grad = mixed_grad.astype(low).reshape(images, SEQ, HEADS // 2, HEAD_DIM)
    score_scale = 1.0 / math.sqrt(HEAD_DIM)
    softmax_rows = jnp.exp(
        matmul("iqhe,ikhe->ihqk", queries, keys) * score_scale - totals[..., None]
    )
    weight_grad = matmul("iqhe,ikhe->ihqk", mixed_grad, values)
    score_grad = (
        softmax_rows * (weight_grad - jnp.sum(weight_grad * softmax_rows, -1, keepdims=True))
    ).astype(low)
    query_grad = (matmul("ihqk,ikhe->iqhe", score_grad, keys) * score_scale).astype(low)
    key_grad = (matmul("ihqk,iqhe->ikhe", score_grad, queries) * score_scale).astype(low)
    value_grad = matmul("ihqk,iqhe->ikhe", softmax_rows.astype(low), mixed_grad).astype(low)
    return jnp.stack([query_grad, key_grad, value_grad], 2).reshape(images, SEQ, 3 * D // 2)


def shards(
    links,
    latents,
    noise,
    timesteps,
    labels,
    dropped,
    block_master,
    block_m,
    block_v,
    stem_master,
    stem_m,
    stem_v,
    ada_w,
    ada_w_m,
    ada_w_v,
):
    low, wide = jnp.bfloat16, jnp.float32
    images = timesteps.shape[0]
    everyone = links.count * images
    own_cols = ada_w.shape[1]
    own_rows = ada_w.shape[0]
    row_at = lax.axis_index(("z", "x")) * own_rows
    col_at = lax.axis_index(("y", "c")) * own_cols
    groups = 6 * D // own_cols

    core = links.place("c")
    chunks, small = chip_rows(links, block_master)
    w_attention = gather_halves(chunks[:, : 2 * D])
    w_mlp = gather_halves(chunks[:, 2 * D :])
    w_qkv = [half[:, : 3 * D // 2] for half in w_attention]
    w_proj = [half[:, 3 * D // 2 :] for half in w_attention]
    w_up = [half[:, : 2 * D] for half in w_mlp]
    w_down = [half[:, 2 * D :] for half in w_mlp]

    window = Window(links, stem_master.shape[0])
    stem = window.fill(stem_master.astype(low))
    ada_low = ada_w.astype(low)
    integers = jnp.stack([timesteps, jnp.where(dropped == 1, CLASSES, labels)])
    digits = jnp.stack([integers // 32, integers % 32]).astype(low).reshape(-1)
    got = links.spread(jnp.concatenate([digits, small]))
    digits = got[:, : 4 * images].astype(jnp.int32).reshape(links.count, 2, 2, images)
    integers = digits[:, 0] * 32 + digits[:, 1]
    small = got[:, 4 * images :].reshape(D, SMALL)
    w_patch, w_head = small[:, :PATCH], small[:, PATCH:]
    all_steps = integers[:, 0].reshape(everyone)
    chosen = integers[:, 1].reshape(everyone)
    timing = frequencies(all_steps).astype(low)
    one_hot = (chosen[:, None] == jnp.arange(CLASSES + 1)[None, :]).astype(low)
    bias_start, bias_extent = STARTS[4], 9
    bias_share = -(-bias_extent * D // links.count)
    mark = jnp.arange(bias_extent)[:, None] + bias_start == (
        window.first + jnp.arange(window.rows)
    )
    bias_part = matmul("br,rd->bd", mark.astype(low), stem).reshape(bias_extent * D)
    bias_part = jnp.pad(bias_part, (0, bias_share * links.count - bias_extent * D))

    before_part = matmul("ir,rd->id", window.cut(timing, STARTS[0]), stem)
    got = links.deliver(
        jnp.concatenate(
            [
                before_part.reshape(links.count, images * D),
                bias_part.reshape(links.count, bias_share),
            ],
            1,
        )
    ).sum(0)
    got = links.spread(got)
    all_before = got[:, : images * D].reshape(everyone, D)
    all_hidden = jax.nn.silu(all_before).astype(low)
    biases = got[:, images * D :].reshape(-1)[: bias_extent * D].reshape(bias_extent, D)
    left = window.cut(jnp.concatenate([all_hidden, one_hot], 1), STARTS[1])
    condition = links.deliver(
        matmul("ir,rd->id", left, stem).reshape(links.count, images, D)
    ).sum(0)
    signal = jax.nn.silu(condition).astype(low)
    all_signal = links.spread(signal).reshape(everyone, D)
    signal_rows = lax.dynamic_slice_in_dim(all_signal, row_at, own_rows, 1)
    parts = links.deliver(
        matmul("ir,rc->ic", signal_rows, ada_low).reshape(links.count, images, own_cols)
    )
    modulation = (
        parts.reshape(-1, groups, images, own_cols).sum(0).transpose(1, 0, 2).reshape(images, 6 * D)
        + biases[3:].reshape(6 * D)
    ).astype(low)
    pieces = jnp.split(modulation.astype(wide), 6, axis=1)
    final_part = window.put(matmul("id,rd->ir", all_signal, stem), STARTS[3], 2 * D)
    final_mod = links.deliver(final_part.reshape(links.count, images, 2 * D)).sum(0) + biases[
        1:3
    ].reshape(2 * D)
    final_shift, final_scale = final_mod[:, :D], final_mod[:, D:]

    sched = plan(timesteps)
    target = noise.reshape(images, SEQ, PATCH)
    noisy_rows = (
        sched[:, 0][:, None, None] * latents.reshape(images, SEQ, PATCH)
        + sched[:, 1][:, None, None] * target
    ).astype(low)
    stream = matmul("isp,dp->isd", noisy_rows, w_patch) + biases[0] + positions()[None]
    normed = modulate(stream, pieces[0], pieces[1]).astype(low)
    mixed, kept = [], []
    for half in range(2):
        rows, saved = attend(normed, w_qkv[half])
        mixed.append(rows)
        kept.append(saved)
    attended = sum(matmul("isd,od->iso", mixed[half], w_proj[half]) for half in range(2))
    middle = stream + pieces[2][:, None, :] * attended
    second = modulate(middle, pieces[3], pieces[4]).astype(low)
    inner = [matmul("isd,df->isf", second, w_up[half]) for half in range(2)]
    active = [gelu_tanh(rows).astype(low) for rows in inner]
    output = sum(matmul("isf,of->iso", active[half], w_down[half]) for half in range(2))
    layer_out = middle + pieces[5][:, None, :] * output
    final_normed = modulate(layer_out, final_shift, final_scale).astype(low)
    prediction = matmul("isd,do->iso", final_normed, w_head)
    loss_local, loss_back = jax.vjp(
        lambda predicted: loss_terms(predicted, target, sched), prediction
    )

    def tokens(rows):
        return rows.reshape(images * SEQ, rows.shape[-1])

    def with_partner(first, second=None):
        if second is None:
            mine, sent = tokens(first), tokens(first)
        else:
            first, second = tokens(first), tokens(second)
            mine, sent = pick(core, first, second), pick(core, second, first)
        return jnp.concatenate([mine, links.send(sent, "c")], 0)

    def together(*values):
        return lax.optimization_barrier(values)

    out_grad = loss_back(jnp.ones_like(loss_local))[0].astype(low)
    grad_head = matmul("iso,isd->do", out_grad, final_normed)
    upstream, shift_grad, scale_grad = modulate_back(
        layer_out, final_shift, final_scale, matmul("iso,do->isd", out_grad, w_head)
    )
    final_grad = jnp.concatenate([shift_grad, scale_grad], 1)
    down_in = (pieces[5][:, None, :] * upstream).astype(low)
    gate_b = jnp.sum(upstream * output, 1)
    active_both = with_partner(*active)
    second_both = with_partner(second)
    mixed_both = with_partner(*mixed)
    normed_both = with_partner(normed)
    down_both = with_partner(down_in)
    inner_grad = [
        smooth_back(
            gelu_tanh, inner[half], matmul("iso,of->isf", down_in, w_down[half])
        ).astype(low)
        for half in range(2)
    ]
    inner_grad, down_both, active_both = together(inner_grad, down_both, active_both)
    grad_down = matmul("to,tf->of", down_both, active_both).astype(low)
    inner_grad, grad_down = together(inner_grad, grad_down)
    reduced_down = lax.psum_scatter(
        grad_down, ("z", "x", "y"), scatter_dimension=0, tiled=True
    ).astype(wide)
    inner_both = with_partner(*inner_grad)
    second_grad = sum(
        matmul("isf,df->isd", inner_grad[half], w_up[half]) for half in range(2)
    )
    back_mid, shift_b, scale_b = modulate_back(middle, pieces[3], pieces[4], second_grad)
    grad_mid = upstream + back_mid
    proj_in = (pieces[2][:, None, :] * grad_mid).astype(low)
    gate_a = jnp.sum(grad_mid * attended, 1)
    proj_both = with_partner(proj_in)
    final_low = final_grad.astype(low)
    early = jnp.concatenate([gate_a, shift_b, scale_b, gate_b], 1).astype(low)
    early = links.spread(jnp.concatenate([early, final_low], 1)).reshape(everyone, 6 * D)
    proj_in, inner_both, proj_both = together(proj_in, inner_both, proj_both)
    grad_up = matmul("td,tf->df", second_both, inner_both)
    grad_proj = matmul("to,td->od", proj_both, mixed_both)
    proj_in, grad_up, grad_proj = together(proj_in, grad_up, grad_proj)
    first = Reduction(links, [grad_up, grad_proj])
    got = first.send("yx")
    qkv_grad = [
        attend_back(kept[half], matmul("iso,od->isd", proj_in, w_proj[half])) for half in range(2)
    ]
    qkv_grad, got = together(qkv_grad, got)
    first.add(got)
    got = first.send("xy")
    qkv_both = with_partner(*qkv_grad)
    normed_grad = sum(matmul("ise,de->isd", qkv_grad[half], w_qkv[half]) for half in range(2))
    back_in, shift_a, scale_a = modulate_back(stream, pieces[0], pieces[1], normed_grad)
    stream_grad = grad_mid + back_in
    late = jnp.concatenate([shift_a, scale_a], 1).astype(low)
    late, stream_grad, got, qkv_both = together(late, stream_grad, got, qkv_both)
    late = links.spread(late).reshape(everyone, 2 * D)
    first.add(got)
    first.join()
    got = first.send("z")
    grad_qkv = matmul("td,te->de", normed_both, qkv_both)
    grad_patch = matmul("isp,isd->dp", noisy_rows, stream_grad.astype(low))
    small_grad = jnp.concatenate([grad_patch, grad_head], 1).reshape(links.count, -1)
    grad_qkv, late = together(grad_qkv, late)
    second = Reduction(links, [grad_qkv])
    more = second.send("yx")

    all_final = early[:, 4 * D :]
    all_modulation = jnp.concatenate([late, early[:, : 4 * D]], 1)
    own_modulation = lax.dynamic_slice_in_dim(all_modulation, col_at, own_cols, 1)
    signal_part = matmul("ir,rd->id", window.cut(all_final, STARTS[3]), stem)
    ada_part = matmul("ic,rc->ir", own_modulation, ada_low)
    signal_part = lax.dynamic_update_slice_in_dim(
        signal_part,
        lax.dynamic_slice_in_dim(signal_part, row_at, own_rows, 1) + ada_part,
        row_at,
        1,
    )
    sums = jnp.concatenate([jnp.sum(stream_grad, (0, 1)), jnp.sum(final_grad, 0)])
    share = -(-sums.shape[0] // links.count)
    sums = jnp.pad(sums, (0, share * links.count - sums.shape[0])).reshape(links.count, share)
    summed = links.deliver(
        jnp.concatenate([signal_part.reshape(links.count, images * D), sums, small_grad], 1)
    ).sum(0)
    small = summed[images * D + share :]
    condition_grad = smooth_back(jax.nn.silu, condition, summed[: images * D].reshape(images, D))
    spreading = jnp.concatenate([condition_grad.reshape(-1), summed[images * D : images * D + share]])
    spreading, got, more = together(spreading, got, more)
    first.add(got)
    second.add(more)
    more = second.send("xy")
    spread = links.spread(spreading)
    all_condition = spread[:, : images * D].reshape(everyone, D)
    all_sums = spread[:, images * D :].reshape(-1)[: 3 * D]
    condition_low = all_condition.astype(low)
    hidden_part = matmul("id,rd->ir", condition_low, stem)
    before_part = window.cut(all_before, STARTS[1])
    before_part = smooth_back(jax.nn.silu, before_part, hidden_part)
    row = window.first + jnp.arange(window.rows)
    before_part = jnp.where((row >= STARTS[1]) & (row < STARTS[2]), before_part, 0.0).astype(low)
    before_part, more = together(before_part, more)
    second.add(more)
    second.join()
    more = second.send("z")
    before_low = window.assemble(links.spread(before_part), STARTS[1], D).astype(low)
    second.add(more)
    reduced_rest = first.result()
    joint = jnp.concatenate(
        [second.result(), reduced_rest[:, 2 * D :], reduced_rest[:, : 2 * D], reduced_down], 1
    )
    block_grad = flat_gradient(links, joint, small)
    totals = links.spread(jnp.stack([loss_local, jnp.sum(block_grad * block_grad)])).sum(0)
    loss_total, squares = totals[0], totals[1]
    bias_rows = jnp.concatenate(
        [all_sums, jnp.sum(all_modulation.astype(wide), 0)]
    ).reshape(bias_extent, D)

    def product_squares(left, right):
        left, right = left.astype(wide), right.astype(wide)
        grams = [jnp.dot(rows, rows.T, precision=HIGHEST_PRECISION) for rows in (left, right)]
        return jnp.sum(grams[0] * grams[1])

    squares = (
        squares
        + product_squares(all_signal, all_modulation)
        + product_squares(all_signal, all_final)
        + product_squares(one_hot, all_condition)
        + product_squares(all_hidden, condition_low)
        + product_squares(timing, before_low)
        + jnp.sum(bias_rows * bias_rows)
    )
    ada_grad = matmul("ir,ic->rc", signal_rows, own_modulation)
    low_left = jnp.concatenate(
        [
            window.cut(timing, STARTS[0]),
            window.cut(all_hidden, STARTS[1]),
            window.cut(all_final, STARTS[3]),
        ],
        0,
    )
    low_right = jnp.concatenate([before_low, condition_low, all_signal], 0)
    stem_rows = matmul("ir,id->rd", low_left, low_right)
    wide_left = jnp.concatenate(
        [window.cut(one_hot.astype(wide), STARTS[2]), mark.astype(wide)], 0
    )
    wide_right = jnp.concatenate([all_condition, bias_rows], 0)
    stem_rows = stem_rows + jnp.dot(wide_left.T, wide_right, precision=HIGHEST_PRECISION)
    stem_grad = window.flatten(stem_rows)
    grad_norm = jnp.sqrt(squares)
    factor = THRESHOLD / jnp.maximum(grad_norm, THRESHOLD)
    block_new = adam_update(block_master, block_grad * factor, block_m, block_v)
    stem_new = adam_update(stem_master, stem_grad * factor, stem_m, stem_v)
    ada_new = adam_update(ada_w, ada_grad * factor, ada_w_m, ada_w_v)
    return (loss_total, grad_norm, *block_new, *stem_new, *ada_new)


def solution(mesh):
    links = Links(mesh.shape["dp"], mesh.shape["mod"])
    grid = jax.sharding.Mesh(
        mesh.devices.reshape(links.z, links.x, links.y, links.core), AXES
    )
    flat, rows, ada = P(AXES), P(AXES, None), P(("z", "x"), ("y", "c"))
    return jax.shard_map(
        functools.partial(shards, links),
        mesh=grid,
        in_specs=(rows, rows) + (flat,) * 9 + (ada,) * 3,
        out_specs=(P(), P()) + (flat,) * 6 + (ada,) * 3,
        check_vma=False,
    )
```

time: 873 us -> 759 us (0.87)
  starting transfers between devices: 199 us -> 85.5 us
  other arithmetic: 131 us -> 82.9 us
  waiting for transfers between devices: 210 us -> 249 us
  between operations: 7.58 us -> 22.3 us
  local copies, waits for them, and re-layouts: 134 us -> 148 us
  blocking collectives: 9.09 us -> 0 us
  matrix products: 170 us -> 161 us
    ppermute x85 -> x24, starting transfers between devices: 133 us -> 24.2 us  [send(): return lax.ppermute(block, AXES, pairs)]
    all_gather x0 -> x2, waiting for transfers between devices: none -> 64.2 us  [gather_halves(): whole = lax.all_gather(chunk, CORE_FIRST, axis=0, tiled=True)]
    select_n x14 -> x0, other arithmetic: 36.6 us -> none  [gather(): jnp.where(own == 0, jnp.concatenate(pieces, dim), jnp.concatenate(pieces[...]
    ppermute x85 -> x24, waiting for transfers between devices: 122 us -> 86.8 us  [send(): return lax.ppermute(block, AXES, pairs)]
    all_to_all x6 -> x5, waiting for transfers between devices: 37.6 us -> 68 us  [deliver(): return lax.all_to_all(blocks, AXES, split_axis=0, concat_axis=0, tiled=True)]
    dot_general x62 -> x48, matrix products: 169 us -> 148 us  [matmul(): return jnp.einsum(form, left, right, preferred_element_type=jnp.float32)]
    all_to_all x8, waiting for transfers between devices: 50.8 us -> 30.4 us  [spread(): return lax.all_to_all(copies, AXES, split_axis=0, concat_axis=0, tiled=True)]
    convert_element_type x25 -> x9, local copies, waits for them, and re-layouts: 25 us -> 9.04 us  [the longest x7 7.33 us: send(): part = self.cut(sources, axis, (own + shift) % extent).astype(self.kind)]
  transfers between devices with their start and end apart: 99 -> 40, of which waited for: 22 -> 18; matrix products, arithmetic and copies ran while one was open for 45% -> 37% of each run, Pallas kernels for 0% -> 0%
where the time goes in v2:
time: 759 us; the launch traced here: 749 us
  waiting for transfers between devices  249 us (33%)
  matrix products  161 us (21%)
  local copies, waits for them, and re-layouts  148 us (19%)
  starting transfers between devices  85.5 us (11%)
  other arithmetic  82.9 us (11%)
  between operations  22.3 us (3%)
    dot_general x48, matrix products, matmul(): return jnp.einsum(form, left, right, preferred_element_type=jnp.float32)  148 us
    ppermute x24, waiting for transfers between devices, send(): return lax.ppermute(block, AXES, pairs)  86.8 us
    all_to_all x5, waiting for transfers between devices, deliver(): return lax.all_to_all(blocks, AXES, split_axis=0, concat_axis=0, tiled=True)  68 us
    all_gather x2, waiting for transfers between devices, gather_halves(): whole = lax.all_gather(chunk, CORE_FIRST, axis=0, tiled=True)  64.2 us
    all_to_all x8, starting transfers between devices, spread(): return lax.all_to_all(copies, AXES, split_axis=0, concat_axis=0, tiled=True)  40.7 us
    all_to_all x8, waiting for transfers between devices, spread(): return lax.all_to_all(copies, AXES, split_axis=0, concat_axis=0, tiled=True)  30.4 us
    ppermute x24, starting transfers between devices, send(): return lax.ppermute(block, AXES, pairs)  24.2 us
    unnamed x306, local copies, waits for them, and re-layouts  21.8 us
  transfers between devices with their start and end apart: 40, of which 18 were waited for; matrix products, arithmetic and copies ran while one was open for 37% of the time, Pallas kernels for 0%

profile of v2, /device:TPU:0, one launch (start us, length us, event | category | flops | bytes accessed | tf_op | source)
XLA Modules:
  0.0 749.5 jit_solution(11174731370023203243)
XLA Ops:
  19.4 7.2 all-to-all-start
  45.0 14.6 %all-to-all-done.1 = f32[32,1,2628]{2,1,0:T(1,128)S(1)} async-done(((f32[32,1,2628]{2,1,0:T(1,128)}), f32[32,1,2628]{2,1,0:T(1,128)S(1)}, u32[]{:S(2)}, u32[]{:S(2)}) %all-to-all-start.1) | async-done | bytes 336416 | tf_op jit(solution)/shard_map/all_to_all | solution.py:156
  69.4 8.5 %all-to-all-done.2 = f32[32,1,2628]{2,1,0:T(1,128)S(1)} async-done(((f32[32,1,2628]{2,1,0:T(1,128)}), f32[32,1,2628]{2,1,0:T(1,128)S(1)}, u32[]{:S(2)}, u32[]{:S(2)}) %all-to-all-start.2) | async-done | bytes 336416 | tf_op jit(solution)/shard_map/all_to_all | solution.py:153
  87.4 14.4 %all-to-all-done.3 = f32[32,2,1152]{2,1,0:T(2,128)S(1)} async-done(((f32[32,2,1152]{2,1,0:T(2,128)}), f32[32,2,1152]{2,1,0:T(2,128)S(1)}, u32[]{:S(2)}, u32[]{:S(2)}) %all-to-all-start.3) | async-done | bytes 294944 | tf_op jit(solution)/shard_map/all_to_all | solution.py:156
  109.7 6.4 all-to-all-done.4
  131.5 15.3 %all-to-all-done.5 = f32[32,2,1728]{2,1,0:T(2,128)} async-done(((f32[32,2,1728]{2,1,0:T(2,128)}), f32[32,2,1728]{2,1,0:T(2,128)}, u32[]{:S(2)}, u32[]{:S(2)}) %all-to-all-start.5) | async-done | bytes 442400 | tf_op jit(solution)/shard_map/all_to_all | solution.py:156
  154.9 23.7 %all-to-all-done.6 = f32[32,2,2304]{2,1,0:T(2,128)} async-done(((f32[32,2,2304]{2,1,0:T(2,128)}), f32[32,2,2304]{2,1,0:T(2,128)}, u32[]{:S(2)}, u32[]{:S(2)}) %all-to-all-start.6) | async-done | bytes 589856 | tf_op jit(solution)/shard_map/all_to_all | solution.py:156
  202.1 64.2 %all-gather.5.cloned.1.call-done = bf16[2304,4608]{1,0:T(8,128)(2,1)} async-done(((bf16[72,4608]{1,0:T(8,128)(2,1)}), bf16[2304,4608]{1,0:T(8,128)(2,1)}) %all-gather.5.cloned.1.call-update) | async-done | bytes 21233680 | tf_op jit(solution)/shard_map/all_gather | solution.py:205
  272.0 7.2 broadcast_select_fusion.3
  279.3 8.3 %fusion.18 = f32[2,256,1152]{2,1,0:T(8,128)S(1)} fusion(bf16[2304,4608]{1,0:T(8,128)(2,1)} %all-gather.5.cloned.1.call-done, f32[2,256,2304]{2,1,0:T(8,128)S(1)} %get-tuple-element.205), kind=kOutput, calls=%fused_computation.41 | convolution fusion | flops 2728525824 | bytes 12386304 | tf_op jit(solution)/shard_map/isf,of->iso/dot_general | solution.py:37
  287.6 6.3 fusion.181
  300.4 8.3 %fusion.8 = bf16[2,256,2304]{2,1,0:T(8,128)(2,1)} fusion(f32[2,256,2304]{2,1,0:T(8,128)S(1)} %bitcast.366, bf16[2,256,1152]{2,1,0:T(8,128)(2,1)S(1)} %get-tuple-element.117, bf16[2304,4608]{1,0:T(8,128)(2,1)} %all-gather.5.cloned.1.call-done), kind=kOutput, calls=%fused_computation.17 | convolution fusion | flops 2741501952 | bytes 13565952 | tf_op jit(solution)/shard_map/iso,of->isf/dot_general | solution.py:37
  308.7 7.8 %fusion.15 = bf16[2,256,2304]{2,1,0:T(8,128)(2,1)} fusion(f32[2,256,2304]{2,1,0:T(8,128)S(1)} %fusion.20, bf16[2,256,1152]{2,1,0:T(8,128)(2,1)S(1)} %get-tuple-element.117, bf16[2304,4608]{1,0:T(8,128)(2,1)} %all-gather.5.cloned.1.call-done), kind=kOutput, calls=%fused_computation.24 | convolution fusion | flops 2741501952 | bytes 13565952 | tf_op jit(solution)/shard_map/iso,of->isf/dot_general | solution.py:37
  317.0 7.7 %convolution_convert_fusion = bf16[1152,2304]{1,0:T(8,128)(2,1)} fusion(bf16[1024,1152]{1,0:T(8,128)(2,1)S(1)} %pad_maximum_fusion.3, bf16[1024,2304]{1,0:T(8,128)(2,1)S(1)} %pad_maximum_fusion), kind=kOutput, calls=%fused_computation | convolution fusion | flops 5438472192 | bytes 12386304 | tf_op jit(solution)/shard_map/to,tf->of/dot_general | solution.py:37
  335.5 6.0 multiply_reduce_fusion.10
  368.4 7.2 fusion.38
  420.2 29.9 %collective-permute-done.8 = bf16[4,2,1,72,1408]{4,3,2,1,0:T(8,128)(2,1)} collective-permute-done((bf16[4,2,1,72,1408]{4,3,2,1,0:T(8,128)(2,1)}, bf16[4,2,1,72,1408]{4,3,2,1,0:T(8,128)(2,1)}, u32[]{:S(2)}, u32[]{:S(2)}) %collective-permute-start.8) | collective-permute-done | bytes 1622048 | tf_op jit(solution)/shard_map/ppermute | solution.py:149
  450.0 9.0 %collective-permute-done.9 = bf16[4,1,2,72,1472]{4,3,2,1,0:T(8,128)(2,1)S(1)} collective-permute-done((bf16[4,1,2,72,1472]{4,3,2,1,0:T(8,128)(2,1)S(1)}, bf16[4,1,2,72,1472]{4,3,2,1,0:T(8,128)(2,1)S(1)}, u32[]{:S(2)}, u32[]{:S(2)}) %collective-permute-start.9) | collective-permute-done | bytes 1695776 | tf_op jit(solution)/shard_map/ppermute | solution.py:149
  503.2 8.4 %all-to-all-done.8 = bf16[32,2,6912]{2,1,0:T(2,128)(2,1)} async-done(((bf16[32,2,6912]{2,1,0:T(2,128)(2,1)}), bf16[32,2,6912]{2,1,0:T(2,128)(2,1)}, u32[]{:S(2)}, u32[]{:S(2)}) %all-to-all-start.8) | async-done | bytes 884768 | tf_op jit(solution)/shard_map/all_to_all | solution.py:153
  543.6 8.4 %fusion.34 = f32[1152,1728]{0,1:T(8,128)} fusion(bf16[1024,1728]{1,0:T(8,128)(2,1)S(1)} %copy-done.34, bf16[512,1152]{1,0:T(8,128)(2,1)} %collective-permute-done.1, bf16[512,1152]{1,0:T(8,128)(2,1)S(1)} %bitcast.347), kind=kOutput, calls=%fused_computation.72 | convolution fusion | flops 4081582080 | bytes 13860864 | tf_op jit(solution)/shard_map/td,te->de/dot_general | solution.py:37
  566.6 9.0 %copy.319 = f32[1152,1728]{1,0:T(8,128)} copy(f32[1152,1728]{0,1:T(8,128)} %fusion.34) | data formatting | bytes 15925248 | tf_op jit(solution)/shard_map/optimization_barrier | solution.py:501
  594.1 11.3 %collective-permute-done.14 = bf16[1,1,1,72,2880]{4,3,2,1,0:T(8,128)(2,1)} collective-permute-done((bf16[1,1,1,72,2880]{4,3,2,1,0:T(8,128)(2,1)}, bf16[1,1,1,72,2880]{4,3,2,1,0:T(8,128)(2,1)}, u32[]{:S(2)}, u32[]{:S(2)}) %collective-permute-start.14) | collective-permute-done | bytes 414752 | tf_op jit(solution)/shard_map/ppermute | solution.py:149
  611.8 7.6 %all-to-all-start.10 = ((f32[32,1,2412]{2,1,0:T(1,128)}), f32[32,1,2412]{2,1,0:T(1,128)}, u32[]{:S(2)}, u32[]{:S(2)}) async-start(f32[32,1,2412]{2,1,0:T(1,128)} %broadcast_in_dim.60), calls=%async_computation.10 | async-start | bytes 622592 | tf_op jit(solution)/shard_map/all_to_all | solution.py:153
  660.9 23.6 %collective-permute-done.21 = bf16[1,1,1,72,1728]{4,3,2,1,0:T(8,128)(2,1)S(1)} collective-permute-done((bf16[1,1,1,72,1728]{4,3,2,1,0:T(8,128)(2,1)S(1)}, bf16[1,1,1,72,1728]{4,3,2,1,0:T(8,128)(2,1)S(1)}, u32[]{:S(2)}, u32[]{:S(2)}) %collective-permute-start.21) | collective-permute-done | bytes 248864 | tf_op jit(solution)/shard_map/ppermute | solution.py:149
  (680 shorter events, 407.0 us)
Async XLA Ops:
  7.2 172.7 %all-gather.3.cloned.1.call-start = ((), (), s32[]{:S(2)}) async-start(), calls=%async_computation.14 | async-start | bytes 10948608 | tf_op jit(solution)/shard_map/all_gather | solution.py:205
  15.3 251.0 %all-gather.5.cloned.1.call-start = ((), (), s32[]{:S(2)}) async-start(), calls=%async_computation.15 | async-start | bytes 21897216 | tf_op jit(solution)/shard_map/all_gather | solution.py:205
  80.7 21.1 %all-to-all-start.3 = ((f32[32,2,1152]{2,1,0:T(2,128)}), f32[32,2,1152]{2,1,0:T(2,128)S(1)}, u32[]{:S(2)}, u32[]{:S(2)}) async-start(f32[32,2,1152]{2,1,0:T(2,128)} %copy.288), calls=%async_computation.3 | async-start | bytes 589824 | tf_op jit(solution)/shard_map/all_to_all | solution.py:156
  120.5 26.3 %all-to-all-start.5 = ((f32[32,2,1728]{2,1,0:T(2,128)}), f32[32,2,1728]{2,1,0:T(2,128)}, u32[]{:S(2)}, u32[]{:S(2)}) async-start(f32[32,2,1728]{2,1,0:T(2,128)} %reshape.931), calls=%async_computation.5 | async-start | bytes 917504 | tf_op jit(solution)/shard_map/all_to_all | solution.py:156
  146.8 31.7 %all-to-all-start.6 = ((f32[32,2,2304]{2,1,0:T(2,128)}), f32[32,2,2304]{2,1,0:T(2,128)}, u32[]{:S(2)}, u32[]{:S(2)}) async-start(f32[32,2,2304]{2,1,0:T(2,128)} %reshape.938), calls=%async_computation.6 | async-start | bytes 1179648 | tf_op jit(solution)/shard_map/all_to_all | solution.py:156
  150.9 534.5 %reduce-scatter.4.cloned.1.call-start = ((), (), s32[]{:S(2)}) async-start(), calls=%async_computation.16 | async-start | bytes 5640192 | tf_op jit(solution)/shard_map/reduce_scatter | solution.py:525
  343.2 22.7 %collective-permute-start.4 = (bf16[512,2304]{1,0:T(8,128)(2,1)}, bf16[512,2304]{1,0:T(8,128)(2,1)}, u32[]{:S(2)}, u32[]{:S(2)}) collective-permute-start(bf16[512,2304]{1,0:T(8,128)(2,1)} %bitcast.42), channel_id=1, source_target_pairs={{0,1},{1,0},{2,3},{3,2},{4,5},{5,4},{6,7},{7,6},{8,9},{9,8},{10,11... | collective-permute-start | bytes 7077896 | tf_op jit(solution)/shard_map/ppermute | solution.py:149
  357.6 186.0 %collective-permute-start.1 = (bf16[512,1152]{1,0:T(8,128)(2,1)}, bf16[512,1152]{1,0:T(8,128)(2,1)}, u32[]{:S(2)}, u32[]{:S(2)}) collective-permute-start(bf16[512,1152]{1,0:T(8,128)(2,1)} %bitcast.346), channel_id=1, source_target_pairs={{0,1},{1,0},{2,3},{3,2},{4,5},{5,4},{6,7},{7,6},{8,9},{9,8},{10,11... | collective-permute-start | bytes 3538952 | tf_op jit(solution)/shard_map/ppermute | solution.py:149
  402.0 48.1 %collective-permute-start.8 = (bf16[4,2,1,72,1408]{4,3,2,1,0:T(8,128)(2,1)}, bf16[4,2,1,72,1408]{4,3,2,1,0:T(8,128)(2,1)}, u32[]{:S(2)}, u32[]{:S(2)}) collective-permute-start(bf16[4,2,1,72,1408]{4,3,2,1,0:T(8,128)(2,1)} %dynamic-slice_convert_fusion), channel_id=1, source_target_pairs={{0,2},{1,3},{2,0},{3,1},{4,6},{5,7},{6,4},{7,5},{8,10},{9,11},{10,... | collective-permute-start | bytes 4866056 | tf_op jit(solution)/shard_map/ppermute | solution.py:149
  408.8 50.3 %collective-permute-start.9 = (bf16[4,1,2,72,1472]{4,3,2,1,0:T(8,128)(2,1)S(1)}, bf16[4,1,2,72,1472]{4,3,2,1,0:T(8,128)(2,1)S(1)}, u32[]{:S(2)}, u32[]{:S(2)}) collective-permute-start(bf16[4,1,2,72,1472]{4,3,2,1,0:T(8,128)(2,1)S(1)} %pad_maximum_fusion.7), channel_id=1, source_target_pairs={{0,4},{1,5},{2,6},{3,7},{4,0},{5,1},{6,2},{7,3},{8,12},{9,13},{10,... | collective-permute-start | bytes 5087240 | tf_op jit(solution)/shard_map/ppermute | solution.py:149
  476.7 34.9 %all-to-all-start.8 = ((bf16[32,2,6912]{2,1,0:T(2,128)(2,1)}), bf16[32,2,6912]{2,1,0:T(2,128)(2,1)}, u32[]{:S(2)}, u32[]{:S(2)}) async-start(bf16[32,2,6912]{2,1,0:T(2,128)(2,1)} %broadcast_in_dim.58), calls=%async_computation.8 | async-start | bytes 1769472 | tf_op jit(solution)/shard_map/all_to_all | solution.py:153
  487.9 31.9 %collective-permute-start.12 = (bf16[512,1728]{0,1:T(8,128)(2,1)}, bf16[512,1728]{0,1:T(8,128)(2,1)}, u32[]{:S(2)}, u32[]{:S(2)}) collective-permute-start(bf16[512,1728]{0,1:T(8,128)(2,1)} %copy.317), channel_id=1, source_target_pairs={{0,1},{1,0},{2,3},{3,2},{4,5},{5,4},{6,7},{7,6},{8,9},{9,8},{10,11... | collective-permute-start | bytes 5308424 | tf_op jit(solution)/shard_map/ppermute | solution.py:149
  492.9 34.8 %collective-permute-start.10 = (bf16[4,1,1,72,1408]{4,3,2,1,0:T(8,128)(2,1)}, bf16[4,1,1,72,1408]{4,3,2,1,0:T(8,128)(2,1)}, u32[]{:S(2)}, u32[]{:S(2)}) collective-permute-start(bf16[4,1,1,72,1408]{4,3,2,1,0:T(8,128)(2,1)} %dynamic-slice_convert_fusion.5), channel_id=1, source_target_pairs={{0,4},{1,5},{2,6},{3,7},{4,0},{5,1},{6,2},{7,3},{8,12},{9,13},{10,... | collective-permute-start | bytes 2433032 | tf_op jit(solution)/shard_map/ppermute | solution.py:149
  498.0 29.8 %collective-permute-start.11 = (bf16[4,1,1,72,1472]{4,3,2,1,0:T(8,128)(2,1)}, bf16[4,1,1,72,1472]{4,3,2,1,0:T(8,128)(2,1)}, u32[]{:S(2)}, u32[]{:S(2)}) collective-permute-start(bf16[4,1,1,72,1472]{4,3,2,1,0:T(8,128)(2,1)} %dynamic-slice_convert_fusion.4), channel_id=1, source_target_pairs={{0,2},{1,3},{2,0},{3,1},{4,6},{5,7},{6,4},{7,5},{8,10},{9,11},{10,... | collective-permute-start | bytes 2543624 | tf_op jit(solution)/shard_map/ppermute | solution.py:149
  528.6 23.4 %all-to-all-start.7 = ((bf16[32,2,2304]{2,1,0:T(2,128)(2,1)}), bf16[32,2,2304]{2,1,0:T(2,128)(2,1)}, u32[]{:S(2)}, u32[]{:S(2)}) async-start(bf16[32,2,2304]{2,1,0:T(2,128)(2,1)} %broadcast_in_dim.57), calls=%async_computation.7 | async-start | bytes 589824 | tf_op jit(solution)/shard_map/all_to_all | solution.py:153
  541.9 52.3 %collective-permute-start.13 = (bf16[1,1,1,72,2880]{4,3,2,1,0:T(8,128)(2,1)}, bf16[1,1,1,72,2880]{4,3,2,1,0:T(8,128)(2,1)}, u32[]{:S(2)}, u32[]{:S(2)}) collective-permute-start(bf16[1,1,1,72,2880]{4,3,2,1,0:T(8,128)(2,1)} %pad_maximum_fusion.12), channel_id=1, source_target_pairs={{0,8},{1,9},{2,10},{3,11},{4,12},{5,13},{6,14},{7,15},{8,16},{9,17... | collective-permute-start | bytes 1244168 | tf_op jit(solution)/shard_map/ppermute | solution.py:149
  561.6 32.2 %all-to-all-start.9 = ((f32[32,1,4140]{2,1,0:T(1,128)}), f32[32,1,4140]{2,1,0:T(1,128)S(1)}, u32[]{:S(2)}, u32[]{:S(2)}) async-start(f32[32,1,4140]{2,1,0:T(1,128)} %all_to_all.67), calls=%async_computation.9 | async-start | bytes 1081344 | tf_op jit(solution)/shard_map/all_to_all | solution.py:156
  579.9 31.0 %collective-permute-start.17 = (bf16[4,1,2,72,960]{4,3,2,1,0:T(8,128)(2,1)}, bf16[4,1,2,72,960]{4,3,2,1,0:T(8,128)(2,1)}, u32[]{:S(2)}, u32[]{:S(2)}) collective-permute-start(bf16[4,1,2,72,960]{4,3,2,1,0:T(8,128)(2,1)} %dynamic-slice_convert_fusion.1), channel_id=1, source_target_pairs={{0,4},{1,5},{2,6},{3,7},{4,0},{5,1},{6,2},{7,3},{8,12},{9,13},{10,... | collective-permute-start | bytes 3317768 | tf_op jit(solution)/shard_map/ppermute | solution.py:149
  582.5 22.9 %collective-permute-start.14 = (bf16[1,1,1,72,2880]{4,3,2,1,0:T(8,128)(2,1)}, bf16[1,1,1,72,2880]{4,3,2,1,0:T(8,128)(2,1)}, u32[]{:S(2)}, u32[]{:S(2)}) collective-permute-start(bf16[1,1,1,72,2880]{4,3,2,1,0:T(8,128)(2,1)} %pad_maximum_fusion.13), channel_id=1, source_target_pairs={{0,16},{1,17},{2,18},{3,19},{4,20},{5,21},{6,22},{7,23},{8,24},{9,... | collective-permute-start | bytes 1244168 | tf_op jit(solution)/shard_map/ppermute | solution.py:149
  589.2 21.7 %collective-permute-start.16 = (bf16[4,2,1,72,768]{4,3,2,1,0:T(8,128)(2,1)}, bf16[4,2,1,72,768]{4,3,2,1,0:T(8,128)(2,1)}, u32[]{:S(2)}, u32[]{:S(2)}) collective-permute-start(bf16[4,2,1,72,768]{4,3,2,1,0:T(8,128)(2,1)} %dynamic-slice_convert_fusion.3), channel_id=1, source_target_pairs={{0,2},{1,3},{2,0},{3,1},{4,6},{5,7},{6,4},{7,5},{8,10},{9,11},{10,... | collective-permute-start | bytes 2654216 | tf_op jit(solution)/shard_map/ppermute | solution.py:149
  611.8 20.6 %all-to-all-start.10 = ((f32[32,1,2412]{2,1,0:T(1,128)}), f32[32,1,2412]{2,1,0:T(1,128)}, u32[]{:S(2)}, u32[]{:S(2)}) async-start(f32[32,1,2412]{2,1,0:T(1,128)} %broadcast_in_dim.60), calls=%async_computation.10 | async-start | bytes 622592 | tf_op jit(solution)/shard_map/all_to_all | solution.py:153
  649.7 34.7 %collective-permute-start.21 = (bf16[1,1,1,72,1728]{4,3,2,1,0:T(8,128)(2,1)S(1)}, bf16[1,1,1,72,1728]{4,3,2,1,0:T(8,128)(2,1)S(1)}, u32[]{:S(2)}, u32[]{:S(2)}) collective-permute-start(bf16[1,1,1,72,1728]{4,3,2,1,0:T(8,128)(2,1)S(1)} %pad_maximum_fusion.17), channel_id=1, source_target_pairs={{0,16},{1,17},{2,18},{3,19},{4,20},{5,21},{6,22},{7,23},{8,24},{9,... | collective-permute-start | bytes 746504 | tf_op jit(solution)/shard_map/ppermute | solution.py:149
  649.9 34.6 %collective-permute-start.20 = (bf16[1,1,1,72,1728]{4,3,2,1,0:T(8,128)(2,1)S(1)}, bf16[1,1,1,72,1728]{4,3,2,1,0:T(8,128)(2,1)S(1)}, u32[]{:S(2)}, u32[]{:S(2)}) collective-permute-start(bf16[1,1,1,72,1728]{4,3,2,1,0:T(8,128)(2,1)S(1)} %pad_maximum_fusion.16), channel_id=1, source_target_pairs={{0,8},{1,9},{2,10},{3,11},{4,12},{5,13},{6,14},{7,15},{8,16},{9,17... | collective-permute-start | bytes 746504 | tf_op jit(solution)/shard_map/ppermute | solution.py:149
  654.7 39.1 %all-to-all-start.12 = ((bf16[32,64,160]{2,1,0:T(8,128)(2,1)}), bf16[32,64,160]{2,1,0:T(8,128)(2,1)}, u32[]{:S(2)}, u32[]{:S(2)}) async-start(bf16[32,64,160]{2,1,0:T(8,128)(2,1)} %broadcast_in_dim.63), calls=%async_computation.12 | async-start | bytes 2097152 | tf_op jit(solution)/shard_map/all_to_all | solution.py:153
  (164 other events, 1999.1 us)
Sparse Core Ops, SparseCore 0:
  15.4 98.2 all-gather.2
  117.3 148.9 all-gather.4
  364.4 152.0 reduce-scatter.3

commit v3 on v2

--- a/solution.py
+++ b/solution.py
@@ -24,7 +24,6 @@
 
 HIGHEST_PRECISION = lax.Precision.HIGHEST
 AXES = ("z", "x", "y", "c")
-CORE_FIRST = ("c", "z", "x", "y")
 LOG_TWO = math.log(2.0)
 THRESHOLD = 1.0
 LEARN_RATE = 0.05
@@ -127,7 +126,7 @@
         self.z = dp // self.x
         self.count = dp * mod
         self.size = {"z": self.z, "x": self.x, "y": self.y, "c": self.core}
-        self.dim = {"z": 0, "x": 1, "y": 2}
+        self.dim = {"x": 0, "y": 1, "z": 2}
 
     def place(self, axis):
         index = lax.axis_index(AXES)
@@ -147,6 +146,14 @@
             target = ((spot["z"] * self.x + spot["x"]) * self.y + spot["y"]) * self.core + spot["c"]
             pairs.append((index, target))
         return lax.ppermute(block, AXES, pairs)
+
+    def inner(self, values):
+        shape = (*values.shape[:-1], self.z, self.x * self.y, -1)
+        return values.reshape(shape).swapaxes(-3, -2).reshape(values.shape)
+
+    def outer(self, values):
+        shape = (*values.shape[:-1], self.x * self.y, self.z, -1)
+        return values.reshape(shape).swapaxes(-3, -2).reshape(values.shape)
 
     def spread(self, block):
         copies = jnp.broadcast_to(block[None], (self.count, *block.shape))
@@ -201,15 +208,15 @@
     return pick(core, halves[0], halves[1]), pick(core, small[0], small[1])
 
 
-def gather_halves(chunk):
-    whole = lax.all_gather(chunk, CORE_FIRST, axis=0, tiled=True)
+def gather_halves(rows):
+    whole = lax.all_gather(rows, ("c", "x", "y", "z"), axis=0, tiled=True)
     return whole[:D], whole[D:]
 
 
 class Reduction:
     def __init__(self, links, gradients, kind=jnp.bfloat16):
         self.links, self.kind = links, kind
-        shape = (links.z, links.x, links.y, D * links.core // links.count)
+        shape = (links.x, links.y, links.z, D * links.core // links.count)
         self.blocks = [rows.reshape(*shape, -1) for rows in gradients]
         total = sum(rows.shape[1] for rows in gradients)
         middle = total // 256 * 128
@@ -411,7 +418,7 @@
     got = links.spread(jnp.concatenate([digits, small]))
     digits = got[:, : 4 * images].astype(jnp.int32).reshape(links.count, 2, 2, images)
     integers = digits[:, 0] * 32 + digits[:, 1]
-    small = got[:, 4 * images :].reshape(D, SMALL)
+    small = links.inner(got[:, 4 * images :].reshape(D, SMALL).T).T
     w_patch, w_head = small[:, :PATCH], small[:, PATCH:]
     all_steps = integers[:, 0].reshape(everyone)
     chosen = integers[:, 1].reshape(everyone)
@@ -453,12 +460,9 @@
         parts.reshape(-1, groups, images, own_cols).sum(0).transpose(1, 0, 2).reshape(images, 6 * D)
         + biases[3:].reshape(6 * D)
     ).astype(low)
-    pieces = jnp.split(modulation.astype(wide), 6, axis=1)
+    pieces = links.inner(modulation.astype(wide).reshape(images, 6, D))
+    pieces = [pieces[:, part] for part in range(6)]
     final_part = window.put(matmul("id,rd->ir", all_signal, stem), STARTS[3], 2 * D)
-    final_mod = links.deliver(final_part.reshape(links.count, images, 2 * D)).sum(0) + biases[
-        1:3
-    ].reshape(2 * D)
-    final_shift, final_scale = final_mod[:, :D], final_mod[:, D:]
 
     sched = plan(timesteps)
     target = noise.reshape(images, SEQ, PATCH)
@@ -466,7 +470,7 @@
         sched[:, 0][:, None, None] * latents.reshape(images, SEQ, PATCH)
         + sched[:, 1][:, None, None] * target
     ).astype(low)
-    stream = matmul("isp,dp->isd", noisy_rows, w_patch) + biases[0] + positions()[None]
+    stream = matmul("isp,dp->isd", noisy_rows, w_patch) + links.inner(biases[0]) + links.inner(positions())[None]
     normed = modulate(stream, pieces[0], pieces[1]).astype(low)
     mixed, kept = [], []
     for half in range(2):
@@ -476,6 +480,12 @@
     attended = sum(matmul("isd,od->iso", mixed[half], w_proj[half]) for half in range(2))
     middle = stream + pieces[2][:, None, :] * attended
     second = modulate(middle, pieces[3], pieces[4]).astype(low)
+    second, final_part = lax.optimization_barrier((second, final_part))
+    final_mod = links.deliver(final_part.reshape(links.count, images, 2 * D)).sum(0) + biases[
+        1:3
+    ].reshape(2 * D)
+    final_mod = links.inner(final_mod.reshape(images, 2, D))
+    final_shift, final_scale = final_mod[:, 0], final_mod[:, 1]
     inner = [matmul("isd,df->isf", second, w_up[half]) for half in range(2)]
     active = [gelu_tanh(rows).astype(low) for rows in inner]
     output = sum(matmul("isf,of->iso", active[half], w_down[half]) for half in range(2))
@@ -497,6 +507,12 @@
             mine, sent = pick(core, first, second), pick(core, second, first)
         return jnp.concatenate([mine, links.send(sent, "c")], 0)
 
+    def sum_near(rows):
+        return lax.psum_scatter(rows, ("x", "y"), scatter_dimension=0, tiled=True)
+
+    def sum_far(rows):
+        return lax.psum_scatter(rows, "z", scatter_dimension=0, tiled=True)
+
     def together(*values):
         return lax.optimization_barrier(values)
 
@@ -505,7 +521,7 @@
     upstream, shift_grad, scale_grad = modulate_back(
         layer_out, final_shift, final_scale, matmul("iso,do->isd", out_grad, w_head)
     )
-    final_grad = jnp.concatenate([shift_grad, scale_grad], 1)
+    final_grad = links.outer(jnp.stack([shift_grad, scale_grad], 1)).reshape(images, 2 * D)
     down_in = (pieces[5][:, None, :] * upstream).astype(low)
     gate_b = jnp.sum(upstream * output, 1)
     active_both = with_partner(*active)
@@ -519,13 +535,14 @@
         ).astype(low)
         for half in range(2)
     ]
+    inner_both = with_partner(*inner_grad)
     inner_grad, down_both, active_both = together(inner_grad, down_both, active_both)
     grad_down = matmul("to,tf->of", down_both, active_both).astype(low)
-    inner_grad, grad_down = together(inner_grad, grad_down)
-    reduced_down = lax.psum_scatter(
-        grad_down, ("z", "x", "y"), scatter_dimension=0, tiled=True
-    ).astype(wide)
-    inner_both = with_partner(*inner_grad)
+    inner_both, grad_down = together(inner_both, grad_down)
+    grad_up = matmul("td,tf->df", second_both, inner_both).astype(low)
+    grad_mlp = jnp.concatenate([grad_up, grad_down], 1)
+    inner_grad, grad_mlp = together(inner_grad, grad_mlp)
+    near_mlp = sum_near(grad_mlp)
     second_grad = sum(
         matmul("isf,df->isd", inner_grad[half], w_up[half]) for half in range(2)
     )
@@ -535,37 +552,29 @@
     gate_a = jnp.sum(grad_mid * attended, 1)
     proj_both = with_partner(proj_in)
     final_low = final_grad.astype(low)
-    early = jnp.concatenate([gate_a, shift_b, scale_b, gate_b], 1).astype(low)
+    early = links.outer(jnp.stack([gate_a, shift_b, scale_b, gate_b], 1)).reshape(images, 4 * D)
+    early = early.astype(low)
     early = links.spread(jnp.concatenate([early, final_low], 1)).reshape(everyone, 6 * D)
-    proj_in, inner_both, proj_both = together(proj_in, inner_both, proj_both)
-    grad_up = matmul("td,tf->df", second_both, inner_both)
-    grad_proj = matmul("to,td->od", proj_both, mixed_both)
-    proj_in, grad_up, grad_proj = together(proj_in, grad_up, grad_proj)
-    first = Reduction(links, [grad_up, grad_proj])
-    got = first.send("yx")
     qkv_grad = [
         attend_back(kept[half], matmul("iso,od->isd", proj_in, w_proj[half])) for half in range(2)
     ]
-    qkv_grad, got = together(qkv_grad, got)
-    first.add(got)
-    got = first.send("xy")
+    grad_proj = matmul("to,td->od", proj_both, mixed_both)
     qkv_both = with_partner(*qkv_grad)
     normed_grad = sum(matmul("ise,de->isd", qkv_grad[half], w_qkv[half]) for half in range(2))
     back_in, shift_a, scale_a = modulate_back(stream, pieces[0], pieces[1], normed_grad)
     stream_grad = grad_mid + back_in
-    late = jnp.concatenate([shift_a, scale_a], 1).astype(low)
-    late, stream_grad, got, qkv_both = together(late, stream_grad, got, qkv_both)
+    late = links.outer(jnp.stack([shift_a, scale_a], 1)).reshape(images, 2 * D).astype(low)
+    late, stream_grad, qkv_both, early = together(late, stream_grad, qkv_both, early)
     late = links.spread(late).reshape(everyone, 2 * D)
-    first.add(got)
-    first.join()
-    got = first.send("z")
     grad_qkv = matmul("td,te->de", normed_both, qkv_both)
     grad_patch = matmul("isp,isd->dp", noisy_rows, stream_grad.astype(low))
-    small_grad = jnp.concatenate([grad_patch, grad_head], 1).reshape(links.count, -1)
-    grad_qkv, late = together(grad_qkv, late)
-    second = Reduction(links, [grad_qkv])
-    more = second.send("yx")
-
+    small_grad = links.outer(jnp.concatenate([grad_patch, grad_head], 1).T).T
+    small_grad = small_grad.reshape(links.count, -1)
+    sums_of_attention = Reduction(links, [grad_qkv, grad_proj])
+    more = sums_of_attention.send("yx")
+
+    late, near_mlp = together(late, near_mlp)
+    reduced_mlp = sum_far(near_mlp)
     all_final = early[:, 4 * D :]
     all_modulation = jnp.concatenate([late, early[:, : 4 * D]], 1)
     own_modulation = lax.dynamic_slice_in_dim(all_modulation, col_at, own_cols, 1)
@@ -577,7 +586,7 @@
         row_at,
         1,
     )
-    sums = jnp.concatenate([jnp.sum(stream_grad, (0, 1)), jnp.sum(final_grad, 0)])
+    sums = jnp.concatenate([links.outer(jnp.sum(stream_grad, (0, 1))), jnp.sum(final_grad, 0)])
     share = -(-sums.shape[0] // links.count)
     sums = jnp.pad(sums, (0, share * links.count - sums.shape[0])).reshape(links.count, share)
     summed = links.deliver(
@@ -586,10 +595,9 @@
     small = summed[images * D + share :]
     condition_grad = smooth_back(jax.nn.silu, condition, summed[: images * D].reshape(images, D))
     spreading = jnp.concatenate([condition_grad.reshape(-1), summed[images * D : images * D + share]])
-    spreading, got, more = together(spreading, got, more)
-    first.add(got)
-    second.add(more)
-    more = second.send("xy")
+    spreading, more = together(spreading, more)
+    sums_of_attention.add(more)
+    more = sums_of_attention.send("xy")
     spread = links.spread(spreading)
     all_condition = spread[:, : images * D].reshape(everyone, D)
     all_sums = spread[:, images * D :].reshape(-1)[: 3 * D]
@@ -600,17 +608,15 @@
     row = window.first + jnp.arange(window.rows)
     before_part = jnp.where((row >= STARTS[1]) & (row < STARTS[2]), before_part, 0.0).astype(low)
     before_part, more = together(before_part, more)
-    second.add(more)
-    second.join()
-    more = second.send("z")
+    sums_of_attention.add(more)
+    sums_of_attention.join()
+    more = sums_of_attention.send("z")
     before_low = window.assemble(links.spread(before_part), STARTS[1], D).astype(low)
-    second.add(more)
-    reduced_rest = first.result()
-    joint = jnp.concatenate(
-        [second.result(), reduced_rest[:, 2 * D :], reduced_rest[:, : 2 * D], reduced_down], 1
-    )
+    sums_of_attention.add(more)
+    joint = jnp.concatenate([sums_of_attention.result(), reduced_mlp.astype(wide)], 1)
+    square = jnp.sum(joint * joint) + jnp.sum(small * small)
+    totals = links.spread(jnp.stack([loss_local, square])).sum(0)
     block_grad = flat_gradient(links, joint, small)
-    totals = links.spread(jnp.stack([loss_local, jnp.sum(block_grad * block_grad)])).sum(0)
     loss_total, squares = totals[0], totals[1]
     bias_rows = jnp.concatenate(
         [all_sums, jnp.sum(all_modulation.astype(wide), 0)]

time: 759 us -> 665 us (0.88)
  local copies, waits for them, and re-layouts: 148 us -> 109 us
  waiting for transfers between devices: 249 us -> 217 us
  starting transfers between devices: 85.5 us -> 67.7 us
    ppermute x24 -> x17, waiting for transfers between devices: 86.8 us -> 51.3 us  [send(): return lax.ppermute(block, AXES, pairs)]
    all_to_all x8, waiting for transfers between devices: 30.4 us -> 45 us  [spread(): return lax.all_to_all(copies, AXES, split_axis=0, concat_axis=0, tiled=True)]
    all_gather x2, waiting for transfers between devices: 64.2 us -> 53.1 us  [gather_halves(): whole = lax.all_gather(rows, ('c', 'x', 'y', 'z'), axis=0, tiled=True)]
    ppermute x24 -> x17, starting transfers between devices: 24.2 us -> 14.2 us  [send(): return lax.ppermute(block, AXES, pairs)]
    optimization_barrier x2 -> x1, local copies, waits for them, and re-layouts: 12.1 us -> 3.47 us  [together(): return lax.optimization_barrier(values)]
    select_n x5 -> x4, local copies, waits for them, and re-layouts: 13.8 us -> 6.1 us  [pick(): return jnp.where(own == 0, first, second)]
    unnamed x306 -> x236, local copies, waits for them, and re-layouts: 21.8 us -> 21.2 us
  transfers between devices with their start and end apart: 40 -> 34, of which waited for: 18 -> 16; matrix products, arithmetic and copies ran while one was open for 37% -> 45% of each run, Pallas kernels for 0% -> 0%
where the time goes in v3:
time: 665 us; the launch traced here: 654 us
  waiting for transfers between devices  217 us (33%)
  matrix products  159 us (24%)
  local copies, waits for them, and re-layouts  109 us (16%)
  other arithmetic  76.7 us (12%)
  starting transfers between devices  67.7 us (10%)
  between operations  24 us (4%)
    dot_general x48, matrix products, matmul(): return jnp.einsum(form, left, right, preferred_element_type=jnp.float32)  151 us
    all_to_all x5, waiting for transfers between devices, deliver(): return lax.all_to_all(blocks, AXES, split_axis=0, concat_axis=0, tiled=True)  67.3 us
    all_gather x2, waiting for transfers between devices, gather_halves(): whole = lax.all_gather(rows, ('c', 'x', 'y', 'z'), axis=0, tiled=True)  53.1 us
    ppermute x17, waiting for transfers between devices, send(): return lax.ppermute(block, AXES, pairs)  51.3 us
    all_to_all x8, waiting for transfers between devices, spread(): return lax.all_to_all(copies, AXES, split_axis=0, concat_axis=0, tiled=True)  45 us
    all_to_all x8, starting transfers between devices, spread(): return lax.all_to_all(copies, AXES, split_axis=0, concat_axis=0, tiled=True)  34.9 us
    unnamed x236, local copies, waits for them, and re-layouts  21.2 us
    all_to_all x5, starting transfers between devices, deliver(): return lax.all_to_all(blocks, AXES, split_axis=0, concat_axis=0, tiled=True)  18.4 us
  transfers between devices with their start and end apart: 34, of which 16 were waited for; matrix products, arithmetic and copies ran while one was open for 45% of the time, Pallas kernels for 0%

profile of v3, /device:TPU:0, one launch (start us, length us, event | category | flops | bytes accessed | tf_op | source)
XLA Modules:
  0.0 653.7 jit_solution(7803570514982836301)
XLA Ops:
  19.4 7.2 %all-to-all-start = ((bf16[32,2,868]{2,1,0:T(2,128)(2,1)}), bf16[32,2,868]{2,1,0:T(2,128)(2,1)S(1)}, u32[]{:S(2)}, u32[]{:S(2)}) async-start(bf16[32,2,868]{2,1,0:T(2,128)(2,1)} %reshape.1041), calls=%async_computation | async-start | bytes 229376 | tf_op jit(solution)/shard_map/all_to_all | solution.py:160
  43.9 14.8 %all-to-all-done.1 = f32[32,1,2628]{2,1,0:T(1,128)S(1)} async-done(((f32[32,1,2628]{2,1,0:T(1,128)}), f32[32,1,2628]{2,1,0:T(1,128)S(1)}, u32[]{:S(2)}, u32[]{:S(2)}) %all-to-all-start.1) | async-done | bytes 336416 | tf_op jit(solution)/shard_map/all_to_all | solution.py:163
  69.3 7.6 %all-to-all-done.2 = f32[32,1,2628]{2,1,0:T(1,128)S(1)} async-done(((f32[32,1,2628]{2,1,0:T(1,128)}), f32[32,1,2628]{2,1,0:T(1,128)S(1)}, u32[]{:S(2)}, u32[]{:S(2)}) %all-to-all-start.2) | async-done | bytes 336416 | tf_op jit(solution)/shard_map/all_to_all | solution.py:160
  85.8 14.6 %all-to-all-done.3 = f32[32,2,1152]{2,1,0:T(2,128)S(1)} async-done(((f32[32,2,1152]{2,1,0:T(2,128)}), f32[32,2,1152]{2,1,0:T(2,128)S(1)}, u32[]{:S(2)}, u32[]{:S(2)}) %all-to-all-start.3) | async-done | bytes 294944 | tf_op jit(solution)/shard_map/all_to_all | solution.py:163
  106.6 8.0 %all-to-all-done.4 = bf16[32,2,1152]{2,1,0:T(2,128)(2,1)S(1)} async-done(((bf16[32,2,1152]{2,1,0:T(2,128)(2,1)}), bf16[32,2,1152]{2,1,0:T(2,128)(2,1)S(1)}, u32[]{:S(2)}, u32[]{:S(2)}) %all-to-all-start.4) | async-done | bytes 147488 | tf_op jit(solution)/shard_map/all_to_all | solution.py:160
  125.9 13.0 %all-to-all-done.5 = f32[32,2,1728]{2,1,0:T(2,128)S(1)} async-done(((f32[32,2,1728]{2,1,0:T(2,128)}), f32[32,2,1728]{2,1,0:T(2,128)S(1)}, u32[]{:S(2)}, u32[]{:S(2)}) %all-to-all-start.5) | async-done | bytes 442400 | tf_op jit(solution)/shard_map/all_to_all | solution.py:163
  158.9 15.0 %fusion.189 = (f32[2,256]{1,0:T(2,128)S(1)}, f32[2,256,1152]{2,1,0:T(8,128)S(1)}, f32[2,256,1152]{2,1,0:T(8,128)}) fusion(f32[2,256,1152]{2,1,0:T(8,128)S(1)} %get-tuple-element.174, f32[2,1152]{1,0:T(2,128)S(1)} %get-tuple-element.148, f32[2,256,1152]{2,1,0:T(8,128)S(1)} %fusion.68, bf16[2,256,576]{1,2,0:T(8,128)(2,1)S(1)} %bitcast.379, ...), kind=kOutput, calls=%fused_computation.443 | convolution fusion | flops 681836032 | bytes 11512832 | tf_op jit(solution)/shard_map/isd,od->iso/dot_general | solution.py:36
  182.7 23.7 %all-to-all-done.6 = f32[32,2,2304]{2,1,0:T(2,128)S(1)} async-done(((f32[32,2,2304]{2,1,0:T(2,128)}), f32[32,2,2304]{2,1,0:T(2,128)S(1)}, u32[]{:S(2)}, u32[]{:S(2)}) %all-to-all-start.6) | async-done | bytes 589856 | tf_op jit(solution)/shard_map/all_to_all | solution.py:163
  206.9 53.1 %all-gather.5.cloned.1.call-done = bf16[2304,4608]{1,0:T(8,128)(2,1)} async-done(((bf16[72,4608]{1,0:T(8,128)(2,1)}), bf16[2304,4608]{1,0:T(8,128)(2,1)}) %all-gather.5.cloned.1.call-update) | async-done | bytes 21233680 | tf_op jit(solution)/shard_map/all_gather | solution.py:212
  260.0 6.1 fusion.20
  266.1 7.6 %broadcast_select_fusion.3 = (bf16[2,256,2304]{2,1,0:T(8,128)(2,1)S(1)}, bf16[2,256,2304]{2,1,0:T(8,128)(2,1)S(1)}, f32[2,256,2304]{2,1,0:T(8,128)S(1)}) fusion(pred[]{:T(512)S(6)} %eq.108, f32[2,256,2304]{2,1,0:T(8,128)S(1)} %fusion.20, bf16[2,256,1152]{2,1,0:T(8,128)(2,1)} %add_convert_fusion.1, bf16[2304,4608]{1,0:T(8,128)(2,1)} %all-gather.5.cloned.1.call-done), kind=kOutput, calls=%fused_computation.114 | convolution fusion | flops 2741501952 | bytes 20643840 | tf_op jit(solution)/shard_map/isd,df->isf/dot_general | solution.py:36
  273.7 8.3 %fusion.18 = f32[2,256,1152]{2,1,0:T(8,128)S(1)} fusion(bf16[2304,4608]{1,0:T(8,128)(2,1)} %all-gather.5.cloned.1.call-done, f32[2,256,2304]{2,1,0:T(8,128)S(1)} %get-tuple-element.182), kind=kOutput, calls=%fused_computation.43 | convolution fusion | flops 2728525824 | bytes 12386304 | tf_op jit(solution)/shard_map/isf,of->iso/dot_general | solution.py:36
  282.1 6.3 fusion.188
  294.7 7.6 %fusion.15 = bf16[2,256,2304]{2,1,0:T(8,128)(2,1)S(1)} fusion(f32[2,256,2304]{2,1,0:T(8,128)S(1)} %fusion.20, bf16[2,256,1152]{2,1,0:T(8,128)(2,1)S(1)} %get-tuple-element.98, bf16[2304,4608]{1,0:T(8,128)(2,1)} %all-gather.5.cloned.1.call-done), kind=kOutput, calls=%fused_computation.26 | convolution fusion | flops 2741501952 | bytes 13565952 | tf_op jit(solution)/shard_map/iso,of->isf/dot_general | solution.py:36
  302.3 9.9 %broadcast_select_fusion.1 = (bf16[2,256,2304]{2,1,0:T(8,128)(2,1)S(1)}, bf16[2,256,2304]{2,1,0:T(8,128)(2,1)}, bf16[2,256,2304]{2,1,0:T(8,128)(2,1)}) fusion(bf16[2,256,2304]{2,1,0:T(8,128)(2,1)S(1)} %fusion.15, pred[]{:T(512)S(6)} %eq.108, f32[2,256,2304]{2,1,0:T(8,128)S(1)} %bitcast.430, bf16[2,256,1152]{2,1,0:T(8,128)(2,1)S(1)} %get-tuple-element.98, ...), kind=kOutput, calls=%fused_computation.112 | convolution fusion | flops 2743861248 | bytes 20643840 | tf_op jit(solution)/shard_map/iso,of->isf/dot_general | solution.py:36
  313.0 6.3 convolution_convert_fusion.1
  319.7 7.9 %convolution_convert_fusion = bf16[1152,2304]{1,0:T(8,128)(2,1)S(1)} fusion(bf16[1024,2304]{1,0:T(8,128)(2,1)S(1)} %pad_maximum_fusion.2, bf16[512,1152]{1,0:T(8,128)(2,1)} %collective-permute-done.4, bf16[512,1152]{1,0:T(8,128)(2,1)} %bitcast.58), kind=kOutput, calls=%fused_computation | convolution fusion | flops 5443190784 | bytes 12386304 | tf_op jit(solution)/shard_map/td,tf->df/dot_general | solution.py:36
  351.1 7.8 %fusion.183 = (bf16[2,1152]{1,0:T(2,128)(2,1)S(1)}, f32[2,256]{1,0:T(2,128)S(1)}, f32[2,256,1152]{2,1,0:T(8,128)}) fusion(f32[2,1152]{1,0:T(2,128)S(1)} %get-tuple-element.145, f32[2,256,1152]{2,1,0:T(8,128)S(1)} %copy-done.7, f32[2,256]{1,0:T(2,128)S(1)} %broadcast_multiply_fusion.2, f32[2,256,1152]{2,1,0:T(8,128)S(1)} %fusion.16, ...), kind=kOutput, calls=%fused_computation.440 | convolution fusion | flops 2721445120 | bytes 14763520 | tf_op jit(solution)/shard_map/isf,df->isd/dot_general | solution.py:36
  486.7 19.0 %collective-permute-done.10 = bf16[1,2,4,72,1152]{4,3,2,1,0:T(8,128)(2,1)} collective-permute-done((bf16[1,2,4,72,1152]{4,3,2,1,0:T(8,128)(2,1)}, bf16[1,2,4,72,1152]{4,3,2,1,0:T(8,128)(2,1)}, u32[]{:S(2)}, u32[]{:S(2)}) %collective-permute-start.10) | collective-permute-done | bytes 1327136 | tf_op jit(solution)/shard_map/ppermute | solution.py:148
  521.1 9.6 %all-to-all-done.10 = f32[32,1,2412]{2,1,0:T(1,128)S(1)} async-done(((f32[32,1,2412]{2,1,0:T(1,128)}), f32[32,1,2412]{2,1,0:T(1,128)S(1)}, u32[]{:S(2)}, u32[]{:S(2)}) %all-to-all-start.10) | async-done | bytes 308768 | tf_op jit(solution)/shard_map/all_to_all | solution.py:160
  555.7 7.0 %collective-permute-done.14 = bf16[1,1,1,72,2304]{4,3,2,1,0:T(8,128)(2,1)S(1)} collective-permute-done((bf16[1,1,1,72,2304]{4,3,2,1,0:T(8,128)(2,1)}, bf16[1,1,1,72,2304]{4,3,2,1,0:T(8,128)(2,1)S(1)}, u32[]{:S(2)}, u32[]{:S(2)}) %collective-permute-start.14) | collective-permute-done | bytes 331808 | tf_op jit(solution)/shard_map/ppermute | solution.py:148
  562.8 23.7 %collective-permute-done.13 = bf16[1,1,1,72,2304]{4,3,2,1,0:T(8,128)(2,1)S(1)} collective-permute-done((bf16[1,1,1,72,2304]{4,3,2,1,0:T(8,128)(2,1)S(1)}, bf16[1,1,1,72,2304]{4,3,2,1,0:T(8,128)(2,1)S(1)}, u32[]{:S(2)}, u32[]{:S(2)}) %collective-permute-start.13) | collective-permute-done | bytes 331808 | tf_op jit(solution)/shard_map/ppermute | solution.py:148
  586.7 11.8 %all-to-all-done.12 = bf16[32,64,160]{2,1,0:T(8,128)(2,1)} async-done(((bf16[32,64,160]{2,1,0:T(8,128)(2,1)}), bf16[32,64,160]{2,1,0:T(8,128)(2,1)}, u32[]{:S(2)}, u32[]{:S(2)}) %all-to-all-start.12) | async-done | bytes 655392 | tf_op jit(solution)/shard_map/all_to_all | solution.py:160
  639.0 6.7 %divide_subtract_fusion = (f32[499392]{0:T(1024)}, f32[499392]{0:T(1024)}, f32[499392]{0:T(1024)}) fusion(f32[499392]{0:T(1024)} %param.20, f32[499392]{0:T(1024)} %mul.991, f32[499392]{0:T(1024)} %param.21, f32[499392]{0:T(1024)} %param.22), kind=kLoop, calls=%fused_computation.120 | loop fusion | flops 5992704 | bytes 13982976 | tf_op jit(solution)/shard_map/sub | solution.py:342
  (612 shorter events, 327.0 us)
Async XLA Ops:
  7.2 135.2 %all-gather.3.cloned.1.call-start = ((), (), s32[]{:S(2)}) async-start(), calls=%async_computation.15 | async-start | bytes 10948608 | tf_op jit(solution)/shard_map/all_gather | solution.py:212
  15.3 244.7 %all-gather.5.cloned.1.call-start = ((), (), s32[]{:S(2)}) async-start(), calls=%async_computation.16 | async-start | bytes 21897216 | tf_op jit(solution)/shard_map/all_gather | solution.py:212
  38.7 20.0 %all-to-all-start.1 = ((f32[32,1,2628]{2,1,0:T(1,128)}), f32[32,1,2628]{2,1,0:T(1,128)S(1)}, u32[]{:S(2)}, u32[]{:S(2)}) async-start(f32[32,1,2628]{2,1,0:T(1,128)} %all_to_all.57), calls=%async_computation.1 | async-start | bytes 688128 | tf_op jit(solution)/shard_map/all_to_all | solution.py:163
  79.1 21.3 %all-to-all-start.3 = ((f32[32,2,1152]{2,1,0:T(2,128)}), f32[32,2,1152]{2,1,0:T(2,128)S(1)}, u32[]{:S(2)}, u32[]{:S(2)}) async-start(f32[32,2,1152]{2,1,0:T(2,128)} %copy.401), calls=%async_computation.3 | async-start | bytes 589824 | tf_op jit(solution)/shard_map/all_to_all | solution.py:163
  117.2 21.7 %all-to-all-start.5 = ((f32[32,2,1728]{2,1,0:T(2,128)}), f32[32,2,1728]{2,1,0:T(2,128)S(1)}, u32[]{:S(2)}, u32[]{:S(2)}) async-start(f32[32,2,1728]{2,1,0:T(2,128)} %reshape.973), calls=%async_computation.5 | async-start | bytes 917504 | tf_op jit(solution)/shard_map/all_to_all | solution.py:163
  178.0 28.4 %all-to-all-start.6 = ((f32[32,2,2304]{2,1,0:T(2,128)}), f32[32,2,2304]{2,1,0:T(2,128)S(1)}, u32[]{:S(2)}, u32[]{:S(2)}) async-start(f32[32,2,2304]{2,1,0:T(2,128)} %reshape.982), calls=%async_computation.6 | async-start | bytes 1179648 | tf_op jit(solution)/shard_map/all_to_all | solution.py:163
  181.4 268.5 %reduce-scatter.7.cloned.1.call-start = ((), (), s32[]{:S(2)}) async-start(), calls=%async_computation.17 | async-start | bytes 13271040
  182.4 137.3 %collective-permute-start.4 = (bf16[512,1152]{1,0:T(8,128)(2,1)}, bf16[512,1152]{1,0:T(8,128)(2,1)}, u32[]{:S(2)}, u32[]{:S(2)}) collective-permute-start(bf16[512,1152]{1,0:T(8,128)(2,1)} %bitcast.58), channel_id=1, source_target_pairs={{0,1},{1,0},{2,3},{3,2},{4,5},{5,4},{6,7},{7,6},{8,9},{9,8},{10,11... | collective-permute-start | bytes 3538952 | tf_op jit(solution)/shard_map/ppermute | solution.py:148
  294.2 18.3 %collective-permute-start.2 = (bf16[512,1152]{1,0:T(8,128)(2,1)S(1)}, bf16[512,1152]{1,0:T(8,128)(2,1)S(1)}, u32[]{:S(2)}, u32[]{:S(2)}) collective-permute-start(bf16[512,1152]{1,0:T(8,128)(2,1)S(1)} %bitcast.377), channel_id=1, source_target_pairs={{0,1},{1,0},{2,3},{3,2},{4,5},{5,4},{6,7},{7,6},{8,9},{9,8},{10,11... | collective-permute-start | bytes 3538952 | tf_op jit(solution)/shard_map/ppermute | solution.py:148
  336.7 83.8 %collective-permute-start.1 = (bf16[512,1152]{1,0:T(8,128)(2,1)}, bf16[512,1152]{1,0:T(8,128)(2,1)}, u32[]{:S(2)}, u32[]{:S(2)}) collective-permute-start(bf16[512,1152]{1,0:T(8,128)(2,1)} %bitcast.401), channel_id=1, source_target_pairs={{0,1},{1,0},{2,3},{3,2},{4,5},{5,4},{6,7},{7,6},{8,9},{9,8},{10,11... | collective-permute-start | bytes 3538952 | tf_op jit(solution)/shard_map/ppermute | solution.py:148
  341.2 68.6 %collective-permute-start.9 = (bf16[512,576]{0,1:T(8,128)(2,1)}, bf16[512,576]{0,1:T(8,128)(2,1)}, u32[]{:S(2)}, u32[]{:S(2)}) collective-permute-start(bf16[512,576]{0,1:T(8,128)(2,1)} %bitcast.157), channel_id=1, source_target_pairs={{0,1},{1,0},{2,3},{3,2},{4,5},{5,4},{6,7},{7,6},{8,9},{9,8},{10,11... | collective-permute-start | bytes 1769480 | tf_op jit(solution)/shard_map/ppermute | solution.py:148
  367.4 48.8 %all-to-all-start.7 = ((bf16[32,2,6912]{2,1,0:T(2,128)(2,1)}), bf16[32,2,6912]{2,1,0:T(2,128)(2,1)S(1)}, u32[]{:S(2)}, u32[]{:S(2)}) async-start(bf16[32,2,6912]{2,1,0:T(2,128)(2,1)} %broadcast_in_dim.57), calls=%async_computation.7 | async-start | bytes 1769472 | tf_op jit(solution)/shard_map/all_to_all | solution.py:160
  371.8 38.0 %collective-permute-start.8 = (bf16[512,1152]{1,0:T(8,128)(2,1)}, bf16[512,1152]{1,0:T(8,128)(2,1)}, u32[]{:S(2)}, u32[]{:S(2)}) collective-permute-start(bf16[512,1152]{1,0:T(8,128)(2,1)} %bitcast.87), channel_id=1, source_target_pairs={{0,1},{1,0},{2,3},{3,2},{4,5},{5,4},{6,7},{7,6},{8,9},{9,8},{10,11... | collective-permute-start | bytes 3538952 | tf_op jit(solution)/shard_map/ppermute | solution.py:148
  393.1 24.4 %collective-permute-start.6 = (bf16[512,1728]{0,1:T(8,128)(2,1)}, bf16[512,1728]{0,1:T(8,128)(2,1)}, u32[]{:S(2)}, u32[]{:S(2)}) collective-permute-start(bf16[512,1728]{0,1:T(8,128)(2,1)} %bitcast.147), channel_id=1, source_target_pairs={{0,1},{1,0},{2,3},{3,2},{4,5},{5,4},{6,7},{7,6},{8,9},{9,8},{10,11... | collective-permute-start | bytes 5308424 | tf_op jit(solution)/shard_map/ppermute | solution.py:148
  443.9 42.8 %collective-permute-start.7 = (bf16[2,1,4,72,1152]{4,3,2,1,0:T(8,128)(2,1)}, bf16[2,1,4,72,1152]{4,3,2,1,0:T(8,128)(2,1)}, u32[]{:S(2)}, u32[]{:S(2)}) collective-permute-start(bf16[2,1,4,72,1152]{4,3,2,1,0:T(8,128)(2,1)} %dynamic-slice_convert_fusion), channel_id=1, source_target_pairs={{0,2},{1,3},{2,0},{3,1},{4,6},{5,7},{6,4},{7,5},{8,10},{9,11},{10,... | collective-permute-start | bytes 3981320 | tf_op jit(solution)/shard_map/ppermute | solution.py:148
  463.2 20.6 %all-to-all-start.9 = ((f32[32,1,4140]{2,1,0:T(1,128)}), f32[32,1,4140]{2,1,0:T(1,128)}, u32[]{:S(2)}, u32[]{:S(2)}) async-start(f32[32,1,4140]{2,1,0:T(1,128)} %all_to_all.67), calls=%async_computation.9 | async-start | bytes 1081344 | tf_op jit(solution)/shard_map/all_to_all | solution.py:163
  468.0 134.7 %reduce-scatter.9.cloned.1.call-start = ((), (), s32[]{:S(2)}) async-start(), calls=%async_computation.18 | async-start | bytes 3317760 | tf_op jit(solution)/shard_map/reduce_scatter | solution.py:514
  470.9 34.8 %collective-permute-start.10 = (bf16[1,2,4,72,1152]{4,3,2,1,0:T(8,128)(2,1)}, bf16[1,2,4,72,1152]{4,3,2,1,0:T(8,128)(2,1)}, u32[]{:S(2)}, u32[]{:S(2)}) collective-permute-start(bf16[1,2,4,72,1152]{4,3,2,1,0:T(8,128)(2,1)} %pad_maximum_fusion.8), channel_id=1, source_target_pairs={{0,4},{1,5},{2,6},{3,7},{4,0},{5,1},{6,2},{7,3},{8,12},{9,13},{10,... | collective-permute-start | bytes 3981320 | tf_op jit(solution)/shard_map/ppermute | solution.py:148
  506.6 24.1 %all-to-all-start.10 = ((f32[32,1,2412]{2,1,0:T(1,128)}), f32[32,1,2412]{2,1,0:T(1,128)S(1)}, u32[]{:S(2)}, u32[]{:S(2)}) async-start(f32[32,1,2412]{2,1,0:T(1,128)} %broadcast_in_dim.60), calls=%async_computation.10 | async-start | bytes 622592 | tf_op jit(solution)/shard_map/all_to_all | solution.py:160
  514.6 25.5 %collective-permute-start.12 = (bf16[1,1,4,72,1152]{4,3,2,1,0:T(8,128)(2,1)}, bf16[1,1,4,72,1152]{4,3,2,1,0:T(8,128)(2,1)}, u32[]{:S(2)}, u32[]{:S(2)}) collective-permute-start(bf16[1,1,4,72,1152]{4,3,2,1,0:T(8,128)(2,1)} %dynamic-slice_convert_fusion.3), channel_id=1, source_target_pairs={{0,2},{1,3},{2,0},{3,1},{4,6},{5,7},{6,4},{7,5},{8,10},{9,11},{10,... | collective-permute-start | bytes 1990664 | tf_op jit(solution)/shard_map/ppermute | solution.py:148
  519.7 20.5 %collective-permute-start.11 = (bf16[1,1,4,72,1152]{4,3,2,1,0:T(8,128)(2,1)}, bf16[1,1,4,72,1152]{4,3,2,1,0:T(8,128)(2,1)}, u32[]{:S(2)}, u32[]{:S(2)}) collective-permute-start(bf16[1,1,4,72,1152]{4,3,2,1,0:T(8,128)(2,1)} %dynamic-slice_convert_fusion.4), channel_id=1, source_target_pairs={{0,4},{1,5},{2,6},{3,7},{4,0},{5,1},{6,2},{7,3},{8,12},{9,13},{10,... | collective-permute-start | bytes 1990664 | tf_op jit(solution)/shard_map/ppermute | solution.py:148
  544.2 18.6 %collective-permute-start.14 = (bf16[1,1,1,72,2304]{4,3,2,1,0:T(8,128)(2,1)}, bf16[1,1,1,72,2304]{4,3,2,1,0:T(8,128)(2,1)S(1)}, u32[]{:S(2)}, u32[]{:S(2)}) collective-permute-start(bf16[1,1,1,72,2304]{4,3,2,1,0:T(8,128)(2,1)} %pad_maximum_fusion.16), channel_id=1, source_target_pairs={{0,16},{1,17},{2,18},{3,19},{4,20},{5,21},{6,22},{7,23},{8,24},{9,... | collective-permute-start | bytes 995336 | tf_op jit(solution)/shard_map/ppermute | solution.py:148
  549.0 49.5 %all-to-all-start.12 = ((bf16[32,64,160]{2,1,0:T(8,128)(2,1)}), bf16[32,64,160]{2,1,0:T(8,128)(2,1)}, u32[]{:S(2)}, u32[]{:S(2)}) async-start(bf16[32,64,160]{2,1,0:T(8,128)(2,1)} %broadcast_in_dim.63), calls=%async_computation.12 | async-start | bytes 2097152 | tf_op jit(solution)/shard_map/all_to_all | solution.py:160
  552.9 33.6 %collective-permute-start.13 = (bf16[1,1,1,72,2304]{4,3,2,1,0:T(8,128)(2,1)S(1)}, bf16[1,1,1,72,2304]{4,3,2,1,0:T(8,128)(2,1)S(1)}, u32[]{:S(2)}, u32[]{:S(2)}) collective-permute-start(bf16[1,1,1,72,2304]{4,3,2,1,0:T(8,128)(2,1)S(1)} %pad_maximum_fusion.15), channel_id=1, source_target_pairs={{0,8},{1,9},{2,10},{3,11},{4,12},{5,13},{6,14},{7,15},{8,16},{9,17... | collective-permute-start | bytes 995336 | tf_op jit(solution)/shard_map/ppermute | solution.py:148
  (123 other events, 1197.7 us)
Sparse Core Ops, SparseCore 0:
  15.4 100.5 all-gather.2
  119.5 140.4 all-gather.4
  332.5 114.5 reduce-scatter.6
  480.6 57.6 reduce-scatter.8

commit v4 on v3

--- a/solution.py
+++ b/solution.py
@@ -4,6 +4,8 @@
 import jax
 import jax.numpy as jnp
 from jax import lax
+from jax.experimental import pallas as pl
+from jax.experimental.pallas import tpu as pltpu
 from jax.sharding import PartitionSpec as P
 
 D = 1152
@@ -209,8 +211,7 @@
 
 
 def gather_halves(rows):
-    whole = lax.all_gather(rows, ("c", "x", "y", "z"), axis=0, tiled=True)
-    return whole[:D], whole[D:]
+    return lax.all_gather(rows, ("c", "x", "y", "z"), axis=0, tiled=True)
 
 
 class Reduction:
@@ -373,6 +374,56 @@
     key_grad = (matmul("ihqk,iqhe->ikhe", score_grad, queries) * score_scale).astype(low)
     value_grad = matmul("ihqk,iqhe->ikhe", softmax_rows.astype(low), mixed_grad).astype(low)
     return jnp.stack([query_grad, key_grad, value_grad], 2).reshape(images, SEQ, 3 * D // 2)
+
+
+def accumulate(total_ref, part):
+    @pl.when(pl.program_id(0) == 0)
+    def _():
+        total_ref[...] = part
+
+    @pl.when(pl.program_id(0) > 0)
+    def _():
+        total_ref[...] += part
+
+
+def product(left, right, dims):
+    return lax.dot_general(left, right, (dims, ((), ())), preferred_element_type=jnp.float32)
+
+
+def mlp_kernel(rows_ref, up_ref, down_ref, inner_ref, active_ref, total_ref):
+    inner = product(rows_ref[...], up_ref[...], ((1,), (0,)))
+    inner_ref[...] = inner
+    active = gelu_tanh(inner).astype(jnp.bfloat16)
+    active_ref[...] = active
+    accumulate(total_ref, product(active, down_ref[...], ((1,), (1,))))
+
+
+def mlp_back_kernel(rows_ref, inner_ref, up_ref, down_ref, grad_ref, total_ref):
+    back = product(rows_ref[...], down_ref[...], ((1,), (0,)))
+    grad = smooth_back(gelu_tanh, inner_ref[...], back).astype(jnp.bfloat16)
+    grad_ref[...] = grad
+    accumulate(total_ref, product(grad, up_ref[...], ((1,), (1,))))
+
+
+def mlp_call(kernel, operands, weights, outputs):
+    count, per_half = FF // D, FF // 2 // D
+    rows = operands[0].shape[0]
+    whole = pl.BlockSpec((rows, D), lambda step: (0, 0))
+    part = pl.BlockSpec((rows, D), lambda step: (0, step))
+    up = pl.BlockSpec((D, D), lambda step: (step // per_half, step % per_half))
+    down = pl.BlockSpec((D, D), lambda step: (step // per_half, per_half + step % per_half))
+    return pl.pallas_call(
+        kernel,
+        grid=(count,),
+        in_specs=[whole] + [part] * (len(operands) - 1) + [up, down],
+        out_specs=[part] * len(outputs) + [whole],
+        out_shape=[jax.ShapeDtypeStruct((rows, FF), kind) for kind in outputs]
+        + [jax.ShapeDtypeStruct((rows, D), jnp.float32)],
+        compiler_params=pltpu.CompilerParams(vmem_limit_bytes=52 * 1024 * 1024),
+        cost_estimate=pl.CostEstimate(
+            flops=4 * rows * D * FF, bytes_accessed=4 * D * FF + 6 * rows * FF, transcendentals=rows * FF
+        ),
+    )(*operands, weights, weights)
 
 
 def shards(
@@ -404,11 +455,10 @@
     core = links.place("c")
     chunks, small = chip_rows(links, block_master)
     w_attention = gather_halves(chunks[:, : 2 * D])
+    w_attention = [w_attention[:D], w_attention[D:]]
     w_mlp = gather_halves(chunks[:, 2 * D :])
     w_qkv = [half[:, : 3 * D // 2] for half in w_attention]
     w_proj = [half[:, 3 * D // 2 :] for half in w_attention]
-    w_up = [half[:, : 2 * D] for half in w_mlp]
-    w_down = [half[:, 2 * D :] for half in w_mlp]
 
     window = Window(links, stem_master.shape[0])
     stem = window.fill(stem_master.astype(low))
@@ -486,9 +536,10 @@
     ].reshape(2 * D)
     final_mod = links.inner(final_mod.reshape(images, 2, D))
     final_shift, final_scale = final_mod[:, 0], final_mod[:, 1]
-    inner = [matmul("isd,df->isf", second, w_up[half]) for half in range(2)]
-    active = [gelu_tanh(rows).astype(low) for rows in inner]
-    output = sum(matmul("isf,of->iso", active[half], w_down[half]) for half in range(2))
+    inner, active, output = mlp_call(
+        mlp_kernel, [second.reshape(images * SEQ, D)], w_mlp, [wide, low]
+    )
+    output = output.reshape(images, SEQ, D)
     layer_out = middle + pieces[5][:, None, :] * output
     final_normed = modulate(layer_out, final_shift, final_scale).astype(low)
     prediction = matmul("isd,do->iso", final_normed, w_head)
@@ -507,6 +558,10 @@
             mine, sent = pick(core, first, second), pick(core, second, first)
         return jnp.concatenate([mine, links.send(sent, "c")], 0)
 
+    def half_with_partner(rows):
+        rows = rows.reshape(images, SEQ, -1)
+        return with_partner(rows[..., : FF // 2], rows[..., FF // 2 :])
+
     def sum_near(rows):
         return lax.psum_scatter(rows, ("x", "y"), scatter_dimension=0, tiled=True)
 
@@ -524,28 +579,23 @@
     final_grad = links.outer(jnp.stack([shift_grad, scale_grad], 1)).reshape(images, 2 * D)
     down_in = (pieces[5][:, None, :] * upstream).astype(low)
     gate_b = jnp.sum(upstream * output, 1)
-    active_both = with_partner(*active)
+    active_both = half_with_partner(active)
     second_both = with_partner(second)
     mixed_both = with_partner(*mixed)
     normed_both = with_partner(normed)
     down_both = with_partner(down_in)
-    inner_grad = [
-        smooth_back(
-            gelu_tanh, inner[half], matmul("iso,of->isf", down_in, w_down[half])
-        ).astype(low)
-        for half in range(2)
-    ]
-    inner_both = with_partner(*inner_grad)
+    inner_grad, second_grad = mlp_call(
+        mlp_back_kernel, [tokens(down_in), inner], w_mlp, [low]
+    )
+    second_grad = second_grad.reshape(images, SEQ, D)
+    inner_both = half_with_partner(inner_grad)
     inner_grad, down_both, active_both = together(inner_grad, down_both, active_both)
     grad_down = matmul("to,tf->of", down_both, active_both).astype(low)
     inner_both, grad_down = together(inner_both, grad_down)
     grad_up = matmul("td,tf->df", second_both, inner_both).astype(low)
     grad_mlp = jnp.concatenate([grad_up, grad_down], 1)
-    inner_grad, grad_mlp = together(inner_grad, grad_mlp)
+    second_grad, grad_mlp = together(second_grad, grad_mlp)
     near_mlp = sum_near(grad_mlp)
-    second_grad = sum(
-        matmul("isf,df->isd", inner_grad[half], w_up[half]) for half in range(2)
-    )
     back_mid, shift_b, scale_b = modulate_back(middle, pieces[3], pieces[4], second_grad)
     grad_mid = upstream + back_mid
     proj_in = (pieces[2][:, None, :] * grad_mid).astype(low)
@@ -574,7 +624,7 @@
     more = sums_of_attention.send("yx")
 
     late, near_mlp = together(late, near_mlp)
-    reduced_mlp = sum_far(near_mlp)
+    reduced_mlp = sum_far(near_mlp).astype(wide)
     all_final = early[:, 4 * D :]
     all_modulation = jnp.concatenate([late, early[:, : 4 * D]], 1)
     own_modulation = lax.dynamic_slice_in_dim(all_modulation, col_at, own_cols, 1)
@@ -611,11 +661,18 @@
     sums_of_attention.add(more)
     sums_of_attention.join()
     more = sums_of_attention.send("z")
-    before_low = window.assemble(links.spread(before_part), STARTS[1], D).astype(low)
+    windows = links.spread(before_part)
     sums_of_attention.add(more)
-    joint = jnp.concatenate([sums_of_attention.result(), reduced_mlp.astype(wide)], 1)
-    square = jnp.sum(joint * joint) + jnp.sum(small * small)
+    reduced_attention = sums_of_attention.result()
+    square = (
+        jnp.sum(reduced_attention * reduced_attention)
+        + jnp.sum(reduced_mlp * reduced_mlp)
+        + jnp.sum(small * small)
+    )
+    windows, square = together(windows, square)
     totals = links.spread(jnp.stack([loss_local, square])).sum(0)
+    before_low = window.assemble(windows, STARTS[1], D).astype(low)
+    joint = jnp.concatenate([reduced_attention, reduced_mlp], 1)
     block_grad = flat_gradient(links, joint, small)
     loss_total, squares = totals[0], totals[1]
     bias_rows = jnp.concatenate(

time: 665 us -> 662 us (level)
  matrix products: 159 us -> 95.5 us
  Pallas kernels: 0 us -> 41.9 us
  other arithmetic: 76.7 us -> 88.4 us
  local copies, waits for them, and re-layouts: 109 us -> 117 us
    dot_general x48 -> x40, matrix products: 151 us -> 85.2 us  [matmul(): return jnp.einsum(form, left, right, preferred_element_type=jnp.float32)]
    pallas_call x0 -> x2, Pallas kernels: none -> 41.9 us  [mlp_call(): pl.pallas_call(kernel, grid=(count,), in_specs=[whole] + [part] * (len(op...]
    all_to_all x8, waiting for transfers between devices: 45 us -> 25.4 us  [spread(): return lax.all_to_all(copies, AXES, split_axis=0, concat_axis=0, tiled=True)]
    all_gather x2, waiting for transfers between devices: 53.1 us -> 62.4 us  [gather_halves(): return lax.all_gather(rows, ('c', 'x', 'y', 'z'), axis=0, tiled=True)]
    all_to_all x5, waiting for transfers between devices: 67.3 us -> 74 us  [deliver(): return lax.all_to_all(blocks, AXES, split_axis=0, concat_axis=0, tiled=True)]
    unnamed x236 -> x275, local copies, waits for them, and re-layouts: 21.2 us -> 21.4 us
  transfers between devices with their start and end apart: 34 -> 34, of which waited for: 16 -> 15; matrix products, arithmetic and copies ran while one was open for 45% -> 38% of each run, Pallas kernels for 0% -> 6%
where the time goes in v4:
time: 662 us; the launch traced here: 650 us
  waiting for transfers between devices  216 us (33%)
  local copies, waits for them, and re-layouts  117 us (18%)
  matrix products  95.5 us (14%)
  other arithmetic  88.4 us (13%)
  starting transfers between devices  67.1 us (10%)
  Pallas kernels  41.9 us (6%)
  between operations  24.4 us (4%)
    dot_general x40, matrix products, matmul(): return jnp.einsum(form, left, right, preferred_element_type=jnp.float32)  85.2 us
    all_to_all x5, waiting for transfers between devices, deliver(): return lax.all_to_all(blocks, AXES, split_axis=0, concat_axis=0, tiled=True)  74 us
    all_gather x2, waiting for transfers between devices, gather_halves(): return lax.all_gather(rows, ('c', 'x', 'y', 'z'), axis=0, tiled=True)  62.4 us
    ppermute x17, waiting for transfers between devices, send(): return lax.ppermute(block, AXES, pairs)  52.2 us
    pallas_call x2, Pallas kernels, mlp_call(): pl.pallas_call(kernel, grid=(count,), in_specs=[whole] + [part] * (len(op...  41.9 us
    all_to_all x8, starting transfers between devices, spread(): return lax.all_to_all(copies, AXES, split_axis=0, concat_axis=0, tiled=True)  35.2 us
    all_to_all x8, waiting for transfers between devices, spread(): return lax.all_to_all(copies, AXES, split_axis=0, concat_axis=0, tiled=True)  25.4 us
    unnamed x275, local copies, waits for them, and re-layouts  21.4 us
  transfers between devices with their start and end apart: 34, of which 15 were waited for; matrix products, arithmetic and copies ran while one was open for 38% of the time, Pallas kernels for 6%

profile of v4, /device:TPU:0, one launch (start us, length us, event | category | flops | bytes accessed | tf_op | source)
XLA Modules:
  0.0 650.2 jit_solution(2841073291262847316)
XLA Ops:
  19.4 7.2 %all-to-all-start = ((bf16[32,2,868]{2,1,0:T(2,128)(2,1)}), bf16[32,2,868]{2,1,0:T(2,128)(2,1)S(1)}, u32[]{:S(2)}, u32[]{:S(2)}) async-start(bf16[32,2,868]{2,1,0:T(2,128)(2,1)} %reshape.1055), calls=%async_computation | async-start | bytes 229376 | tf_op jit(solution)/shard_map/all_to_all | solution.py:162
  26.7 4.6 concatenate.218
  43.8 14.8 %all-to-all-done.1 = f32[32,1,2628]{2,1,0:T(1,128)S(1)} async-done(((f32[32,1,2628]{2,1,0:T(1,128)}), f32[32,1,2628]{2,1,0:T(1,128)S(1)}, u32[]{:S(2)}, u32[]{:S(2)}) %all-to-all-start.1) | async-done | bytes 336416 | tf_op jit(solution)/shard_map/all_to_all | solution.py:165
  59.7 4.8 all-to-all-start.2
  69.2 7.6 %all-to-all-done.2 = f32[32,1,2628]{2,1,0:T(1,128)S(1)} async-done(((f32[32,1,2628]{2,1,0:T(1,128)}), f32[32,1,2628]{2,1,0:T(1,128)S(1)}, u32[]{:S(2)}, u32[]{:S(2)}) %all-to-all-start.2) | async-done | bytes 336416 | tf_op jit(solution)/shard_map/all_to_all | solution.py:162
  85.3 15.3 %all-to-all-done.3 = f32[32,2,1152]{2,1,0:T(2,128)S(1)} async-done(((f32[32,2,1152]{2,1,0:T(2,128)}), f32[32,2,1152]{2,1,0:T(2,128)S(1)}, u32[]{:S(2)}, u32[]{:S(2)}) %all-to-all-start.3) | async-done | bytes 294944 | tf_op jit(solution)/shard_map/all_to_all | solution.py:165
  106.4 8.2 %all-to-all-done.4 = bf16[32,2,1152]{2,1,0:T(2,128)(2,1)S(1)} async-done(((bf16[32,2,1152]{2,1,0:T(2,128)(2,1)}), bf16[32,2,1152]{2,1,0:T(2,128)(2,1)S(1)}, u32[]{:S(2)}, u32[]{:S(2)}) %all-to-all-start.4) | async-done | bytes 147488 | tf_op jit(solution)/shard_map/all_to_all | solution.py:162
  125.9 13.1 %all-to-all-done.5 = f32[32,2,1728]{2,1,0:T(2,128)S(1)} async-done(((f32[32,2,1728]{2,1,0:T(2,128)}), f32[32,2,1728]{2,1,0:T(2,128)S(1)}, u32[]{:S(2)}, u32[]{:S(2)}) %all-to-all-start.5) | async-done | bytes 442400 | tf_op jit(solution)/shard_map/all_to_all | solution.py:165
  141.7 5.2 fusion.9
  173.6 22.9 %all-to-all-done.6 = f32[32,2,2304]{2,1,0:T(2,128)} async-done(((f32[32,2,2304]{2,1,0:T(2,128)}), f32[32,2,2304]{2,1,0:T(2,128)}, u32[]{:S(2)}, u32[]{:S(2)}) %all-to-all-start.6) | async-done | bytes 589856 | tf_op jit(solution)/shard_map/all_to_all | solution.py:165
  204.7 62.4 %all-gather.5.cloned.1.call-done.up_ref.down_ref = bf16[2304,4608]{1,0:T(8,128)(2,1)} async-done(((bf16[72,4608]{1,0:T(8,128)(2,1)}), bf16[2304,4608]{1,0:T(8,128)(2,1)}) %all-gather.5.cloned.1.call-update) | async-done | bytes 21233680 | tf_op jit(solution)/shard_map/all_gather | solution.py:214
  267.1 20.1 %shard_map.230 = (f32[512,4608]{1,0:T(8,128)}, bf16[512,4608]{1,0:T(8,128)(2,1)}, f32[512,1152]{1,0:T(8,128)}) custom-call(bf16[512,1152]{1,0:T(8,128)(2,1)S(1)} %bitcast.329, bf16[2304,4608]{1,0:T(8,128)(2,1)} %all-gather.5.cloned.1.call-done.up_ref.down_ref, bf16[2304,4608]{1,0:T(8,128)(2,1)} %all-gather.5.cloned.1.call-done.up_ref.down_ref), custom_call_target="tpu_custom_call" | custom-call | flops 10871635968 | bytes 35389440 | tf_op jit(solution)/shard_map/pallas_call | solution.py:415
  298.8 21.9 %shard_map.231 = (bf16[512,4608]{1,0:T(8,128)(2,1)}, f32[512,1152]{1,0:T(8,128)}) custom-call(bf16[512,1152]{1,0:T(8,128)(2,1)S(1)} %bitcast.326, f32[512,4608]{1,0:T(8,128)} %get-tuple-element.41.inner_ref, bf16[2304,4608]{1,0:T(8,128)(2,1)} %all-gather.5.cloned.1.call-done.up_ref.down_ref, bf16[2304,4608]{1,0:T(8,128)(2,1)} %all-gather.5.cloned.1.call-done.up_ref.down_ref), custom_call_target="tpu_custom_call" | custom-call | flops 10871635968 | bytes 35389440 | tf_op jit(solution)/shard_map/pallas_call | solution.py:415
  328.4 6.4 convolution_convert_fusion.1
  336.9 7.6 %convolution_convert_fusion = bf16[1152,2304]{1,0:T(8,128)(2,1)S(1)} fusion(bf16[1024,2304]{1,0:T(8,128)(2,1)S(1)} %pad_maximum_fusion.1, bf16[512,1152]{1,0:T(8,128)(2,1)} %collective-permute-done.1, bf16[512,1152]{1,0:T(8,128)(2,1)S(1)} %bitcast.330), kind=kOutput, calls=%fused_computation | convolution fusion | flops 5443190784 | bytes 12386304 | tf_op jit(solution)/shard_map/td,tf->df/dot_general | solution.py:38
  398.7 5.8 fusion.5
  404.5 5.2 multiply_reduce_fusion.8
  429.5 5.9 fusion.15
  440.8 5.8 all-to-all-start.8
  490.1 8.0 %all-to-all-done.9 = f32[32,1,4140]{2,1,0:T(1,128)} async-done(((f32[32,1,4140]{2,1,0:T(1,128)}), f32[32,1,4140]{2,1,0:T(1,128)}, u32[]{:S(2)}, u32[]{:S(2)}) %all-to-all-start.9) | async-done | bytes 529952 | tf_op jit(solution)/shard_map/all_to_all | solution.py:165
  517.4 7.0 %all-to-all-done.10 = f32[32,1,2412]{2,1,0:T(1,128)} async-done(((f32[32,1,2412]{2,1,0:T(1,128)}), f32[32,1,2412]{2,1,0:T(1,128)}, u32[]{:S(2)}, u32[]{:S(2)}) %all-to-all-start.10) | async-done | bytes 308768 | tf_op jit(solution)/shard_map/all_to_all | solution.py:162
  547.7 19.5 %collective-permute-done.15 = bf16[1,1,1,72,2304]{4,3,2,1,0:T(8,128)(2,1)S(1)} collective-permute-done((bf16[1,1,1,72,2304]{4,3,2,1,0:T(8,128)(2,1)S(1)}, bf16[1,1,1,72,2304]{4,3,2,1,0:T(8,128)(2,1)S(1)}, u32[]{:S(2)}, u32[]{:S(2)}) %collective-permute-start.15) | collective-permute-done | bytes 331808 | tf_op jit(solution)/shard_map/ppermute | solution.py:150
  567.2 31.1 %collective-permute-done.14 = bf16[1,1,1,72,2304]{4,3,2,1,0:T(8,128)(2,1)S(1)} collective-permute-done((bf16[1,1,1,72,2304]{4,3,2,1,0:T(8,128)(2,1)S(1)}, bf16[1,1,1,72,2304]{4,3,2,1,0:T(8,128)(2,1)S(1)}, u32[]{:S(2)}, u32[]{:S(2)}) %collective-permute-start.14) | collective-permute-done | bytes 331808 | tf_op jit(solution)/shard_map/ppermute | solution.py:150
  635.7 6.7 %divide_subtract_fusion = (f32[499392]{0:T(1024)}, f32[499392]{0:T(1024)}, f32[499392]{0:T(1024)}) fusion(f32[499392]{0:T(1024)} %param.20, f32[499392]{0:T(1024)} %mul.882, f32[499392]{0:T(1024)} %param.21, f32[499392]{0:T(1024)} %param.22), kind=kLoop, calls=%fused_computation.87 | loop fusion | flops 5992704 | bytes 13982976 | tf_op jit(solution)/shard_map/sub | solution.py:343
  (646 shorter events, 308.8 us)
Async XLA Ops:
  7.2 134.5 %all-gather.3.cloned.1.call-start = ((), (), s32[]{:S(2)}) async-start(), calls=%async_computation.15 | async-start | bytes 10948608 | tf_op jit(solution)/shard_map/all_gather | solution.py:214
  15.3 251.8 %all-gather.5.cloned.1.call-start = ((), (), s32[]{:S(2)}) async-start(), calls=%async_computation.16 | async-start | bytes 21897216 | tf_op jit(solution)/shard_map/all_gather | solution.py:214
  79.7 20.9 %all-to-all-start.3 = ((f32[32,2,1152]{2,1,0:T(2,128)}), f32[32,2,1152]{2,1,0:T(2,128)S(1)}, u32[]{:S(2)}, u32[]{:S(2)}) async-start(f32[32,2,1152]{2,1,0:T(2,128)} %copy.369), calls=%async_computation.3 | async-start | bytes 589824 | tf_op jit(solution)/shard_map/all_to_all | solution.py:165
  117.3 21.7 %all-to-all-start.5 = ((f32[32,2,1728]{2,1,0:T(2,128)}), f32[32,2,1728]{2,1,0:T(2,128)S(1)}, u32[]{:S(2)}, u32[]{:S(2)}) async-start(f32[32,2,1728]{2,1,0:T(2,128)} %reshape.987), calls=%async_computation.5 | async-start | bytes 917504 | tf_op jit(solution)/shard_map/all_to_all | solution.py:165
  165.8 30.7 %all-to-all-start.6 = ((f32[32,2,2304]{2,1,0:T(2,128)}), f32[32,2,2304]{2,1,0:T(2,128)}, u32[]{:S(2)}, u32[]{:S(2)}) async-start(f32[32,2,2304]{2,1,0:T(2,128)} %reshape.998), calls=%async_computation.6 | async-start | bytes 1179648 | tf_op jit(solution)/shard_map/all_to_all | solution.py:165
  169.4 297.9 %reduce-scatter.3.cloned.1.call-start = ((), (), s32[]{:S(2)}) async-start(), calls=%async_computation.17 | async-start | bytes 13271040 | tf_op jit(solution)/shard_map/reduce_scatter | solution.py:566
  173.4 163.5 %collective-permute-start.1 = (bf16[512,1152]{1,0:T(8,128)(2,1)S(1)}, bf16[512,1152]{1,0:T(8,128)(2,1)}, u32[]{:S(2)}, u32[]{:S(2)}) collective-permute-start(bf16[512,1152]{1,0:T(8,128)(2,1)S(1)} %bitcast.328), channel_id=1, source_target_pairs={{0,1},{1,0},{2,3},{3,2},{4,5},{5,4},{6,7},{7,6},{8,9},{9,8},{10,11... | collective-permute-start | bytes 3538952 | tf_op jit(solution)/shard_map/ppermute | solution.py:150
  295.9 30.5 %collective-permute-start.4 = (bf16[512,2304]{1,0:T(8,128)(2,1)}, bf16[512,2304]{1,0:T(8,128)(2,1)}, u32[]{:S(2)}, u32[]{:S(2)}) collective-permute-start(bf16[512,2304]{1,0:T(8,128)(2,1)} %bitcast.59), channel_id=1, source_target_pairs={{0,1},{1,0},{2,3},{3,2},{4,5},{5,4},{6,7},{7,6},{8,9},{9,8},{10,11... | collective-permute-start | bytes 7077896 | tf_op jit(solution)/shard_map/ppermute | solution.py:150
  298.5 26.4 %collective-permute-start.3 = (bf16[512,1152]{1,0:T(8,128)(2,1)S(1)}, bf16[512,1152]{1,0:T(8,128)(2,1)}, u32[]{:S(2)}, u32[]{:S(2)}) collective-permute-start(bf16[512,1152]{1,0:T(8,128)(2,1)S(1)} %bitcast.325), channel_id=1, source_target_pairs={{0,1},{1,0},{2,3},{3,2},{4,5},{5,4},{6,7},{7,6},{8,9},{9,8},{10,11... | collective-permute-start | bytes 3538952 | tf_op jit(solution)/shard_map/ppermute | solution.py:150
  356.2 73.3 %collective-permute-start.6 = (bf16[512,1152]{1,0:T(8,128)(2,1)}, bf16[512,1152]{1,0:T(8,128)(2,1)}, u32[]{:S(2)}, u32[]{:S(2)}) collective-permute-start(bf16[512,1152]{1,0:T(8,128)(2,1)} %bitcast.377), channel_id=1, source_target_pairs={{0,1},{1,0},{2,3},{3,2},{4,5},{5,4},{6,7},{7,6},{8,9},{9,8},{10,11... | collective-permute-start | bytes 3538952 | tf_op jit(solution)/shard_map/ppermute | solution.py:150
  358.1 61.7 %collective-permute-start.9 = (bf16[512,576]{0,1:T(8,128)(2,1)}, bf16[512,576]{0,1:T(8,128)(2,1)}, u32[]{:S(2)}, u32[]{:S(2)}) collective-permute-start(bf16[512,576]{0,1:T(8,128)(2,1)} %bitcast.151), channel_id=1, source_target_pairs={{0,1},{1,0},{2,3},{3,2},{4,5},{5,4},{6,7},{7,6},{8,9},{9,8},{10,11... | collective-permute-start | bytes 1769480 | tf_op jit(solution)/shard_map/ppermute | solution.py:150
  392.9 33.4 %collective-permute-start.5 = (bf16[512,1728]{0,1:T(8,128)(2,1)}, bf16[512,1728]{0,1:T(8,128)(2,1)}, u32[]{:S(2)}, u32[]{:S(2)}) collective-permute-start(bf16[512,1728]{0,1:T(8,128)(2,1)} %bitcast.141), channel_id=1, source_target_pairs={{0,1},{1,0},{2,3},{3,2},{4,5},{5,4},{6,7},{7,6},{8,9},{9,8},{10,11... | collective-permute-start | bytes 5308424 | tf_op jit(solution)/shard_map/ppermute | solution.py:150
  395.0 30.8 %all-to-all-start.7 = ((bf16[32,2,6912]{2,1,0:T(2,128)(2,1)}), bf16[32,2,6912]{2,1,0:T(2,128)(2,1)S(1)}, u32[]{:S(2)}, u32[]{:S(2)}) async-start(bf16[32,2,6912]{2,1,0:T(2,128)(2,1)} %broadcast_in_dim.58), calls=%async_computation.7 | async-start | bytes 1769472 | tf_op jit(solution)/shard_map/all_to_all | solution.py:162
  440.8 22.7 %all-to-all-start.8 = ((bf16[32,2,2304]{2,1,0:T(2,128)(2,1)}), bf16[32,2,2304]{2,1,0:T(2,128)(2,1)}, u32[]{:S(2)}, u32[]{:S(2)}) async-start(bf16[32,2,2304]{2,1,0:T(2,128)(2,1)} %broadcast_in_dim.59), calls=%async_computation.8 | async-start | bytes 589824 | tf_op jit(solution)/shard_map/all_to_all | solution.py:162
  457.1 42.4 %collective-permute-start.7 = (bf16[2,1,4,72,1152]{4,3,2,1,0:T(8,128)(2,1)}, bf16[2,1,4,72,1152]{4,3,2,1,0:T(8,128)(2,1)}, u32[]{:S(2)}, u32[]{:S(2)}) collective-permute-start(bf16[2,1,4,72,1152]{4,3,2,1,0:T(8,128)(2,1)} %dynamic-slice_convert_fusion), channel_id=1, source_target_pairs={{0,2},{1,3},{2,0},{3,1},{4,6},{5,7},{6,4},{7,5},{8,10},{9,11},{10,... | collective-permute-start | bytes 3981320 | tf_op jit(solution)/shard_map/ppermute | solution.py:150
  460.4 39.2 %collective-permute-start.10 = (bf16[1,2,4,72,1152]{4,3,2,1,0:T(8,128)(2,1)}, bf16[1,2,4,72,1152]{4,3,2,1,0:T(8,128)(2,1)}, u32[]{:S(2)}, u32[]{:S(2)}) collective-permute-start(bf16[1,2,4,72,1152]{4,3,2,1,0:T(8,128)(2,1)} %pad_maximum_fusion.7), channel_id=1, source_target_pairs={{0,4},{1,5},{2,6},{3,7},{4,0},{5,1},{6,2},{7,3},{8,12},{9,13},{10,... | collective-permute-start | bytes 3981320 | tf_op jit(solution)/shard_map/ppermute | solution.py:150
  476.5 21.7 %all-to-all-start.9 = ((f32[32,1,4140]{2,1,0:T(1,128)}), f32[32,1,4140]{2,1,0:T(1,128)}, u32[]{:S(2)}, u32[]{:S(2)}) async-start(f32[32,1,4140]{2,1,0:T(1,128)} %all_to_all.67), calls=%async_computation.10 | async-start | bytes 1081344 | tf_op jit(solution)/shard_map/all_to_all | solution.py:165
  481.1 118.0 %reduce-scatter.5.cloned.1.call-start = ((), (), s32[]{:S(2)}) async-start(), calls=%async_computation.18 | async-start | bytes 3317760 | tf_op jit(solution)/shard_map/reduce_scatter | solution.py:569
  500.5 24.0 %all-to-all-start.10 = ((f32[32,1,2412]{2,1,0:T(1,128)}), f32[32,1,2412]{2,1,0:T(1,128)}, u32[]{:S(2)}, u32[]{:S(2)}) async-start(f32[32,1,2412]{2,1,0:T(1,128)} %broadcast_in_dim.60), calls=%async_computation.11 | async-start | bytes 622592 | tf_op jit(solution)/shard_map/all_to_all | solution.py:162
  508.6 26.6 %collective-permute-start.11 = (bf16[1,1,4,72,1152]{4,3,2,1,0:T(8,128)(2,1)}, bf16[1,1,4,72,1152]{4,3,2,1,0:T(8,128)(2,1)}, u32[]{:S(2)}, u32[]{:S(2)}) collective-permute-start(bf16[1,1,4,72,1152]{4,3,2,1,0:T(8,128)(2,1)} %dynamic-slice_convert_fusion.4), channel_id=1, source_target_pairs={{0,4},{1,5},{2,6},{3,7},{4,0},{5,1},{6,2},{7,3},{8,12},{9,13},{10,... | collective-permute-start | bytes 1990664 | tf_op jit(solution)/shard_map/ppermute | solution.py:150
  536.2 66.8 %all-to-all-start.11 = ((bf16[32,64,160]{2,1,0:T(8,128)(2,1)}), bf16[32,64,160]{2,1,0:T(8,128)(2,1)}, u32[]{:S(2)}, u32[]{:S(2)}) async-start(bf16[32,64,160]{2,1,0:T(8,128)(2,1)} %broadcast_in_dim.62), calls=%async_computation.12 | async-start | bytes 2097152 | tf_op jit(solution)/shard_map/all_to_all | solution.py:162
  542.7 24.4 %collective-permute-start.15 = (bf16[1,1,1,72,2304]{4,3,2,1,0:T(8,128)(2,1)S(1)}, bf16[1,1,1,72,2304]{4,3,2,1,0:T(8,128)(2,1)S(1)}, u32[]{:S(2)}, u32[]{:S(2)}) collective-permute-start(bf16[1,1,1,72,2304]{4,3,2,1,0:T(8,128)(2,1)S(1)} %pad_maximum_fusion.16), channel_id=1, source_target_pairs={{0,24},{1,25},{2,26},{3,27},{4,28},{5,29},{6,30},{7,31},{8,0},{9,1... | collective-permute-start | bytes 995336 | tf_op jit(solution)/shard_map/ppermute | solution.py:150
  546.4 51.9 %collective-permute-start.14 = (bf16[1,1,1,72,2304]{4,3,2,1,0:T(8,128)(2,1)S(1)}, bf16[1,1,1,72,2304]{4,3,2,1,0:T(8,128)(2,1)S(1)}, u32[]{:S(2)}, u32[]{:S(2)}) collective-permute-start(bf16[1,1,1,72,2304]{4,3,2,1,0:T(8,128)(2,1)S(1)} %pad_maximum_fusion.15), channel_id=1, source_target_pairs={{0,16},{1,17},{2,18},{3,19},{4,20},{5,21},{6,22},{7,23},{8,24},{9,... | collective-permute-start | bytes 995336 | tf_op jit(solution)/shard_map/ppermute | solution.py:150
  546.5 51.8 %collective-permute-start.13 = (bf16[1,1,1,72,2304]{4,3,2,1,0:T(8,128)(2,1)S(1)}, bf16[1,1,1,72,2304]{4,3,2,1,0:T(8,128)(2,1)S(1)}, u32[]{:S(2)}, u32[]{:S(2)}) collective-permute-start(bf16[1,1,1,72,2304]{4,3,2,1,0:T(8,128)(2,1)S(1)} %pad_maximum_fusion.14), channel_id=1, source_target_pairs={{0,8},{1,9},{2,10},{3,11},{4,12},{5,13},{6,14},{7,15},{8,16},{9,17... | collective-permute-start | bytes 995336 | tf_op jit(solution)/shard_map/ppermute | solution.py:150
  (143 other events, 908.9 us)
Sparse Core Ops, SparseCore 0:
  15.4 100.6 all-gather.2
  119.5 147.5 all-gather.4
  349.2 118.0 reduce-scatter.2
  487.9 59.5 reduce-scatter.4

commit v5 on v4

--- a/solution.py
+++ b/solution.py
@@ -674,6 +674,7 @@
     before_low = window.assemble(windows, STARTS[1], D).astype(low)
     joint = jnp.concatenate([reduced_attention, reduced_mlp], 1)
     block_grad = flat_gradient(links, joint, small)
+    totals, block_grad = together(totals, block_grad)
     loss_total, squares = totals[0], totals[1]
     bias_rows = jnp.concatenate(
         [all_sums, jnp.sum(all_modulation.astype(wide), 0)]

time: 662 us -> 661 us (level)
    unnamed x275 -> x285, local copies, waits for them, and re-layouts: 21.4 us -> 21.1 us
  transfers between devices with their start and end apart: 34 -> 34, of which waited for: 15 -> 15; matrix products, arithmetic and copies ran while one was open for 38% -> 37% of each run, Pallas kernels for 6% -> 6%
where the time goes in v5:
time: 661 us; the launch traced here: 650 us
  waiting for transfers between devices  217 us (33%)
  local copies, waits for them, and re-layouts  119 us (18%)
  matrix products  98.3 us (15%)
  other arithmetic  81.8 us (12%)
  starting transfers between devices  66.7 us (10%)
  Pallas kernels  42.1 us (6%)
  between operations  24.4 us (4%)
    dot_general x40, matrix products, matmul(): return jnp.einsum(form, left, right, preferred_element_type=jnp.float32)  86.5 us
    all_to_all x5, waiting for transfers between devices, deliver(): return lax.all_to_all(blocks, AXES, split_axis=0, concat_axis=0, tiled=True)  73.3 us
    all_gather x2, waiting for transfers between devices, gather_halves(): return lax.all_gather(rows, ('c', 'x', 'y', 'z'), axis=0, tiled=True)  62.4 us
    ppermute x17, waiting for transfers between devices, send(): return lax.ppermute(block, AXES, pairs)  52.4 us
    pallas_call x2, Pallas kernels, mlp_call(): pl.pallas_call(kernel, grid=(count,), in_specs=[whole] + [part] * (len(op...  42.1 us
    all_to_all x8, starting transfers between devices, spread(): return lax.all_to_all(copies, AXES, split_axis=0, concat_axis=0, tiled=True)  35.1 us
    all_to_all x8, waiting for transfers between devices, spread(): return lax.all_to_all(copies, AXES, split_axis=0, concat_axis=0, tiled=True)  27.2 us
    unnamed x285, local copies, waits for them, and re-layouts  21.1 us
  transfers between devices with their start and end apart: 34, of which 15 were waited for; matrix products, arithmetic and copies ran while one was open for 37% of the time, Pallas kernels for 6%

profile of v5, /device:TPU:0, one launch (start us, length us, event | category | flops | bytes accessed | tf_op | source)
XLA Modules:
  0.0 649.9 jit_solution(17822258417739664875)
XLA Ops:
  19.4 7.2 %all-to-all-start = ((bf16[32,2,868]{2,1,0:T(2,128)(2,1)}), bf16[32,2,868]{2,1,0:T(2,128)(2,1)S(1)}, u32[]{:S(2)}, u32[]{:S(2)}) async-start(bf16[32,2,868]{2,1,0:T(2,128)(2,1)} %reshape.1056), calls=%async_computation | async-start | bytes 229376 | tf_op jit(solution)/shard_map/all_to_all | solution.py:162
  43.8 14.8 %all-to-all-done.1 = f32[32,1,2628]{2,1,0:T(1,128)S(1)} async-done(((f32[32,1,2628]{2,1,0:T(1,128)}), f32[32,1,2628]{2,1,0:T(1,128)S(1)}, u32[]{:S(2)}, u32[]{:S(2)}) %all-to-all-start.1) | async-done | bytes 336416 | tf_op jit(solution)/shard_map/all_to_all | solution.py:165
  59.7 4.8 all-to-all-start.2
  69.2 7.6 %all-to-all-done.2 = f32[32,1,2628]{2,1,0:T(1,128)S(1)} async-done(((f32[32,1,2628]{2,1,0:T(1,128)}), f32[32,1,2628]{2,1,0:T(1,128)S(1)}, u32[]{:S(2)}, u32[]{:S(2)}) %all-to-all-start.2) | async-done | bytes 336416 | tf_op jit(solution)/shard_map/all_to_all | solution.py:162
  85.2 15.4 %all-to-all-done.3 = f32[32,2,1152]{2,1,0:T(2,128)S(1)} async-done(((f32[32,2,1152]{2,1,0:T(2,128)}), f32[32,2,1152]{2,1,0:T(2,128)S(1)}, u32[]{:S(2)}, u32[]{:S(2)}) %all-to-all-start.3) | async-done | bytes 294944 | tf_op jit(solution)/shard_map/all_to_all | solution.py:165
  106.2 8.3 %all-to-all-done.4 = bf16[32,2,1152]{2,1,0:T(2,128)(2,1)S(1)} async-done(((bf16[32,2,1152]{2,1,0:T(2,128)(2,1)}), bf16[32,2,1152]{2,1,0:T(2,128)(2,1)S(1)}, u32[]{:S(2)}, u32[]{:S(2)}) %all-to-all-start.4) | async-done | bytes 147488 | tf_op jit(solution)/shard_map/all_to_all | solution.py:162
  125.9 13.0 %all-to-all-done.5 = f32[32,2,1728]{2,1,0:T(2,128)S(1)} async-done(((f32[32,2,1728]{2,1,0:T(2,128)}), f32[32,2,1728]{2,1,0:T(2,128)S(1)}, u32[]{:S(2)}, u32[]{:S(2)}) %all-to-all-start.5) | async-done | bytes 442400 | tf_op jit(solution)/shard_map/all_to_all | solution.py:165
  141.7 5.2 fusion.9
  173.6 22.9 %all-to-all-done.6 = f32[32,2,2304]{2,1,0:T(2,128)} async-done(((f32[32,2,2304]{2,1,0:T(2,128)}), f32[32,2,2304]{2,1,0:T(2,128)}, u32[]{:S(2)}, u32[]{:S(2)}) %all-to-all-start.6) | async-done | bytes 589856 | tf_op jit(solution)/shard_map/all_to_all | solution.py:165
  204.7 62.4 %all-gather.5.cloned.1.call-done.up_ref.down_ref = bf16[2304,4608]{1,0:T(8,128)(2,1)} async-done(((bf16[72,4608]{1,0:T(8,128)(2,1)}), bf16[2304,4608]{1,0:T(8,128)(2,1)}) %all-gather.5.cloned.1.call-update) | async-done | bytes 21233680 | tf_op jit(solution)/shard_map/all_gather | solution.py:214
  267.1 20.2 %shard_map.230 = (f32[512,4608]{1,0:T(8,128)}, bf16[512,4608]{1,0:T(8,128)(2,1)}, f32[512,1152]{1,0:T(8,128)}) custom-call(bf16[512,1152]{1,0:T(8,128)(2,1)S(1)} %bitcast.329, bf16[2304,4608]{1,0:T(8,128)(2,1)} %all-gather.5.cloned.1.call-done.up_ref.down_ref, bf16[2304,4608]{1,0:T(8,128)(2,1)} %all-gather.5.cloned.1.call-done.up_ref.down_ref), custom_call_target="tpu_custom_call" | custom-call | flops 10871635968 | bytes 35389440 | tf_op jit(solution)/shard_map/pallas_call | solution.py:415
  298.8 21.9 %shard_map.231 = (bf16[512,4608]{1,0:T(8,128)(2,1)}, f32[512,1152]{1,0:T(8,128)}) custom-call(bf16[512,1152]{1,0:T(8,128)(2,1)S(1)} %bitcast.326, f32[512,4608]{1,0:T(8,128)} %get-tuple-element.43.inner_ref, bf16[2304,4608]{1,0:T(8,128)(2,1)} %all-gather.5.cloned.1.call-done.up_ref.down_ref, bf16[2304,4608]{1,0:T(8,128)(2,1)} %all-gather.5.cloned.1.call-done.up_ref.down_ref), custom_call_target="tpu_custom_call" | custom-call | flops 10871635968 | bytes 35389440 | tf_op jit(solution)/shard_map/pallas_call | solution.py:415
  328.5 6.4 convolution_convert_fusion.1
  337.0 7.6 %convolution_convert_fusion = bf16[1152,2304]{1,0:T(8,128)(2,1)S(1)} fusion(bf16[1024,2304]{1,0:T(8,128)(2,1)S(1)} %pad_maximum_fusion.1, bf16[512,1152]{1,0:T(8,128)(2,1)} %collective-permute-done.1, bf16[512,1152]{1,0:T(8,128)(2,1)S(1)} %bitcast.330), kind=kOutput, calls=%fused_computation | convolution fusion | flops 5443190784 | bytes 12386304 | tf_op jit(solution)/shard_map/td,tf->df/dot_general | solution.py:38
  398.8 5.8 fusion.5
  404.7 5.2 multiply_reduce_fusion.8
  429.6 5.9 fusion.15
  440.8 5.8 all-to-all-start.8
  491.1 7.2 %all-to-all-done.9 = f32[32,1,4140]{2,1,0:T(1,128)} async-done(((f32[32,1,4140]{2,1,0:T(1,128)}), f32[32,1,4140]{2,1,0:T(1,128)}, u32[]{:S(2)}, u32[]{:S(2)}) %all-to-all-start.9) | async-done | bytes 529952 | tf_op jit(solution)/shard_map/all_to_all | solution.py:165
  517.5 7.0 %all-to-all-done.10 = f32[32,1,2412]{2,1,0:T(1,128)} async-done(((f32[32,1,2412]{2,1,0:T(1,128)}), f32[32,1,2412]{2,1,0:T(1,128)}, u32[]{:S(2)}, u32[]{:S(2)}) %all-to-all-start.10) | async-done | bytes 308768 | tf_op jit(solution)/shard_map/all_to_all | solution.py:162
  547.7 19.7 %collective-permute-done.15 = bf16[1,1,1,72,2304]{4,3,2,1,0:T(8,128)(2,1)S(1)} collective-permute-done((bf16[1,1,1,72,2304]{4,3,2,1,0:T(8,128)(2,1)S(1)}, bf16[1,1,1,72,2304]{4,3,2,1,0:T(8,128)(2,1)S(1)}, u32[]{:S(2)}, u32[]{:S(2)}) %collective-permute-start.15) | collective-permute-done | bytes 331808 | tf_op jit(solution)/shard_map/ppermute | solution.py:150
  567.3 31.1 %collective-permute-done.14 = bf16[1,1,1,72,2304]{4,3,2,1,0:T(8,128)(2,1)S(1)} collective-permute-done((bf16[1,1,1,72,2304]{4,3,2,1,0:T(8,128)(2,1)S(1)}, bf16[1,1,1,72,2304]{4,3,2,1,0:T(8,128)(2,1)S(1)}, u32[]{:S(2)}, u32[]{:S(2)}) %collective-permute-start.14) | collective-permute-done | bytes 331808 | tf_op jit(solution)/shard_map/ppermute | solution.py:150
  630.2 4.7 divide_subtract_fusion.1
  635.0 5.1 divide_subtract_fusion
  (655 shorter events, 310.4 us)
Async XLA Ops:
  7.2 134.5 %all-gather.3.cloned.1.call-start = ((), (), s32[]{:S(2)}) async-start(), calls=%async_computation.15 | async-start | bytes 10948608 | tf_op jit(solution)/shard_map/all_gather | solution.py:214
  15.3 251.8 %all-gather.5.cloned.1.call-start = ((), (), s32[]{:S(2)}) async-start(), calls=%async_computation.16 | async-start | bytes 21897216 | tf_op jit(solution)/shard_map/all_gather | solution.py:214
  79.7 20.9 %all-to-all-start.3 = ((f32[32,2,1152]{2,1,0:T(2,128)}), f32[32,2,1152]{2,1,0:T(2,128)S(1)}, u32[]{:S(2)}, u32[]{:S(2)}) async-start(f32[32,2,1152]{2,1,0:T(2,128)} %copy.369), calls=%async_computation.3 | async-start | bytes 589824 | tf_op jit(solution)/shard_map/all_to_all | solution.py:165
  117.2 21.7 %all-to-all-start.5 = ((f32[32,2,1728]{2,1,0:T(2,128)}), f32[32,2,1728]{2,1,0:T(2,128)S(1)}, u32[]{:S(2)}, u32[]{:S(2)}) async-start(f32[32,2,1728]{2,1,0:T(2,128)} %reshape.987), calls=%async_computation.5 | async-start | bytes 917504 | tf_op jit(solution)/shard_map/all_to_all | solution.py:165
  165.8 30.7 %all-to-all-start.6 = ((f32[32,2,2304]{2,1,0:T(2,128)}), f32[32,2,2304]{2,1,0:T(2,128)}, u32[]{:S(2)}, u32[]{:S(2)}) async-start(f32[32,2,2304]{2,1,0:T(2,128)} %reshape.998), calls=%async_computation.6 | async-start | bytes 1179648 | tf_op jit(solution)/shard_map/all_to_all | solution.py:165
  169.4 298.0 %reduce-scatter.3.cloned.1.call-start = ((), (), s32[]{:S(2)}) async-start(), calls=%async_computation.17 | async-start | bytes 13271040 | tf_op jit(solution)/shard_map/reduce_scatter | solution.py:566
  173.4 163.6 %collective-permute-start.1 = (bf16[512,1152]{1,0:T(8,128)(2,1)S(1)}, bf16[512,1152]{1,0:T(8,128)(2,1)}, u32[]{:S(2)}, u32[]{:S(2)}) collective-permute-start(bf16[512,1152]{1,0:T(8,128)(2,1)S(1)} %bitcast.328), channel_id=1, source_target_pairs={{0,1},{1,0},{2,3},{3,2},{4,5},{5,4},{6,7},{7,6},{8,9},{9,8},{10,11... | collective-permute-start | bytes 3538952 | tf_op jit(solution)/shard_map/ppermute | solution.py:150
  296.0 30.6 %collective-permute-start.4 = (bf16[512,2304]{1,0:T(8,128)(2,1)}, bf16[512,2304]{1,0:T(8,128)(2,1)}, u32[]{:S(2)}, u32[]{:S(2)}) collective-permute-start(bf16[512,2304]{1,0:T(8,128)(2,1)} %bitcast.59), channel_id=1, source_target_pairs={{0,1},{1,0},{2,3},{3,2},{4,5},{5,4},{6,7},{7,6},{8,9},{9,8},{10,11... | collective-permute-start | bytes 7077896 | tf_op jit(solution)/shard_map/ppermute | solution.py:150
  298.6 26.5 %collective-permute-start.3 = (bf16[512,1152]{1,0:T(8,128)(2,1)S(1)}, bf16[512,1152]{1,0:T(8,128)(2,1)}, u32[]{:S(2)}, u32[]{:S(2)}) collective-permute-start(bf16[512,1152]{1,0:T(8,128)(2,1)S(1)} %bitcast.325), channel_id=1, source_target_pairs={{0,1},{1,0},{2,3},{3,2},{4,5},{5,4},{6,7},{7,6},{8,9},{9,8},{10,11... | collective-permute-start | bytes 3538952 | tf_op jit(solution)/shard_map/ppermute | solution.py:150
  356.3 73.3 %collective-permute-start.6 = (bf16[512,1152]{1,0:T(8,128)(2,1)}, bf16[512,1152]{1,0:T(8,128)(2,1)}, u32[]{:S(2)}, u32[]{:S(2)}) collective-permute-start(bf16[512,1152]{1,0:T(8,128)(2,1)} %bitcast.377), channel_id=1, source_target_pairs={{0,1},{1,0},{2,3},{3,2},{4,5},{5,4},{6,7},{7,6},{8,9},{9,8},{10,11... | collective-permute-start | bytes 3538952 | tf_op jit(solution)/shard_map/ppermute | solution.py:150
  358.1 61.7 %collective-permute-start.9 = (bf16[512,576]{0,1:T(8,128)(2,1)}, bf16[512,576]{0,1:T(8,128)(2,1)}, u32[]{:S(2)}, u32[]{:S(2)}) collective-permute-start(bf16[512,576]{0,1:T(8,128)(2,1)} %bitcast.151), channel_id=1, source_target_pairs={{0,1},{1,0},{2,3},{3,2},{4,5},{5,4},{6,7},{7,6},{8,9},{9,8},{10,11... | collective-permute-start | bytes 1769480 | tf_op jit(solution)/shard_map/ppermute | solution.py:150
  393.0 33.4 %collective-permute-start.5 = (bf16[512,1728]{0,1:T(8,128)(2,1)}, bf16[512,1728]{0,1:T(8,128)(2,1)}, u32[]{:S(2)}, u32[]{:S(2)}) collective-permute-start(bf16[512,1728]{0,1:T(8,128)(2,1)} %bitcast.141), channel_id=1, source_target_pairs={{0,1},{1,0},{2,3},{3,2},{4,5},{5,4},{6,7},{7,6},{8,9},{9,8},{10,11... | collective-permute-start | bytes 5308424 | tf_op jit(solution)/shard_map/ppermute | solution.py:150
  395.1 30.8 %all-to-all-start.7 = ((bf16[32,2,6912]{2,1,0:T(2,128)(2,1)}), bf16[32,2,6912]{2,1,0:T(2,128)(2,1)S(1)}, u32[]{:S(2)}, u32[]{:S(2)}) async-start(bf16[32,2,6912]{2,1,0:T(2,128)(2,1)} %broadcast_in_dim.58), calls=%async_computation.7 | async-start | bytes 1769472 | tf_op jit(solution)/shard_map/all_to_all | solution.py:162
  440.8 22.7 %all-to-all-start.8 = ((bf16[32,2,2304]{2,1,0:T(2,128)(2,1)}), bf16[32,2,2304]{2,1,0:T(2,128)(2,1)}, u32[]{:S(2)}, u32[]{:S(2)}) async-start(bf16[32,2,2304]{2,1,0:T(2,128)(2,1)} %broadcast_in_dim.59), calls=%async_computation.8 | async-start | bytes 589824 | tf_op jit(solution)/shard_map/all_to_all | solution.py:162
  457.2 42.5 %collective-permute-start.7 = (bf16[2,1,4,72,1152]{4,3,2,1,0:T(8,128)(2,1)}, bf16[2,1,4,72,1152]{4,3,2,1,0:T(8,128)(2,1)}, u32[]{:S(2)}, u32[]{:S(2)}) collective-permute-start(bf16[2,1,4,72,1152]{4,3,2,1,0:T(8,128)(2,1)} %dynamic-slice_convert_fusion), channel_id=1, source_target_pairs={{0,2},{1,3},{2,0},{3,1},{4,6},{5,7},{6,4},{7,5},{8,10},{9,11},{10,... | collective-permute-start | bytes 3981320 | tf_op jit(solution)/shard_map/ppermute | solution.py:150
  460.5 39.2 %collective-permute-start.10 = (bf16[1,2,4,72,1152]{4,3,2,1,0:T(8,128)(2,1)}, bf16[1,2,4,72,1152]{4,3,2,1,0:T(8,128)(2,1)}, u32[]{:S(2)}, u32[]{:S(2)}) collective-permute-start(bf16[1,2,4,72,1152]{4,3,2,1,0:T(8,128)(2,1)} %pad_maximum_fusion.7), channel_id=1, source_target_pairs={{0,4},{1,5},{2,6},{3,7},{4,0},{5,1},{6,2},{7,3},{8,12},{9,13},{10,... | collective-permute-start | bytes 3981320 | tf_op jit(solution)/shard_map/ppermute | solution.py:150
  476.6 21.6 %all-to-all-start.9 = ((f32[32,1,4140]{2,1,0:T(1,128)}), f32[32,1,4140]{2,1,0:T(1,128)}, u32[]{:S(2)}, u32[]{:S(2)}) async-start(f32[32,1,4140]{2,1,0:T(1,128)} %all_to_all.67), calls=%async_computation.10 | async-start | bytes 1081344 | tf_op jit(solution)/shard_map/all_to_all | solution.py:165
  481.2 118.1 %reduce-scatter.5.cloned.1.call-start = ((), (), s32[]{:S(2)}) async-start(), calls=%async_computation.18 | async-start | bytes 3317760 | tf_op jit(solution)/shard_map/reduce_scatter | solution.py:569
  500.6 23.9 %all-to-all-start.10 = ((f32[32,1,2412]{2,1,0:T(1,128)}), f32[32,1,2412]{2,1,0:T(1,128)}, u32[]{:S(2)}, u32[]{:S(2)}) async-start(f32[32,1,2412]{2,1,0:T(1,128)} %broadcast_in_dim.60), calls=%async_computation.11 | async-start | bytes 622592 | tf_op jit(solution)/shard_map/all_to_all | solution.py:162
  508.6 26.5 %collective-permute-start.11 = (bf16[1,1,4,72,1152]{4,3,2,1,0:T(8,128)(2,1)}, bf16[1,1,4,72,1152]{4,3,2,1,0:T(8,128)(2,1)}, u32[]{:S(2)}, u32[]{:S(2)}) collective-permute-start(bf16[1,1,4,72,1152]{4,3,2,1,0:T(8,128)(2,1)} %dynamic-slice_convert_fusion.4), channel_id=1, source_target_pairs={{0,4},{1,5},{2,6},{3,7},{4,0},{5,1},{6,2},{7,3},{8,12},{9,13},{10,... | collective-permute-start | bytes 1990664 | tf_op jit(solution)/shard_map/ppermute | solution.py:150
  536.3 68.4 %all-to-all-start.11 = ((bf16[32,64,160]{2,1,0:T(8,128)(2,1)}), bf16[32,64,160]{2,1,0:T(8,128)(2,1)}, u32[]{:S(2)}, u32[]{:S(2)}) async-start(bf16[32,64,160]{2,1,0:T(8,128)(2,1)} %broadcast_in_dim.62), calls=%async_computation.12 | async-start | bytes 2097152 | tf_op jit(solution)/shard_map/all_to_all | solution.py:162
  542.7 24.6 %collective-permute-start.15 = (bf16[1,1,1,72,2304]{4,3,2,1,0:T(8,128)(2,1)S(1)}, bf16[1,1,1,72,2304]{4,3,2,1,0:T(8,128)(2,1)S(1)}, u32[]{:S(2)}, u32[]{:S(2)}) collective-permute-start(bf16[1,1,1,72,2304]{4,3,2,1,0:T(8,128)(2,1)S(1)} %pad_maximum_fusion.16), channel_id=1, source_target_pairs={{0,24},{1,25},{2,26},{3,27},{4,28},{5,29},{6,30},{7,31},{8,0},{9,1... | collective-permute-start | bytes 995336 | tf_op jit(solution)/shard_map/ppermute | solution.py:150
  546.4 52.1 %collective-permute-start.14 = (bf16[1,1,1,72,2304]{4,3,2,1,0:T(8,128)(2,1)S(1)}, bf16[1,1,1,72,2304]{4,3,2,1,0:T(8,128)(2,1)S(1)}, u32[]{:S(2)}, u32[]{:S(2)}) collective-permute-start(bf16[1,1,1,72,2304]{4,3,2,1,0:T(8,128)(2,1)S(1)} %pad_maximum_fusion.15), channel_id=1, source_target_pairs={{0,16},{1,17},{2,18},{3,19},{4,20},{5,21},{6,22},{7,23},{8,24},{9,... | collective-permute-start | bytes 995336 | tf_op jit(solution)/shard_map/ppermute | solution.py:150
  546.5 52.0 %collective-permute-start.13 = (bf16[1,1,1,72,2304]{4,3,2,1,0:T(8,128)(2,1)S(1)}, bf16[1,1,1,72,2304]{4,3,2,1,0:T(8,128)(2,1)S(1)}, u32[]{:S(2)}, u32[]{:S(2)}) collective-permute-start(bf16[1,1,1,72,2304]{4,3,2,1,0:T(8,128)(2,1)S(1)} %pad_maximum_fusion.14), channel_id=1, source_target_pairs={{0,8},{1,9},{2,10},{3,11},{4,12},{5,13},{6,14},{7,15},{8,16},{9,17... | collective-permute-start | bytes 995336 | tf_op jit(solution)/shard_map/ppermute | solution.py:150
  (148 other events, 945.5 us)
Sparse Core Ops, SparseCore 0:
  15.4 100.6 all-gather.2
  119.6 147.5 all-gather.4
  349.2 118.0 reduce-scatter.2
  488.1 59.7 reduce-scatter.4
